TPU v7x, 256 devices: a whole 4x4x8 slice. The times are simulated.
256 devices in a mesh: band: 64 (over x, z, core), mem: 4 (over y).
Axes of the slice: x: 4, y: 4, z: 8, core: 2. Of those that a mesh axis runs over, the one named last changes fastest.
Arguments:
- perturb: bfloat16 [80, 4, 256, 1536], P('mem', None, 'band'), may hold values from -0.8984375 to 0.8984375
- alpha_control: bfloat16 [80, 4, 256, 1536], P('mem', None, 'band'), may hold values from -6 to 6
- loc_factor: bfloat16 [1536, 1536], replicated
- static_control: bfloat16 [4, 1024, 4608], P(None, 'band'), may hold values from -6 to 6
- innovation: bfloat16 [4, 1024, 4608], P(None, 'band'), may hold values from -6 to 6
- obs_weight: bfloat16 [4, 1024, 4608], P(None, 'band'), may hold values from 0.099609375 to 1
- coarse_rows: int32 [64], replicated, may hold values from 2 to 4, as said below
- fine_rows: int32 [64], replicated, may hold values from 2 to 16, as said below
- source_row: int32 [1024], P('band'), may hold values from 0 to 190, as said below
- row_weight: float32 [1024], P('band'), may hold values from 0 to 1
Outputs:
- grad_alpha: bfloat16 [80, 4, 256, 1536], P('mem', None, 'band')
- grad_static: float32 [4, 1024, 4608], P(None, 'band')
Inputs may be any that keep to these rules, and one draw needn't show every extreme that they name: `coarse_rows`: pairs of bands (2k, 2k+1) hold 3 + t and 3 - t rows with t in -1..1; the rows sum to 192. `fine_rows`: the fine rows sum to 576; the first fine row of band b lies within 2 of three times the first coarse row of band b. `source_row`: for a fine slot whose row index is j (slot s of band b stands for row first_f[b] + s, also past the band's live rows), the value is j // 3 or j // 3 - 1, clipped to 0 .. 190.
All inputs are finite; a program needn't handle non-finite values.
Results may differ from a plain program's by a relative error of at most 0.0029.
Values sent between devices are 32-bit elements; how exact they have to be, the bound alone decides.
No kernel may reach another device: no remote copies, remote signals or barrier semaphores. Data moves between devices by JAX's collectives and lax.ppermute only.
A program may use at most 64 MiB of HBM per device.

v0:
```python
import math

import jax
import jax.numpy as jnp
from jax import lax
from jax.sharding import PartitionSpec as P

DIFF_STEPS = 2


diffusivity = 0.2


def passed_along(shard, axis, by):
    peers = lax.axis_size(axis)
    pairs = [(i, i + by) for i in range(peers) if 0 <= i + by < peers]
    return lax.ppermute(shard, axis, pairs)


def with_halo(shard, sides, width):
    for axis, dim in sides:
        peers, length = (lax.axis_size(axis), shard.shape[dim])
        up = [(i, (i + 1) % peers) for i in range(peers - 1)]
        down = [(j, i) for i, j in up]
        last = lax.slice_in_dim(shard, length - width, length, axis=dim)
        leading = lax.slice_in_dim(shard, 0, width, axis=dim)
        before = lax.ppermute(last, axis, up)
        after = lax.ppermute(leading, axis, down)
        shard = jnp.concatenate([before, shard, after], axis=dim)
    return shard


def column_tables(width):
    rows = jnp.arange(width)[:, None]
    columns = jnp.arange(3 * width)[None, :]
    own_table = jnp.where(
        columns == 3 * rows,
        1.0,
        jnp.where(
            columns == 3 * rows + 1, 2.0 / 3.0, jnp.where(columns == 3 * rows + 2, 1.0 / 3.0, 0.0)
        ),
    ).astype(jnp.float32)
    carry_table = jnp.where(
        columns == 3 * rows + 1, 1.0 / 3.0, jnp.where(columns == 3 * rows + 2, 2.0 / 3.0, 0.0)
    ).astype(jnp.float32)
    return (own_table, carry_table)


def refine_along(coarse):
    count = coarse.shape[-1]
    width = math.gcd(count, 128)
    own_table, carry_table = column_tables(width)
    lead = coarse.shape[:-1]
    following = jnp.roll(coarse, -1, axis=-1)
    blocks = coarse.reshape(lead + (count // width, width))
    next_blocks = following.reshape(lead + (count // width, width))
    fine = jnp.einsum("lsbi,ij->lsbj", blocks, own_table, precision=lax.Precision.HIGHEST)
    fine = fine + jnp.einsum(
        "lsbi,ij->lsbj", next_blocks, carry_table, precision=lax.Precision.HIGHEST
    )
    return fine.reshape(lead + (3 * count,))


def coarsen_along(gradient):
    count = gradient.shape[-1] // 3
    width = math.gcd(count, 128)
    own_table, carry_table = column_tables(width)
    lead = gradient.shape[:-1]
    blocks = gradient.reshape(lead + (count // width, 3 * width))
    own_part = jnp.einsum(
        "lsbj,ij->lsbi", blocks, own_table, precision=lax.Precision.HIGHEST
    ).reshape(lead + (count,))
    carried = jnp.einsum(
        "lsbj,ij->lsbi", blocks, carry_table, precision=lax.Precision.HIGHEST
    ).reshape(lead + (count,))
    return own_part + jnp.roll(carried, 1, axis=-1)


def diffuse(extended, width, live_count, device, band_total):
    total_rows = extended.shape[1]
    fine_cap = total_rows - 2 * width
    position = jnp.arange(total_rows)
    inside = position - width
    first_below = (position == width + fine_cap)[None, :, None]
    last_live = (position == width + live_count - 1)[None, :, None]
    usable = jnp.where(
        inside < 0,
        device > 0,
        jnp.where(inside < fine_cap, inside < live_count, device < band_total - 1),
    )
    usable = usable.astype(jnp.float32)[None, :, None]
    zero_row = jnp.zeros_like(extended[:, :1])
    shifted_down = jnp.concatenate([zero_row, extended[:, :-1]], axis=1)
    shifted_up = jnp.concatenate([extended[:, 1:], zero_row], axis=1)
    live_end = lax.dynamic_slice_in_dim(extended, width + live_count - 1, 1, 1)
    below_start = extended[:, width + fine_cap : width + fine_cap + 1]
    upper_rows = jnp.where(first_below, live_end, shifted_down)
    lower_rows = jnp.where(last_live, below_start, shifted_up)
    eastern = jnp.roll(extended, -1, axis=2)
    western = jnp.roll(extended, 1, axis=2)
    extended = (
        extended + diffusivity * (upper_rows + lower_rows + eastern + western - 4.0 * extended)
    ) * usable
    return extended


def spread(values, live_count, device, band_total):
    for number in range(DIFF_STEPS):
        tail_rows = lax.dynamic_slice_in_dim(values, live_count - 1, 1, 1)
        from_earlier = passed_along(tail_rows, "band", 1)
        from_later = passed_along(values[:, :1], "band", -1)
        extended = jnp.concatenate([from_earlier, values, from_later], axis=1)
        extended = diffuse(extended, 1, live_count, device, band_total)
        values = extended[:, 1:-1]
    return values


def on_device(
    perturb,
    alpha_control,
    loc_factor,
    static_control,
    innovation,
    obs_weight,
    coarse_rows,
    fine_rows,
    source_row,
    row_weight,
):
    device = lax.axis_index("band")
    band_total = lax.axis_size("band")
    capacity = perturb.shape[2]
    fine_cap = static_control.shape[1]
    first_coarse = jnp.concatenate([jnp.zeros((1,), jnp.int32), jnp.cumsum(coarse_rows)])
    own_coarse = coarse_rows[device]
    own_fine = fine_rows[device]
    coarse_live = (jnp.arange(capacity) < own_coarse).astype(jnp.float32)
    fine_live = (jnp.arange(fine_cap) < own_fine).astype(jnp.float32)
    localized = jnp.dot(
        alpha_control.reshape(-1, alpha_control.shape[3]),
        loc_factor,
        preferred_element_type=jnp.float32,
    ).reshape(alpha_control.shape)
    partial_sum = jnp.sum(perturb.astype(jnp.float32) * localized, axis=0)
    increment = lax.psum(partial_sum, "mem")
    extended = with_halo(increment, (("band", 1),), capacity)
    position = jnp.arange(3 * capacity)
    neighbour = device - 1 + position // capacity
    clipped = jnp.clip(neighbour, 0, band_total - 1)
    offset_in = position % capacity
    latitude = first_coarse[clipped] + offset_in
    usable = (neighbour >= 0) & (neighbour < band_total) & (offset_in < coarse_rows[clipped])
    hit_low = (latitude[None, :] == source_row[:, None]).astype(jnp.float32)
    hit_high = (latitude[None, :] == source_row[:, None] + 1).astype(jnp.float32)
    interp = (
        fine_live[:, None]
        * usable.astype(jnp.float32)[None, :]
        * ((1.0 - row_weight)[:, None] * hit_low + row_weight[:, None] * hit_high)
    )
    fine_band = jnp.einsum("sq,lqx->lsx", interp, extended, precision=lax.Precision.HIGHEST)
    ensemble = refine_along(fine_band)
    control = static_control.astype(jnp.float32) * fine_live[None, :, None]
    static_part = spread(control, own_fine, device, band_total)
    residual = (
        obs_weight.astype(jnp.float32)
        * (ensemble + static_part - innovation.astype(jnp.float32))
        * fine_live[None, :, None]
    )
    grad_static = (control + spread(residual, own_fine, device, band_total)) * fine_live[
        None, :, None
    ]
    back_band = coarsen_along(residual)
    pulled_back = jnp.einsum("sq,lsx->lqx", interp, back_band, precision=lax.Precision.HIGHEST)
    from_later = passed_along(pulled_back[:, :capacity], "band", -1)
    from_earlier = passed_along(pulled_back[:, 2 * capacity :], "band", 1)
    coarse_back = pulled_back[:, capacity : 2 * capacity] + from_later + from_earlier
    schur_term = (perturb.astype(jnp.float32) * coarse_back[None]).astype(jnp.bfloat16)
    pulled = lax.dot_general(
        schur_term.reshape(-1, schur_term.shape[3]),
        loc_factor,
        (((1,), (1,)), ((), ())),
        preferred_element_type=jnp.float32,
    ).reshape(alpha_control.shape)
    grad_alpha = (
        (alpha_control.astype(jnp.float32) + pulled) * coarse_live[None, None, :, None]
    ).astype(jnp.bfloat16)
    return (grad_alpha, grad_static)


def solution(mesh):
    placed = (
        P("mem", None, "band", None),
        P("mem", None, "band", None),
        P(),
        P(None, "band", None),
        P(None, "band", None),
        P(None, "band", None),
        P(),
        P(),
        P("band"),
        P("band"),
    )
    return jax.shard_map(
        on_device,
        mesh=mesh,
        in_specs=placed,
        out_specs=(P("mem", None, "band", None), P(None, "band", None)),
        check_vma=False,
    )
```

profile of v0, /device:TPU:6, one launch (start us, length us, event | category | flops | bytes accessed | tf_op | source)
XLA Modules:
  0.0 125.2 jit_solution(10426871739915464433)
XLA Ops:
  7.2 6.3 %fusion.41 = f32[4,4,1536]{2,1,0:T(4,128)} fusion(bf16[1536,1536]{1,0:T(8,128)(2,1)} %param.12, bf16[20,4,4,1536]{3,2,1,0:T(4,128)(2,1)} %param.10, bf16[20,4,4,1536]{3,2,1,0:T(4,128)(2,1)} %param.11), kind=kOutput, calls=%fused_computation.55 | convolution fusion | flops 1511399424 | bytes 6782976 | tf_op jit(solution)/shard_map/dot_general | solution.py:139
  16.6 1.9 %collective-permute-start.2 = (f32[4,1,4608]{2,1,0:T(1,128)S(1)}, f32[4,1,4608]{2,1,0:T(1,128)S(1)}, u32[]{:S(2)}, u32[]{:S(2)}) collective-permute-start(f32[4,1,4608]{2,1,0:T(1,128)S(1)} %get-tuple-element.24), channel_id=1, source_target_pairs={{0,4},{4,8},{8,12},{12,16},{16,20},{20,24},{24,28},{28,32},{32,36}... | collective-permute-start | bytes 221192 | tf_op jit(solution)/shard_map/ppermute | solution.py:17
  18.5 7.5 %collective-permute-start.3 = (f32[4,1,4608]{2,1,0:T(1,128)S(1)}, f32[4,1,4608]{2,1,0:T(1,128)S(1)}, u32[]{:S(2)}, u32[]{:S(2)}) collective-permute-start(f32[4,1,4608]{2,1,0:T(1,128)S(1)} %get-tuple-element.25), channel_id=1, source_target_pairs={{4,0},{8,4},{12,8},{16,12},{20,16},{24,20},{28,24},{32,28},{36,32}... | collective-permute-start | bytes 221192 | tf_op jit(solution)/shard_map/ppermute | solution.py:17
  32.4 1.6 %fusion.39 = f32[4,18,4608]{2,1,0:T(8,128)S(1)} fusion(f32[4,1,4608]{2,1,0:T(1,128)S(1)} %collective-permute-done.3, f32[4,16,4608]{2,1,0:T(8,128)S(1)} %convert_multiply_fusion.1, f32[4,1,4608]{2,1,0:T(1,128)S(1)} %collective-permute-done.2, f32[4,18,1]{2,1,0:T(8,128)S(1)} %get-tuple-element.19, f32[4,18,4607]{2,1,0:T(8,128)S(1)} %get-tuple-element.21, ...), kind=kLoop, calls=%fused_computation.42 | loop fusion | flops 7299072 | bytes 5455980 | tf_op jit(solution)/shard_map/mul | solution.py:101
  34.2 1.9 %collective-permute-start.4 = (f32[4,1,4608]{2,1,0:T(1,128)S(1)}, f32[4,1,4608]{2,1,0:T(1,128)S(1)}, u32[]{:S(2)}, u32[]{:S(2)}) collective-permute-start(f32[4,1,4608]{2,1,0:T(1,128)S(1)} %constant_dynamic-slice_fusion.5), channel_id=1, source_target_pairs={{0,4},{4,8},{8,12},{12,16},{16,20},{20,24},{24,28},{28,32},{32,36}... | collective-permute-start | bytes 221192 | tf_op jit(solution)/shard_map/ppermute | solution.py:17
  36.1 5.8 %collective-permute-start.5 = (f32[4,1,4608]{2,1,0:T(1,128)S(1)}, f32[4,1,4608]{2,1,0:T(1,128)S(1)}, u32[]{:S(2)}, u32[]{:S(2)}) collective-permute-start(f32[4,1,4608]{2,1,0:T(1,128)S(1)} %slice.162), channel_id=1, source_target_pairs={{4,0},{8,4},{12,8},{16,12},{20,16},{24,20},{28,24},{32,28},{36,32}... | collective-permute-start | bytes 221192 | tf_op jit(solution)/shard_map/ppermute | solution.py:17
  42.6 20.3 %all-reduce.10.cloned.1.call-done = f32[4,4,1536]{2,1,0:T(4,128)} async-done(((f32[4,4,1536]{2,1,0:T(4,128)}), f32[4,4,1536]{2,1,0:T(4,128)}) %all-reduce.10.cloned.1.call-update) | async-done | bytes 98320 | tf_op jit(solution)/shard_map/psum | solution.py:145
  62.9 2.9 %collective-permute-start.1 = (f32[4,4,1536]{2,1,0:T(4,128)}, f32[4,4,1536]{2,1,0:T(4,128)S(1)}, u32[]{:S(2)}, u32[]{:S(2)}) collective-permute-start(f32[4,4,1536]{2,1,0:T(4,128)} %all-reduce.10.cloned.1.call-done), channel_id=1, source_target_pairs={{4,0},{8,4},{12,8},{16,12},{20,16},{24,20},{28,24},{32,28},{36,32}... | collective-permute-start | bytes 294920 | tf_op jit(solution)/shard_map/ppermute | solution.py:28
  65.8 2.1 %collective-permute-start = (f32[4,4,1536]{2,1,0:T(4,128)}, f32[4,4,1536]{2,1,0:T(4,128)S(1)}, u32[]{:S(2)}, u32[]{:S(2)}) collective-permute-start(f32[4,4,1536]{2,1,0:T(4,128)} %all-reduce.10.cloned.1.call-done), channel_id=1, source_target_pairs={{0,4},{4,8},{8,12},{12,16},{16,20},{20,24},{24,28},{28,32},{32,36}... | collective-permute-start | bytes 294920 | tf_op jit(solution)/shard_map/ppermute | solution.py:27
  69.5 4.5 %collective-permute-done = f32[4,4,1536]{2,1,0:T(4,128)S(1)} collective-permute-done((f32[4,4,1536]{2,1,0:T(4,128)}, f32[4,4,1536]{2,1,0:T(4,128)S(1)}, u32[]{:S(2)}, u32[]{:S(2)}) %collective-permute-start) | collective-permute-done | bytes 98336 | tf_op jit(solution)/shard_map/ppermute | solution.py:27
  74.8 1.2 fusion.71
  76.0 1.2 fusion.44
  80.0 2.3 %fusion.92 = f32[4,16,12,128]{3,2,1,0:T(8,128)} fusion(f32[4,16,12,384]{3,2,1,0:T(8,128)S(1)} %reshape.201, s32[128]{0:T(128)S(1)} %get-tuple-element.33, s32[128]{0:T(128)S(1)} %broadcast_add_fusion.1, s32[128]{0:T(128)S(1)} %get-tuple-element.32), kind=kOutput, calls=%fused_computation.110 | convolution fusion | flops 453279744 | bytes 1574400 | tf_op jit(solution)/shard_map/lsbj,ij->lsbi/dot_general | solution.py:70
  82.3 2.3 %fusion.89 = f32[4,16,12,128]{3,2,1,0:T(8,128)} fusion(f32[4,16,12,384]{3,2,1,0:T(8,128)S(1)} %reshape.201, s32[128]{0:T(128)S(1)} %get-tuple-element.33, s32[128]{0:T(128)S(1)} %broadcast_add_fusion.1), kind=kOutput, calls=%fused_computation.109 | convolution fusion | flops 453181440 | bytes 1573888 | tf_op jit(solution)/shard_map/lsbj,ij->lsbi/dot_general | solution.py:73
  84.6 1.9 %collective-permute-start.8 = (f32[4,1,4608]{2,1,0:T(1,128)S(1)}, f32[4,1,4608]{2,1,0:T(1,128)S(1)}, u32[]{:S(2)}, u32[]{:S(2)}) collective-permute-start(f32[4,1,4608]{2,1,0:T(1,128)S(1)} %get-tuple-element.22), channel_id=1, source_target_pairs={{0,4},{4,8},{8,12},{12,16},{16,20},{20,24},{24,28},{28,32},{32,36}... | collective-permute-start | bytes 221192 | tf_op jit(solution)/shard_map/ppermute | solution.py:17
  86.5 5.8 %collective-permute-start.9 = (f32[4,1,4608]{2,1,0:T(1,128)S(1)}, f32[4,1,4608]{2,1,0:T(1,128)S(1)}, u32[]{:S(2)}, u32[]{:S(2)}) collective-permute-start(f32[4,1,4608]{2,1,0:T(1,128)S(1)} %get-tuple-element.23), channel_id=1, source_target_pairs={{4,0},{8,4},{12,8},{16,12},{20,16},{24,20},{28,24},{32,28},{36,32}... | collective-permute-start | bytes 221192 | tf_op jit(solution)/shard_map/ppermute | solution.py:17
  95.2 1.9 %collective-permute-start.6 = (f32[4,4,1536]{2,1,0:T(4,128)S(1)}, f32[4,4,1536]{2,1,0:T(4,128)S(1)}, u32[]{:S(2)}, u32[]{:S(2)}) collective-permute-start(f32[4,4,1536]{2,1,0:T(4,128)S(1)} %get-tuple-element.26), channel_id=1, source_target_pairs={{4,0},{8,4},{12,8},{16,12},{20,16},{24,20},{28,24},{32,28},{36,32}... | collective-permute-start | bytes 294920 | tf_op jit(solution)/shard_map/ppermute | solution.py:17
  97.1 2.6 %collective-permute-start.7 = (f32[4,4,1536]{2,1,0:T(4,128)S(1)}, f32[4,4,1536]{2,1,0:T(4,128)S(1)}, u32[]{:S(2)}, u32[]{:S(2)}) collective-permute-start(f32[4,4,1536]{2,1,0:T(4,128)S(1)} %get-tuple-element.27), channel_id=1, source_target_pairs={{0,4},{4,8},{8,12},{12,16},{16,20},{20,24},{24,28},{28,32},{32,36}... | collective-permute-start | bytes 294920 | tf_op jit(solution)/shard_map/ppermute | solution.py:17
  100.9 1.6 %fusion.27 = f32[4,18,4608]{2,1,0:T(8,128)S(1)} fusion(f32[4,1,4608]{2,1,0:T(1,128)S(1)} %collective-permute-done.9, f32[4,16,4608]{2,1,0:T(8,128)S(1)} %fusion.64, f32[4,1,4608]{2,1,0:T(1,128)S(1)} %collective-permute-done.8, f32[4,18,1]{2,1,0:T(8,128)S(1)} %get-tuple-element.11, f32[4,18,4607]{2,1,0:T(8,128)S(1)} %get-tuple-element.13, ...), kind=kLoop, calls=%fused_computation.26 | loop fusion | flops 7299072 | bytes 5455980 | tf_op jit(solution)/shard_map/mul | solution.py:101
  102.7 2.1 %collective-permute-start.10 = (f32[4,1,4608]{2,1,0:T(1,128)S(1)}, f32[4,1,4608]{2,1,0:T(1,128)S(1)}, u32[]{:S(2)}, u32[]{:S(2)}) collective-permute-start(f32[4,1,4608]{2,1,0:T(1,128)S(1)} %constant_dynamic-slice_fusion.1), channel_id=1, source_target_pairs={{0,4},{4,8},{8,12},{12,16},{16,20},{20,24},{24,28},{28,32},{32,36}... | collective-permute-start | bytes 221192 | tf_op jit(solution)/shard_map/ppermute | solution.py:17
  104.8 5.8 %collective-permute-start.11 = (f32[4,1,4608]{2,1,0:T(1,128)S(1)}, f32[4,1,4608]{2,1,0:T(1,128)S(1)}, u32[]{:S(2)}, u32[]{:S(2)}) collective-permute-start(f32[4,1,4608]{2,1,0:T(1,128)S(1)} %slice.183), channel_id=1, source_target_pairs={{4,0},{8,4},{12,8},{16,12},{20,16},{24,20},{28,24},{32,28},{36,32}... | collective-permute-start | bytes 221192 | tf_op jit(solution)/shard_map/ppermute | solution.py:17
  110.7 2.6 %fusion.13 = bf16[20,4,4,1536]{3,0,2,1:T(8,128)(2,1)S(1)} fusion(bf16[1536,1536]{1,0:T(8,128)(2,1)S(1)} %bitcast.103, f32[4]{0:T(128)S(1)} %compare_convert_fusion, f32[4,4,1536]{2,1,0:T(4,128)S(1)} %fusion.95, bf16[20,4,4,1536]{3,2,1,0:T(4,128)(2,1)S(1)} %copy-done.7, bf16[20,4,4,1536]{3,2,1,0:T(4,128)(2,1)S(1)} %copy-done.8), kind=kOutput, calls=%fused_computation.10 | convolution fusion | flops 1513390080 | bytes 7766032 | tf_op jit(solution)/shard_map/dot_general | solution.py:178
  113.3 1.5 %copy.34 = bf16[20,4,4,1536]{3,2,1,0:T(4,128)(2,1)} copy(bf16[20,4,4,1536]{3,0,2,1:T(8,128)(2,1)S(1)} %fusion.13) | data formatting | bytes 1966080
  116.4 2.0 %fusion.53 = f32[4,16,4608]{2,1,0:T(8,128)} fusion(f32[4,18,4607]{2,1,0:T(8,128)S(1)} %get-tuple-element.9, f32[4,18,1]{2,1,0:T(8,128)S(1)} %get-tuple-element.7, f32[4,18,4607]{2,1,0:T(8,128)S(1)} %get-tuple-element.8, f32[4,18,1]{2,1,0:T(8,128)S(1)} %get-tuple-element.6, f32[4,18,4608]{2,1,0:T(8,128)S(1)} %fusion.18, ...), kind=kLoop, calls=%fused_computation.66 | loop fusion | flops 3833856 | bytes 6783104 | tf_op jit(solution)/shard_map/mul | solution.py:169
  (107 shorter events, 17.6 us)
Async XLA Ops:
  7.2 6.4 %copy-start.9 = (s32[64]{0:T(128)S(1)}, s32[64]{0:T(128)}, u32[]{:S(2)}) copy-start(s32[64]{0:T(128)} %param.17) | copy-start | bytes 772
  7.2 9.1 %copy-start.1 = (bf16[4,16,4608]{2,1,0:T(8,128)(2,1)S(1)}, bf16[4,16,4608]{2,1,0:T(8,128)(2,1)}, u32[]{:S(2)}) copy-start(bf16[4,16,4608]{2,1,0:T(8,128)(2,1)} %param.13) | copy-start | bytes 1769476
  7.2 55.7 %all-reduce.10.cloned.1.call-start = ((), (), s32[]{:S(2)}) async-start(), calls=%async_computation | async-start | bytes 196608 | tf_op jit(solution)/shard_map/psum | solution.py:145
  13.6 13.1 %copy-start = (s32[64]{0:T(128)S(1)}, s32[64]{0:T(128)}, u32[]{:S(2)}) copy-start(s32[64]{0:T(128)} %param.16) | copy-start | bytes 772
  13.6 15.2 %copy-start.6 = (s32[16]{0:T(128)S(1)}, s32[16]{0:T(128)}, u32[]{:S(2)}) copy-start(s32[16]{0:T(128)} %param.18) | copy-start | bytes 196
  13.6 15.2 %copy-start.5 = (f32[16]{0:T(128)S(1)}, f32[16]{0:T(128)}, u32[]{:S(2)}) copy-start(f32[16]{0:T(128)} %param.19) | copy-start | bytes 196
  16.6 14.7 %collective-permute-start.2 = (f32[4,1,4608]{2,1,0:T(1,128)S(1)}, f32[4,1,4608]{2,1,0:T(1,128)S(1)}, u32[]{:S(2)}, u32[]{:S(2)}) collective-permute-start(f32[4,1,4608]{2,1,0:T(1,128)S(1)} %get-tuple-element.24), channel_id=1, source_target_pairs={{0,4},{4,8},{8,12},{12,16},{16,20},{20,24},{24,28},{28,32},{32,36}... | collective-permute-start | bytes 221192 | tf_op jit(solution)/shard_map/ppermute | solution.py:17
  18.5 12.7 %collective-permute-start.3 = (f32[4,1,4608]{2,1,0:T(1,128)S(1)}, f32[4,1,4608]{2,1,0:T(1,128)S(1)}, u32[]{:S(2)}, u32[]{:S(2)}) collective-permute-start(f32[4,1,4608]{2,1,0:T(1,128)S(1)} %get-tuple-element.25), channel_id=1, source_target_pairs={{4,0},{8,4},{12,8},{16,12},{20,16},{24,20},{28,24},{32,28},{36,32}... | collective-permute-start | bytes 221192 | tf_op jit(solution)/shard_map/ppermute | solution.py:17
  34.2 33.7 %collective-permute-start.4 = (f32[4,1,4608]{2,1,0:T(1,128)S(1)}, f32[4,1,4608]{2,1,0:T(1,128)S(1)}, u32[]{:S(2)}, u32[]{:S(2)}) collective-permute-start(f32[4,1,4608]{2,1,0:T(1,128)S(1)} %constant_dynamic-slice_fusion.5), channel_id=1, source_target_pairs={{0,4},{4,8},{8,12},{12,16},{16,20},{20,24},{24,28},{28,32},{32,36}... | collective-permute-start | bytes 221192 | tf_op jit(solution)/shard_map/ppermute | solution.py:17
  36.1 31.8 %collective-permute-start.5 = (f32[4,1,4608]{2,1,0:T(1,128)S(1)}, f32[4,1,4608]{2,1,0:T(1,128)S(1)}, u32[]{:S(2)}, u32[]{:S(2)}) collective-permute-start(f32[4,1,4608]{2,1,0:T(1,128)S(1)} %slice.162), channel_id=1, source_target_pairs={{4,0},{8,4},{12,8},{16,12},{20,16},{24,20},{28,24},{32,28},{36,32}... | collective-permute-start | bytes 221192 | tf_op jit(solution)/shard_map/ppermute | solution.py:17
  62.9 6.7 %collective-permute-start.1 = (f32[4,4,1536]{2,1,0:T(4,128)}, f32[4,4,1536]{2,1,0:T(4,128)S(1)}, u32[]{:S(2)}, u32[]{:S(2)}) collective-permute-start(f32[4,4,1536]{2,1,0:T(4,128)} %all-reduce.10.cloned.1.call-done), channel_id=1, source_target_pairs={{4,0},{8,4},{12,8},{16,12},{20,16},{24,20},{28,24},{32,28},{36,32}... | collective-permute-start | bytes 294920 | tf_op jit(solution)/shard_map/ppermute | solution.py:28
  65.8 8.3 %collective-permute-start = (f32[4,4,1536]{2,1,0:T(4,128)}, f32[4,4,1536]{2,1,0:T(4,128)S(1)}, u32[]{:S(2)}, u32[]{:S(2)}) collective-permute-start(f32[4,4,1536]{2,1,0:T(4,128)} %all-reduce.10.cloned.1.call-done), channel_id=1, source_target_pairs={{0,4},{4,8},{8,12},{12,16},{16,20},{20,24},{24,28},{28,32},{32,36}... | collective-permute-start | bytes 294920 | tf_op jit(solution)/shard_map/ppermute | solution.py:27
  68.9 5.2 %copy-start.4 = (f32[4,4,1536]{2,1,0:T(4,128)S(1)}, f32[4,4,1536]{2,1,0:T(4,128)}, u32[]{:S(2)}) copy-start(f32[4,4,1536]{2,1,0:T(4,128)} %all-reduce.10.cloned.1.call-done) | copy-start | bytes 294916
  77.2 1.2 copy-start.3
  84.6 15.1 %collective-permute-start.8 = (f32[4,1,4608]{2,1,0:T(1,128)S(1)}, f32[4,1,4608]{2,1,0:T(1,128)S(1)}, u32[]{:S(2)}, u32[]{:S(2)}) collective-permute-start(f32[4,1,4608]{2,1,0:T(1,128)S(1)} %get-tuple-element.22), channel_id=1, source_target_pairs={{0,4},{4,8},{8,12},{12,16},{16,20},{20,24},{24,28},{28,32},{32,36}... | collective-permute-start | bytes 221192 | tf_op jit(solution)/shard_map/ppermute | solution.py:17
  86.5 13.2 %collective-permute-start.9 = (f32[4,1,4608]{2,1,0:T(1,128)S(1)}, f32[4,1,4608]{2,1,0:T(1,128)S(1)}, u32[]{:S(2)}, u32[]{:S(2)}) collective-permute-start(f32[4,1,4608]{2,1,0:T(1,128)S(1)} %get-tuple-element.23), channel_id=1, source_target_pairs={{4,0},{8,4},{12,8},{16,12},{20,16},{24,20},{28,24},{32,28},{36,32}... | collective-permute-start | bytes 221192 | tf_op jit(solution)/shard_map/ppermute | solution.py:17
  95.2 15.4 %collective-permute-start.6 = (f32[4,4,1536]{2,1,0:T(4,128)S(1)}, f32[4,4,1536]{2,1,0:T(4,128)S(1)}, u32[]{:S(2)}, u32[]{:S(2)}) collective-permute-start(f32[4,4,1536]{2,1,0:T(4,128)S(1)} %get-tuple-element.26), channel_id=1, source_target_pairs={{4,0},{8,4},{12,8},{16,12},{20,16},{24,20},{28,24},{32,28},{36,32}... | collective-permute-start | bytes 294920 | tf_op jit(solution)/shard_map/ppermute | solution.py:17
  97.1 13.5 %collective-permute-start.7 = (f32[4,4,1536]{2,1,0:T(4,128)S(1)}, f32[4,4,1536]{2,1,0:T(4,128)S(1)}, u32[]{:S(2)}, u32[]{:S(2)}) collective-permute-start(f32[4,4,1536]{2,1,0:T(4,128)S(1)} %get-tuple-element.27), channel_id=1, source_target_pairs={{0,4},{4,8},{8,12},{12,16},{16,20},{20,24},{24,28},{28,32},{32,36}... | collective-permute-start | bytes 294920 | tf_op jit(solution)/shard_map/ppermute | solution.py:17
  100.2 10.5 %slice-start = ((s8[4718592]{0:T(1024)(128)(4,1)}), s8[4194304]{0:T(1024)(128)(4,1)S(1)}, s32[]{:S(2)}) async-start(s8[4718592]{0:T(1024)(128)(4,1)} %bitcast.102), calls=%async_computation.1 | async-start | bytes 8388608
  100.9 9.8 %slice-start.1 = ((s8[4718592]{0:T(1024)(128)(4,1)}), s8[524288]{0:T(1024)(128)(4,1)S(1)}, s32[]{:S(2)}) async-start(s8[4718592]{0:T(1024)(128)(4,1)} %bitcast.102), calls=%async_computation.2 | async-start | bytes 1048576
  102.5 8.2 %copy-start.7 = (bf16[20,4,4,1536]{3,2,1,0:T(4,128)(2,1)S(1)}, bf16[20,4,4,1536]{3,2,1,0:T(4,128)(2,1)}, u32[]{:S(2)}) copy-start(bf16[20,4,4,1536]{3,2,1,0:T(4,128)(2,1)} %param.10) | copy-start | bytes 2949124
  102.5 8.2 %copy-start.8 = (bf16[20,4,4,1536]{3,2,1,0:T(4,128)(2,1)S(1)}, bf16[20,4,4,1536]{3,2,1,0:T(4,128)(2,1)}, u32[]{:S(2)}) copy-start(bf16[20,4,4,1536]{3,2,1,0:T(4,128)(2,1)} %param.11) | copy-start | bytes 2949124
  102.7 12.0 %collective-permute-start.10 = (f32[4,1,4608]{2,1,0:T(1,128)S(1)}, f32[4,1,4608]{2,1,0:T(1,128)S(1)}, u32[]{:S(2)}, u32[]{:S(2)}) collective-permute-start(f32[4,1,4608]{2,1,0:T(1,128)S(1)} %constant_dynamic-slice_fusion.1), channel_id=1, source_target_pairs={{0,4},{4,8},{8,12},{12,16},{16,20},{20,24},{24,28},{28,32},{32,36}... | collective-permute-start | bytes 221192 | tf_op jit(solution)/shard_map/ppermute | solution.py:17
  104.8 9.9 %collective-permute-start.11 = (f32[4,1,4608]{2,1,0:T(1,128)S(1)}, f32[4,1,4608]{2,1,0:T(1,128)S(1)}, u32[]{:S(2)}, u32[]{:S(2)}) collective-permute-start(f32[4,1,4608]{2,1,0:T(1,128)S(1)} %slice.183), channel_id=1, source_target_pairs={{4,0},{8,4},{12,8},{16,12},{20,16},{24,20},{28,24},{32,28},{36,32}... | collective-permute-start | bytes 221192 | tf_op jit(solution)/shard_map/ppermute | solution.py:17
  (1 other events, 1.1 us)
Sparse Core Ops, SparseCore 0:
  13.7 49.0 all-reduce.9
where the time goes:
time: 126 us; the launch traced here: 125 us
  starting transfers between devices  42.1 us (33%)
  waiting for transfers between devices  24.8 us (20%)
  between operations  18.2 us (14%)
  matrix products  17.1 us (14%)
  local copies, waits for them, and re-layouts  11.9 us (9%)
  other arithmetic  11 us (9%)
    ppermute x10, starting transfers between devices, passed_along(): return lax.ppermute(shard, axis, pairs)  37.1 us
    psum x1, waiting for transfers between devices, on_device(): increment = lax.psum(partial_sum, 'mem')  20.3 us
    dot_general x1, matrix products, on_device(): jnp.dot(alpha_control.reshape(-1, alpha_control.shape[3]), loc_factor, pr...  6.34 us
    ppermute x1, waiting for transfers between devices, with_halo(): before = lax.ppermute(last, axis, up)  4.49 us
    mul x2, other arithmetic, diffuse(): (extended + diffusivity * (upper_rows + lower_rows + eastern + western -...  3.19 us
    ppermute x1, starting transfers between devices, with_halo(): after = lax.ppermute(leading, axis, down)  2.9 us
    unnamed x33, local copies, waits for them, and re-layouts  2.8 us
    slice x8, local copies, waits for them, and re-layouts, diffuse(): western = jnp.roll(extended, 1, axis=2)  2.71 us
  transfers between devices with their start and end apart: 13, of which 2 were waited for; matrix products, arithmetic and copies ran while one was open for 16% of the time, Pallas kernels for 0%

commit v1 on v0

v1 whole, which is shorter than its diff:
```python
import jax
import jax.numpy as jnp
from jax import lax
from jax.experimental import pallas as pl
from jax.experimental.pallas import tpu as pltpu
from jax.sharding import PartitionSpec as P

F32 = jnp.float32
BF16 = jnp.bfloat16
THIRD = 1.0 / 3.0
VMEM = pl.BlockSpec(memory_space=pltpu.VMEM)
SMEM = pl.BlockSpec(memory_space=pltpu.SMEM)


def params(mib):
    return pltpu.CompilerParams(vmem_limit_bytes=mib << 20)


def same_chip(x):
    peers = lax.axis_size("band")
    return lax.ppermute(x, "band", [(i, i ^ 1) for i in range(peers)])


def cross_chip(x):
    peers = lax.axis_size("band")
    pairs = [(i, (i + 1) % peers) for i in range(1, peers, 2)]
    return lax.ppermute(x, "band", pairs + [(j, i) for i, j in pairs])


def mem_peer(x, by):
    peers = lax.axis_size("mem")
    return lax.ppermute(x, "mem", [(i, (i + by) % peers) for i in range(peers)])


def triple_table(width, transposed):
    rows = lax.broadcasted_iota(jnp.int32, (3 * width, 3 * width), 0)
    cols = lax.broadcasted_iota(jnp.int32, (3 * width, 3 * width), 1)
    if transposed:
        rows, cols = cols, rows
    return (rows == 3 * (cols % width) + cols // width).astype(BF16)


def lane_roll(x, by):
    return pltpu.roll(x, by % x.shape[-1], x.ndim - 1)


def smooth(planes, north, south):
    f0, f1, f2 = planes
    west0 = lane_roll(f2, 1)
    east2 = lane_roll(f0, -1)
    common = f0 + f1
    tail = f1 + f2
    return (
        0.2 * (common + west0 + (north[0] + south[0])),
        0.2 * (common + f2 + (north[1] + south[1])),
        0.2 * (tail + east2 + (north[2] + south[2])),
    )


def spread_level(own, first, last, below, above, live, row_ids, exists):
    top = row_ids == 0
    bottom = row_ids == live - 1
    count = own[0].shape[0]

    def shifted(v, lower, upper):
        north = [jnp.where(top, lo, pltpu.roll(x, 1, 0)) for x, lo in zip(v, lower)]
        south = [jnp.where(bottom, up, pltpu.roll(x, count - 1, 0)) for x, up in zip(v, upper)]
        return north, south

    edge = [b[1:2] for b in below]
    far = [b[0:1] for b in below]
    edge_below = [e * exists[0] for e in smooth(edge, far, first)]
    edge2 = [a[0:1] for a in above]
    far2 = [a[1:2] for a in above]
    edge_above = [e * exists[1] for e in smooth(edge2, last, far2)]
    once = smooth(own, *shifted(own, edge, edge2))
    return smooth(once, *shifted(once, edge_below, edge_above))


def localize_kernel(alpha_ref, perturb_ref, loc_ref, out_ref):
    members, levels, slots, count = alpha_ref.shape
    alpha = alpha_ref[...].reshape(members * levels * slots, count)
    localized = jnp.dot(alpha, loc_ref[...], preferred_element_type=F32)
    width = localized.shape[1]
    perturb = perturb_ref[...].astype(F32).reshape(members * levels * slots, width)
    out_ref[...] = jnp.sum((perturb * localized).reshape(members, levels * slots, width), axis=0)


def split_kernel(scalars_ref, control_ref, innovation_ref, weight_ref, control_out, innovation_out, weight_out, same_out, cross_out):
    own_fine, parity = scalars_ref[1], scalars_ref[3]
    levels, slots, count = control_ref.shape
    width = 128
    table = triple_table(width, False)
    live = (lax.broadcasted_iota(jnp.int32, (levels * slots, 1), 0) % slots < own_fine).astype(F32)
    for block in range(count // (3 * width)):
        span = slice(3 * width * block, 3 * width * (block + 1))
        stacked = jnp.concatenate(
            [r[:, :, span].reshape(levels * slots, 3 * width) for r in (control_ref, innovation_ref, weight_ref)], axis=0
        )
        planes = jnp.dot(stacked, table, preferred_element_type=F32)
        rows = levels * slots
        out = slice(width * block, width * (block + 1))
        for p in range(3):
            part = planes[:, p * width : (p + 1) * width]
            control_out[p, :, :, out] = (part[:rows] * live).reshape(levels, slots, width)
            innovation_out[p, :, :, out] = part[rows : 2 * rows].reshape(levels, slots, width).astype(BF16)
            weight_out[p, :, :, out] = (part[2 * rows :] * live).reshape(levels, slots, width).astype(BF16)
    same_start = jnp.where(parity == 0, own_fine - 2, 0)
    cross_start = jnp.where(parity == 0, 0, own_fine - 2)
    for p in range(3):
        for l in range(levels):
            at = (p * levels + l) * 2
            for k in range(2):
                same_out[at + k : at + k + 1, :] = control_out[p, l, pl.ds(same_start + k, 1), :]
                cross_out[at + k : at + k + 1, :] = control_out[p, l, pl.ds(cross_start + k, 1), :]


def neighbours(scalars_ref):
    device, bands = scalars_ref[2], scalars_ref[4]
    return (device > 0).astype(F32), (device < bands - 1).astype(F32)


def halo_rows(same_ref, cross_ref, scalars_ref, at):
    device, parity, bands = scalars_ref[2], scalars_ref[3], scalars_ref[4]
    same, cross = same_ref[at : at + 2, :], cross_ref[at : at + 2, :]
    below = jnp.where(parity == 0, cross, same) * (device > 0).astype(F32)
    above = jnp.where(parity == 0, same, cross) * (device < bands - 1).astype(F32)
    return below, above


def static_kernel(scalars_ref, control_ref, innovation_ref, same_ref, cross_ref, out_ref):
    own_fine = scalars_ref[1]
    planes, levels, slots, count = control_ref.shape
    row_ids = lax.broadcasted_iota(jnp.int32, (slots, 1), 0)
    exists = neighbours(scalars_ref)
    for l in range(levels):
        halos = [halo_rows(same_ref, cross_ref, scalars_ref, (p * levels + l) * 2) for p in range(3)]
        own = [control_ref[p, l] for p in range(3)]
        first = [control_ref[p, l, 0:1, :] for p in range(3)]
        last = [control_ref[p, l, pl.ds(own_fine - 1, 1), :] for p in range(3)]
        result = spread_level(own, first, last, [h[0] for h in halos], [h[1] for h in halos], own_fine, row_ids, exists)
        for p in range(3):
            out_ref[p, l] = result[p] - innovation_ref[p, l].astype(F32)


def increment_kernel(scalars_ref, own_ref, a_ref, b_ref, c_ref, total_ref, same_out, cross_out):
    own_coarse, parity = scalars_ref[0], scalars_ref[3]
    total_ref[...] = (own_ref[...] + a_ref[...]) + (b_ref[...] + c_ref[...])
    rows = total_ref.shape[0]
    same_start = jnp.where(parity == 0, own_coarse - 2, 0)
    cross_start = jnp.where(parity == 0, 0, own_coarse - 2)
    for l in range(rows // 4):
        for k in range(2):
            same_out[2 * l + k : 2 * l + k + 1, :] = total_ref[pl.ds(4 * l + same_start + k, 1), :]
            cross_out[2 * l + k : 2 * l + k + 1, :] = total_ref[pl.ds(4 * l + cross_start + k, 1), :]


def residual_kernel(
    scalars_ref, source_ref, upper_ref, total_ref, same_ref, cross_ref, static_ref, weight_ref,
    residual_out, back_out, same_out, cross_out, lower_scr, higher_scr,
):
    own_coarse, own_fine, device, parity, bands, first_row = (scalars_ref[i] for i in range(6))
    planes, levels, slots, count = static_ref.shape
    row_ids = lax.broadcasted_iota(jnp.int32, (slots, 1), 0)
    picked = lax.broadcasted_iota(jnp.int32, (slots, slots), 0) == lax.broadcasted_iota(jnp.int32, (slots, slots), 1)
    source = jnp.sum(jnp.where(picked, source_ref[...], 0), axis=1, keepdims=True)
    upper = jnp.sum(jnp.where(picked, upper_ref[...], 0.0), axis=1, keepdims=True)
    live = (row_ids < own_fine).astype(F32)
    low_weight, high_weight = live * (1.0 - upper), live * upper
    latitudes = [first_row - 2, first_row - 1] + [first_row + s for s in range(4)]
    latitudes += [first_row + own_coarse, first_row + own_coarse + 1]
    usable = [device > 0] * 2 + [s < own_coarse for s in range(4)] + [device < bands - 1] * 2
    coefficients = [
        (jnp.where(source == lat, low_weight, 0.0) + jnp.where(source + 1 == lat, high_weight, 0.0)) * ok.astype(F32)
        for lat, ok in zip(latitudes, usable)
    ]
    for l in range(levels):
        below, above = halo_rows(same_ref, cross_ref, scalars_ref, 2 * l)
        rows = [below[0:1], below[1:2]] + [total_ref[4 * l + s : 4 * l + s + 1, :] for s in range(4)]
        rows += [above[0:1], above[1:2]]
        band = coefficients[0] * rows[0]
        for c, r in zip(coefficients[1:], rows[1:]):
            band = band + c * r
        following = lane_roll(band, -1)
        fine = (band, (2.0 * band + following) * THIRD, (band + 2.0 * following) * THIRD)
        residual = []
        for p in range(3):
            value = weight_ref[p, l].astype(F32) * (fine[p] + static_ref[p, l])
            value = jnp.where(row_ids < own_fine, value, 0.0)
            residual_out[p, l] = value
            residual.append(value)
        g0, g1, g2 = residual
        back = (g0 + g1 * (2.0 * THIRD) + g2 * THIRD) + lane_roll(g1 * THIRD + g2 * (2.0 * THIRD), 1)
        sums = [jnp.sum(c * back, axis=0, keepdims=True) for c in coefficients]
        for s in range(4):
            back_out[4 * l + s : 4 * l + s + 1, :] = sums[2 + s]
        for k in range(2):
            lower_scr[2 * l + k : 2 * l + k + 1, :] = sums[k]
            higher_scr[2 * l + k : 2 * l + k + 1, :] = sums[6 + k]
    same_start = jnp.where(parity == 0, own_fine - 2, 0)
    cross_start = jnp.where(parity == 0, 0, own_fine - 2)
    for p in range(3):
        for l in range(levels):
            at = (p * levels + l) * 2
            for k in range(2):
                same_out[at + k : at + k + 1, :] = residual_out[p, l, pl.ds(same_start + k, 1), :]
                cross_out[at + k : at + k + 1, :] = residual_out[p, l, pl.ds(cross_start + k, 1), :]
    lower, higher = lower_scr[...], higher_scr[...]
    at = 3 * levels * 2
    same_out[at : at + 2 * levels, :] = jnp.where(parity == 0, higher, lower)
    cross_out[at : at + 2 * levels, :] = jnp.where(parity == 0, lower, higher)


def gradient_kernel(scalars_ref, back_ref, same_ref, cross_ref, alpha_ref, perturb_ref, loc_ref, out_ref, full_scr):
    own_coarse, device, parity, bands = scalars_ref[0], scalars_ref[2], scalars_ref[3], scalars_ref[4]
    members, levels, slots, count = perturb_ref.shape
    at = 3 * levels * 2
    same, cross = same_ref[at : at + 2 * levels, :], cross_ref[at : at + 2 * levels, :]
    below = jnp.where(parity == 0, cross, same) * (device > 0).astype(F32)
    above = jnp.where(parity == 0, same, cross) * (device < bands - 1).astype(F32)
    full_scr[...] = back_ref[...]
    for l in range(levels):
        full_scr[4 * l : 4 * l + 2, :] += below[2 * l : 2 * l + 2]
        for k in range(2):
            full_scr[pl.ds(4 * l + own_coarse - 2 + k, 1), :] += above[2 * l + k : 2 * l + k + 1]
    rows = members * levels * slots
    perturb = perturb_ref[...].astype(F32).reshape(members, levels * slots, count)
    schur = (perturb * full_scr[...][None]).astype(BF16).reshape(rows, count)
    pulled = lax.dot_general(schur, loc_ref[...], (((1,), (1,)), ((), ())), preferred_element_type=F32)
    width = pulled.shape[1]
    alpha = alpha_ref[...].astype(F32).reshape(rows, width)
    live = (lax.broadcasted_iota(jnp.int32, (rows, 1), 0) % slots < own_coarse).astype(F32)
    out_ref[...] = ((alpha + pulled) * live).reshape(members, levels, slots, width).astype(BF16)


def final_kernel(scalars_ref, control_ref, residual_ref, same_ref, cross_ref, out_ref, grad_scr):
    own_fine = scalars_ref[1]
    planes, levels, slots, count = control_ref.shape
    row_ids = lax.broadcasted_iota(jnp.int32, (slots, 1), 0)
    exists = neighbours(scalars_ref)
    for l in range(levels):
        halos = [halo_rows(same_ref, cross_ref, scalars_ref, (p * levels + l) * 2) for p in range(3)]
        own = [residual_ref[p, l] for p in range(3)]
        first = [residual_ref[p, l, 0:1, :] for p in range(3)]
        last = [residual_ref[p, l, pl.ds(own_fine - 1, 1), :] for p in range(3)]
        result = spread_level(own, first, last, [h[0] for h in halos], [h[1] for h in halos], own_fine, row_ids, exists)
        for p in range(3):
            grad_scr[p, l] = jnp.where(row_ids < own_fine, control_ref[p, l] + result[p], 0.0)
    width = 128
    table = triple_table(width, True)
    for block in range(count // width):
        span = slice(width * block, width * (block + 1))
        joined = jnp.concatenate([grad_scr[p, :, :, span].reshape(levels * slots, width) for p in range(3)], axis=1)
        high = joined.astype(BF16)
        low = (joined - high.astype(F32)).astype(BF16)
        mixed = jnp.dot(high, table, preferred_element_type=F32) + jnp.dot(low, table, preferred_element_type=F32)
        out_ref[:, :, 3 * width * block : 3 * width * (block + 1)] = mixed.reshape(levels, slots, 3 * width)


def on_device(
    perturb, alpha_control, loc_factor, static_control, innovation, obs_weight, coarse_rows, fine_rows, source_row, row_weight
):
    device = lax.axis_index("band")
    bands = lax.axis_size("band")
    members, levels, slots, count = perturb.shape
    fine_slots = static_control.shape[1]
    here = jnp.arange(bands, dtype=jnp.int32)
    counts = jnp.stack([
        jnp.sum(jnp.where(here == device, coarse_rows, 0)),
        jnp.sum(jnp.where(here == device, fine_rows, 0)),
        device,
        device % 2,
        jnp.int32(bands),
        jnp.sum(jnp.where(here < device, coarse_rows, 0)),
    ]).astype(jnp.int32)
    rows = levels * slots
    chunk = 256
    steps = count // chunk

    partial = pl.pallas_call(
        localize_kernel,
        out_shape=jax.ShapeDtypeStruct((rows, count), F32),
        grid=(steps,),
        in_specs=[
            pl.BlockSpec((members, levels, slots, count), lambda i: (0, 0, 0, 0)),
            pl.BlockSpec((members, levels, slots, chunk), lambda i: (0, 0, 0, i)),
            pl.BlockSpec((count, chunk), lambda i: (0, i)),
        ],
        out_specs=pl.BlockSpec((rows, chunk), lambda i: (0, i)),
        compiler_params=params(24),
    )(alpha_control, perturb, loc_factor)
    peers = [mem_peer(partial, by) for by in (1, 2, 3)]

    plane = (3, levels, fine_slots, count)
    wide = jax.ShapeDtypeStruct((6 * levels, count), F32)
    control, innovation_planes, weight_planes, control_same, control_cross = pl.pallas_call(
        split_kernel,
        out_shape=(
            jax.ShapeDtypeStruct(plane, F32), jax.ShapeDtypeStruct(plane, BF16), jax.ShapeDtypeStruct(plane, BF16), wide, wide
        ),
        in_specs=[SMEM, VMEM, VMEM, VMEM],
        out_specs=(VMEM,) * 5,
        compiler_params=params(24),
    )(counts, static_control, innovation, obs_weight)
    control_from_same = same_chip(control_same)
    control_from_cross = cross_chip(control_cross)
    static_minus = pl.pallas_call(
        static_kernel,
        out_shape=jax.ShapeDtypeStruct(plane, F32),
        in_specs=[SMEM, VMEM, VMEM, VMEM, VMEM],
        out_specs=VMEM,
        compiler_params=params(24),
    )(counts, control, innovation_planes, control_from_same, control_from_cross)

    pair = jax.ShapeDtypeStruct((2 * levels, count), F32)
    total, total_same, total_cross = pl.pallas_call(
        increment_kernel,
        out_shape=(jax.ShapeDtypeStruct((rows, count), F32), pair, pair),
        in_specs=[SMEM] + [VMEM] * 4,
        out_specs=(VMEM,) * 3,
        compiler_params=params(24),
    )(counts, partial, *peers)
    total_from_same = same_chip(total_same)
    total_from_cross = cross_chip(total_cross)

    outgoing = jax.ShapeDtypeStruct((8 * levels, count), F32)
    residual, back, residual_same, residual_cross = pl.pallas_call(
        residual_kernel,
        out_shape=(jax.ShapeDtypeStruct(plane, F32), jax.ShapeDtypeStruct((rows, count), F32), outgoing, outgoing),
        in_specs=[SMEM] + [VMEM] * 7,
        out_specs=(VMEM,) * 4,
        scratch_shapes=[pltpu.VMEM((2 * levels, count), F32), pltpu.VMEM((2 * levels, count), F32)],
        compiler_params=params(24),
    )(
        counts, source_row.reshape(1, fine_slots), row_weight.reshape(1, fine_slots), total, total_from_same, total_from_cross,
        static_minus, weight_planes,
    )
    from_same = same_chip(residual_same)
    from_cross = cross_chip(residual_cross)

    grad_alpha = pl.pallas_call(
        gradient_kernel,
        out_shape=jax.ShapeDtypeStruct(perturb.shape, BF16),
        grid=(steps,),
        in_specs=[
            SMEM,
            pl.BlockSpec((rows, count), lambda i: (0, 0)),
            pl.BlockSpec((8 * levels, count), lambda i: (0, 0)),
            pl.BlockSpec((8 * levels, count), lambda i: (0, 0)),
            pl.BlockSpec((members, levels, slots, chunk), lambda i: (0, 0, 0, i)),
            pl.BlockSpec((members, levels, slots, count), lambda i: (0, 0, 0, 0)),
            pl.BlockSpec((chunk, count), lambda i: (i, 0)),
        ],
        out_specs=pl.BlockSpec((members, levels, slots, chunk), lambda i: (0, 0, 0, i)),
        scratch_shapes=[pltpu.VMEM((rows, count), F32)],
        compiler_params=params(24),
    )(counts, back, from_same, from_cross, alpha_control, perturb, loc_factor)

    grad_static = pl.pallas_call(
        final_kernel,
        out_shape=jax.ShapeDtypeStruct(static_control.shape, F32),
        in_specs=[SMEM] + [VMEM] * 4,
        out_specs=VMEM,
        scratch_shapes=[pltpu.VMEM(plane, F32)],
        compiler_params=params(24),
    )(counts, control, residual, from_same, from_cross)
    return (grad_alpha, grad_static)


def solution(mesh):
    placed = (
        P("mem", None, "band", None),
        P("mem", None, "band", None),
        P(),
        P(None, "band", None),
        P(None, "band", None),
        P(None, "band", None),
        P(),
        P(),
        P("band"),
        P("band"),
    )
    return jax.shard_map(
        on_device,
        mesh=mesh,
        in_specs=placed,
        out_specs=(P("mem", None, "band", None), P(None, "band", None)),
        check_vma=False,
    )
```

time: 126 us -> 54.3 us (0.43)
  the two profiles are of different devices: /device:TPU:6 before, /device:TPU:8 now
where the time goes in v1:
time: 54.3 us; the launch traced here: 54.1 us
  Pallas kernels  19.2 us (35%)
  starting transfers between devices  17.4 us (32%)
  waiting for transfers between devices  9.37 us (17%)
  local copies, waits for them, and re-layouts  6.69 us (12%)
  between operations  0.78 us (1%)
  other arithmetic  0.68 us (1%)
    ppermute x3, starting transfers between devices, cross_chip(): return lax.ppermute(x, 'band', pairs + [(j, i) for i, j in pairs])  12.1 us
    ppermute x3, waiting for transfers between devices, cross_chip(): return lax.ppermute(x, 'band', pairs + [(j, i) for i, j in pairs])  9.35 us
    ppermute x3, starting transfers between devices, mem_peer(): return lax.ppermute(x, 'mem', [(i, (i + by) % peers) for i in range(peers)])  5 us
    pallas_call x1, Pallas kernels, on_device(): pl.pallas_call(gradient_kernel, out_shape=jax.ShapeDtypeStruct(perturb.sh...  4.85 us
    unnamed x28, local copies, waits for them, and re-layouts  4.78 us
    pallas_call x1, Pallas kernels, on_device(): pl.pallas_call(final_kernel, out_shape=jax.ShapeDtypeStruct(static_contro...  4.33 us
    pallas_call x1, Pallas kernels, on_device(): pl.pallas_call(localize_kernel, out_shape=jax.ShapeDtypeStruct((rows, cou...  3.16 us
    pallas_call x1, Pallas kernels, on_device(): pl.pallas_call(static_kernel, out_shape=jax.ShapeDtypeStruct(plane, F32),...  2.3 us
  transfers between devices with their start and end apart: 9, of which 3 were waited for; matrix products, arithmetic and copies ran while one was open for 5% of the time, Pallas kernels for 9%

profile of v1, /device:TPU:8, one launch (start us, length us, event | category | flops | bytes accessed | tf_op | source)
XLA Modules:
  0.0 54.1 jit_solution(9140380310076064138)
XLA Ops:
  0.6 2.3 %copy-done = bf16[1536,1536]{1,0:T(8,128)(2,1)S(1)} copy-done((bf16[1536,1536]{1,0:T(8,128)(2,1)S(1)}, bf16[1536,1536]{1,0:T(8,128)(2,1)}, u32[]{:S(2)}) %copy-start) | copy-done | bytes 4718616
  3.0 1.2 %copy-done.1 = bf16[20,4,4,1536]{3,2,1,0:T(4,128)(2,1)S(1)} copy-done((bf16[20,4,4,1536]{3,2,1,0:T(4,128)(2,1)S(1)}, bf16[20,4,4,1536]{3,2,1,0:T(4,128)(2,1)}, u32[]{:S(2)}) %copy-start.1) | copy-done | bytes 983064
  4.2 1.2 %copy-done.3 = bf16[20,4,4,1536]{3,2,1,0:T(4,128)(2,1)S(1)} copy-done((bf16[20,4,4,1536]{3,2,1,0:T(4,128)(2,1)S(1)}, bf16[20,4,4,1536]{3,2,1,0:T(4,128)(2,1)}, u32[]{:S(2)}) %copy-start.3) | copy-done | bytes 983064
  5.4 3.2 %shard_map.113.own_ref = f32[16,1536]{1,0:T(8,128)S(1)} custom-call(bf16[20,4,4,1536]{3,2,1,0:T(4,128)(2,1)S(1)} %copy-done.1, bf16[20,4,4,1536]{3,2,1,0:T(4,128)(2,1)S(1)} %copy-done.3, bf16[1536,1536]{1,0:T(8,128)(2,1)S(1)} %copy-done), custom_call_target="tpu_custom_call" | custom-call | tf_op jit(solution)/shard_map/pallas_call | solution.py:280
  8.6 2.3 %collective-permute-start.2 = (f32[16,1536]{1,0:T(8,128)S(1)}, f32[16,1536]{1,0:T(8,128)S(1)}, u32[]{:S(2)}, u32[]{:S(2)}) collective-permute-start(f32[16,1536]{1,0:T(8,128)S(1)} %shard_map.113.own_ref), channel_id=1, source_target_pairs={{0,3},{1,0},{2,1},{3,2},{4,7},{5,4},{6,5},{7,6},{8,11},{9,8},{10,9... | collective-permute-start | bytes 294920 | tf_op jit(solution)/shard_map/ppermute | solution.py:32
  10.8 0.9 %collective-permute-start.1 = (f32[16,1536]{1,0:T(8,128)S(1)}, f32[16,1536]{1,0:T(8,128)S(1)}, u32[]{:S(2)}, u32[]{:S(2)}) collective-permute-start(f32[16,1536]{1,0:T(8,128)S(1)} %shard_map.113.own_ref), channel_id=1, source_target_pairs={{0,2},{1,3},{2,0},{3,1},{4,6},{5,7},{6,4},{7,5},{8,10},{9,11},{10,... | collective-permute-start | bytes 294920 | tf_op jit(solution)/shard_map/ppermute | solution.py:32
  11.7 1.9 %collective-permute-start = (f32[16,1536]{1,0:T(8,128)S(1)}, f32[16,1536]{1,0:T(8,128)S(1)}, u32[]{:S(2)}, u32[]{:S(2)}) collective-permute-start(f32[16,1536]{1,0:T(8,128)S(1)} %shard_map.113.own_ref), channel_id=1, source_target_pairs={{0,1},{1,2},{2,3},{3,0},{4,5},{5,6},{6,7},{7,4},{8,9},{9,10},{10,1... | collective-permute-start | bytes 294920 | tf_op jit(solution)/shard_map/ppermute | solution.py:32
  13.6 0.7 %fusion.2 = (s32[]{:T(128)}, s32[]{:T(128)}, s32[]{:T(128)}) fusion(s32[64]{0:T(128)S(1)} %copy-done.10, s32[]{:T(128)} %axis_index.15, s32[64]{0:T(128)S(1)} %copy-done.11), kind=kLoop, calls=%fused_computation.5 | loop fusion | flops 509 | bytes 528 | tf_op jit(solution)/shard_map/reduce_sum | solution.py:274
  14.3 1.9 %stack.23.scalars_ref = s32[6]{0:T(128)S(1)} concatenate(s32[1]{0:T(128)} %bitcast, s32[1]{0:T(128)} %bitcast.1, s32[1]{0:T(128)} %bitcast.2, s32[1]{0:T(128)} %bitcast.3, s32[1]{0:T(128)} %constant.21.clone.1, s32[1]{0:T(128)} %bitcast.4), dimensions={0} | concatenate | bytes 48 | tf_op jit(solution)/shard_map/stack | solution.py:268
  16.2 1.9 %shard_map.115 = (f32[3,4,16,1536]{3,2,1,0:T(8,128)S(1)}, bf16[3,4,16,1536]{3,2,1,0:T(8,128)(2,1)S(1)}, bf16[3,4,16,1536]{3,2,1,0:T(8,128)(2,1)S(1)}, f32[24,1536]{1,0:T(8,128)S(1)}, f32[24,1536]{1,0:T(8,128)S(1)}) custom-call(s32[6]{0:T(128)S(1)} %stack.23.scalars_ref, bf16[4,16,4608]{2,1,0:T(8,128)(2,1)S(1)} %copy-done.5, ...), custom_call_target="tpu_custom_call" | custom-call | tf_op jit(solution)/shard_map/pallas_call | solution.py:296
  18.1 0.1 collective-permute-start.5
  18.2 8.2 %collective-permute-start.6 = (f32[24,1536]{1,0:T(8,128)S(1)}, f32[24,1536]{1,0:T(8,128)S(1)}, u32[]{:S(2)}, u32[]{:S(2)}) collective-permute-start(f32[24,1536]{1,0:T(8,128)S(1)} %get-tuple-element.20), channel_id=1, source_target_pairs={{4,8},{12,16},{20,24},{28,32},{36,40},{44,48},{52,56},{60,64},{68,... | collective-permute-start | bytes 442376 | tf_op jit(solution)/shard_map/ppermute | solution.py:27
  26.4 0.6 %shard_map.114 = (f32[16,1536]{1,0:T(8,128)S(1)}, f32[8,1536]{1,0:T(8,128)S(1)}, f32[8,1536]{1,0:T(8,128)S(1)}) custom-call(s32[6]{0:T(128)S(1)} %stack.23.scalars_ref, f32[16,1536]{1,0:T(8,128)S(1)} %shard_map.113.own_ref, f32[16,1536]{1,0:T(8,128)S(1)} %collective-permute-done.a_ref, f32[16,1536]{1,0:T(8,128)S(1)} %collective-permute-done.1.b_ref, ...), custom_call_target="tpu_custom_call" | custom-call | tf_op jit(solution)/shard_map/pallas_call | solution.py:316
  27.0 0.1 collective-permute-start.3
  27.1 1.1 %collective-permute-start.4 = (f32[8,1536]{1,0:T(8,128)S(1)}, f32[8,1536]{1,0:T(8,128)S(1)}, u32[]{:S(2)}, u32[]{:S(2)}) collective-permute-start(f32[8,1536]{1,0:T(8,128)S(1)} %get-tuple-element.16), channel_id=1, source_target_pairs={{4,8},{12,16},{20,24},{28,32},{36,40},{44,48},{52,56},{60,64},{68,... | collective-permute-start | bytes 147464 | tf_op jit(solution)/shard_map/ppermute | solution.py:27
  28.2 1.0 %collective-permute-done.6.cross_ref = f32[24,1536]{1,0:T(8,128)S(1)} collective-permute-done((f32[24,1536]{1,0:T(8,128)S(1)}, f32[24,1536]{1,0:T(8,128)S(1)}, u32[]{:S(2)}, u32[]{:S(2)}) %collective-permute-start.6) | collective-permute-done | bytes 147488 | tf_op jit(solution)/shard_map/ppermute | solution.py:27
  29.2 2.3 %shard_map.116.static_ref = f32[3,4,16,1536]{3,2,1,0:T(8,128)S(1)} custom-call(s32[6]{0:T(128)S(1)} %stack.23.scalars_ref, f32[3,4,16,1536]{3,2,1,0:T(8,128)S(1)} %get-tuple-element.17.control_ref, bf16[3,4,16,1536]{3,2,1,0:T(8,128)(2,1)S(1)} %get-tuple-element.18.innovation_ref, f32[24,1536]{1,0:T(8,128)S(1)} %collective-permute-done.5.same_ref, ...), custom_call_target="tpu_custom_call" | custom-call | tf_op jit(solution)/shard_map/pallas_call | solution.py:307
  31.5 2.5 %collective-permute-done.4.cross_ref = f32[8,1536]{1,0:T(8,128)S(1)} collective-permute-done((f32[8,1536]{1,0:T(8,128)S(1)}, f32[8,1536]{1,0:T(8,128)S(1)}, u32[]{:S(2)}, u32[]{:S(2)}) %collective-permute-start.4) | collective-permute-done | bytes 49184 | tf_op jit(solution)/shard_map/ppermute | solution.py:27
  34.0 2.0 %shard_map.117 = (f32[3,4,16,1536]{3,2,1,0:T(8,128)S(1)}, f32[16,1536]{1,0:T(8,128)S(1)}, f32[32,1536]{1,0:T(8,128)S(1)}, f32[32,1536]{1,0:T(8,128)S(1)}) custom-call(s32[6]{0:T(128)S(1)} %stack.23.scalars_ref, s32[1,16]{1,0:T(1,128)S(1)} %bitcast.9, f32[1,16]{1,0:T(1,128)S(1)} %bitcast.10, f32[16,1536]{1,0:T(8,128)S(1)} %get-tuple-element.14.total_ref, ...), custom_call_target="tpu_custom_call" | custom-call | tf_op jit(solution)/shard_map/pallas_call | solution.py:327
  36.1 0.1 collective-permute-start.7
  36.2 2.8 %collective-permute-start.8 = (f32[32,1536]{1,0:T(8,128)S(1)}, f32[32,1536]{1,0:T(8,128)S(1)}, u32[]{:S(2)}, u32[]{:S(2)}) collective-permute-start(f32[32,1536]{1,0:T(8,128)S(1)} %get-tuple-element.24), channel_id=1, source_target_pairs={{4,8},{12,16},{20,24},{28,32},{36,40},{44,48},{52,56},{60,64},{68,... | collective-permute-start | bytes 589832 | tf_op jit(solution)/shard_map/ppermute | solution.py:27
  39.0 5.8 %collective-permute-done.8.cross_ref = f32[32,1536]{1,0:T(8,128)S(1)} collective-permute-done((f32[32,1536]{1,0:T(8,128)S(1)}, f32[32,1536]{1,0:T(8,128)S(1)}, u32[]{:S(2)}, u32[]{:S(2)}) %collective-permute-start.8) | collective-permute-done | bytes 196640 | tf_op jit(solution)/shard_map/ppermute | solution.py:27
  44.8 4.3 %shard_map.119 = f32[4,16,4608]{2,1,0:T(8,128)} custom-call(s32[6]{0:T(128)S(1)} %stack.23.scalars_ref, f32[3,4,16,1536]{3,2,1,0:T(8,128)S(1)} %get-tuple-element.17.control_ref, f32[3,4,16,1536]{3,2,1,0:T(8,128)S(1)} %get-tuple-element.25.residual_ref, f32[32,1536]{1,0:T(8,128)S(1)} %collective-permute-done.7.same_ref, ...), custom_call_target="tpu_custom_call" | custom-call | tf_op jit(solution)/shard_map/pallas_call | solution.py:359
  49.2 4.8 %shard_map.118 = bf16[20,4,4,1536]{3,2,1,0:T(4,128)(2,1)} custom-call(s32[6]{0:T(128)S(1)} %stack.23.scalars_ref, f32[16,1536]{1,0:T(8,128)S(1)} %get-tuple-element.22.back_ref, f32[32,1536]{1,0:T(8,128)S(1)} %collective-permute-done.7.same_ref, f32[32,1536]{1,0:T(8,128)S(1)} %collective-permute-done.8.cross_ref, bf16[20,4,4,1536]{3,2,1,0:T(4,128)(2,1)S(1)} %copy-done.2, ...), custom_call_target="tpu_custom_call" | custom-call | tf_op jit(solution)/shard_map/pallas_call | solution.py:341
  (32 shorter events, 0.1 us)
Async XLA Ops:
  0.6 2.3 %copy-start = (bf16[1536,1536]{1,0:T(8,128)(2,1)S(1)}, bf16[1536,1536]{1,0:T(8,128)(2,1)}, u32[]{:S(2)}) copy-start(bf16[1536,1536]{1,0:T(8,128)(2,1)} %loc_ref.3) | copy-start | bytes 14155780
  3.0 1.2 %copy-start.1 = (bf16[20,4,4,1536]{3,2,1,0:T(4,128)(2,1)S(1)}, bf16[20,4,4,1536]{3,2,1,0:T(4,128)(2,1)}, u32[]{:S(2)}) copy-start(bf16[20,4,4,1536]{3,2,1,0:T(4,128)(2,1)} %alpha_ref.3) | copy-start | bytes 2949124
  4.2 1.2 %copy-start.3 = (bf16[20,4,4,1536]{3,2,1,0:T(4,128)(2,1)S(1)}, bf16[20,4,4,1536]{3,2,1,0:T(4,128)(2,1)}, u32[]{:S(2)}) copy-start(bf16[20,4,4,1536]{3,2,1,0:T(4,128)(2,1)} %perturb_ref.3) | copy-start | bytes 2949124
  5.4 8.2 %copy-start.10 = (s32[64]{0:T(128)S(1)}, s32[64]{0:T(128)}, u32[]{:S(2)}) copy-start(s32[64]{0:T(128)} %param.16) | copy-start | bytes 772
  5.4 8.2 %copy-start.11 = (s32[64]{0:T(128)S(1)}, s32[64]{0:T(128)}, u32[]{:S(2)}) copy-start(s32[64]{0:T(128)} %param.17) | copy-start | bytes 772
  5.4 10.8 %copy-start.5 = (bf16[4,16,4608]{2,1,0:T(8,128)(2,1)S(1)}, bf16[4,16,4608]{2,1,0:T(8,128)(2,1)}, u32[]{:S(2)}) copy-start(bf16[4,16,4608]{2,1,0:T(8,128)(2,1)} %control_ref.1) | copy-start | bytes 1769476
  5.4 10.8 %copy-start.6 = (bf16[4,16,4608]{2,1,0:T(8,128)(2,1)S(1)}, bf16[4,16,4608]{2,1,0:T(8,128)(2,1)}, u32[]{:S(2)}) copy-start(bf16[4,16,4608]{2,1,0:T(8,128)(2,1)} %innovation_ref.1) | copy-start | bytes 1769476
  5.4 10.8 %copy-start.7 = (bf16[4,16,4608]{2,1,0:T(8,128)(2,1)S(1)}, bf16[4,16,4608]{2,1,0:T(8,128)(2,1)}, u32[]{:S(2)}) copy-start(bf16[4,16,4608]{2,1,0:T(8,128)(2,1)} %weight_ref.1) | copy-start | bytes 1769476
  5.4 43.8 %slice-start = ((s8[4718592]{0:T(1024)(128)(4,1)}), s8[524288]{0:T(1024)(128)(4,1)S(1)}, s32[]{:S(2)}) async-start(s8[4718592]{0:T(1024)(128)(4,1)} %bitcast.7), calls=%async_computation | async-start | bytes 1048576
  8.6 17.8 %collective-permute-start.2 = (f32[16,1536]{1,0:T(8,128)S(1)}, f32[16,1536]{1,0:T(8,128)S(1)}, u32[]{:S(2)}, u32[]{:S(2)}) collective-permute-start(f32[16,1536]{1,0:T(8,128)S(1)} %shard_map.113.own_ref), channel_id=1, source_target_pairs={{0,3},{1,0},{2,1},{3,2},{4,7},{5,4},{6,5},{7,6},{8,11},{9,8},{10,9... | collective-permute-start | bytes 294920 | tf_op jit(solution)/shard_map/ppermute | solution.py:32
  10.8 15.5 %collective-permute-start.1 = (f32[16,1536]{1,0:T(8,128)S(1)}, f32[16,1536]{1,0:T(8,128)S(1)}, u32[]{:S(2)}, u32[]{:S(2)}) collective-permute-start(f32[16,1536]{1,0:T(8,128)S(1)} %shard_map.113.own_ref), channel_id=1, source_target_pairs={{0,2},{1,3},{2,0},{3,1},{4,6},{5,7},{6,4},{7,5},{8,10},{9,11},{10,... | collective-permute-start | bytes 294920 | tf_op jit(solution)/shard_map/ppermute | solution.py:32
  11.7 14.7 %collective-permute-start = (f32[16,1536]{1,0:T(8,128)S(1)}, f32[16,1536]{1,0:T(8,128)S(1)}, u32[]{:S(2)}, u32[]{:S(2)}) collective-permute-start(f32[16,1536]{1,0:T(8,128)S(1)} %shard_map.113.own_ref), channel_id=1, source_target_pairs={{0,1},{1,2},{2,3},{3,0},{4,5},{5,6},{6,7},{7,4},{8,9},{9,10},{10,1... | collective-permute-start | bytes 294920 | tf_op jit(solution)/shard_map/ppermute | solution.py:32
  18.1 10.1 %collective-permute-start.5 = (f32[24,1536]{1,0:T(8,128)S(1)}, f32[24,1536]{1,0:T(8,128)S(1)}, u32[]{:S(2)}, u32[]{:S(2)}) collective-permute-start(f32[24,1536]{1,0:T(8,128)S(1)} %get-tuple-element.19), channel_id=1, source_target_pairs={{0,4},{4,0},{8,12},{12,8},{16,20},{20,16},{24,28},{28,24},{32,36},... | collective-permute-start | bytes 442376 | tf_op jit(solution)/shard_map/ppermute | solution.py:21
  18.2 11.0 %collective-permute-start.6 = (f32[24,1536]{1,0:T(8,128)S(1)}, f32[24,1536]{1,0:T(8,128)S(1)}, u32[]{:S(2)}, u32[]{:S(2)}) collective-permute-start(f32[24,1536]{1,0:T(8,128)S(1)} %get-tuple-element.20), channel_id=1, source_target_pairs={{4,8},{12,16},{20,24},{28,32},{36,40},{44,48},{52,56},{60,64},{68,... | collective-permute-start | bytes 442376 | tf_op jit(solution)/shard_map/ppermute | solution.py:27
  26.4 7.7 %copy-start.8 = (s32[16]{0:T(128)S(1)}, s32[16]{0:T(128)}, u32[]{:S(2)}) copy-start(s32[16]{0:T(128)} %param.18) | copy-start | bytes 196
  26.4 7.6 %copy-start.9 = (f32[16]{0:T(128)S(1)}, f32[16]{0:T(128)}, u32[]{:S(2)}) copy-start(f32[16]{0:T(128)} %param.19) | copy-start | bytes 196
  27.0 4.5 %collective-permute-start.3 = (f32[8,1536]{1,0:T(8,128)S(1)}, f32[8,1536]{1,0:T(8,128)S(1)}, u32[]{:S(2)}, u32[]{:S(2)}) collective-permute-start(f32[8,1536]{1,0:T(8,128)S(1)} %get-tuple-element.15), channel_id=1, source_target_pairs={{0,4},{4,0},{8,12},{12,8},{16,20},{20,16},{24,28},{28,24},{32,36},... | collective-permute-start | bytes 147464 | tf_op jit(solution)/shard_map/ppermute | solution.py:21
  27.1 6.9 %collective-permute-start.4 = (f32[8,1536]{1,0:T(8,128)S(1)}, f32[8,1536]{1,0:T(8,128)S(1)}, u32[]{:S(2)}, u32[]{:S(2)}) collective-permute-start(f32[8,1536]{1,0:T(8,128)S(1)} %get-tuple-element.16), channel_id=1, source_target_pairs={{4,8},{12,16},{20,24},{28,32},{36,40},{44,48},{52,56},{60,64},{68,... | collective-permute-start | bytes 147464 | tf_op jit(solution)/shard_map/ppermute | solution.py:27
  29.2 20.0 %slice-start.1 = ((s8[4718592]{0:T(1024)(128)(4,1)}), s8[4194304]{0:T(1024)(128)(4,1)S(1)}, s32[]{:S(2)}) async-start(s8[4718592]{0:T(1024)(128)(4,1)} %bitcast.7), calls=%async_computation.1 | async-start | bytes 8388608
  36.1 2.9 %collective-permute-start.7 = (f32[32,1536]{1,0:T(8,128)S(1)}, f32[32,1536]{1,0:T(8,128)S(1)}, u32[]{:S(2)}, u32[]{:S(2)}) collective-permute-start(f32[32,1536]{1,0:T(8,128)S(1)} %get-tuple-element.23), channel_id=1, source_target_pairs={{0,4},{4,0},{8,12},{12,8},{16,20},{20,16},{24,28},{28,24},{32,36},... | collective-permute-start | bytes 589832 | tf_op jit(solution)/shard_map/ppermute | solution.py:21
  36.2 8.7 %collective-permute-start.8 = (f32[32,1536]{1,0:T(8,128)S(1)}, f32[32,1536]{1,0:T(8,128)S(1)}, u32[]{:S(2)}, u32[]{:S(2)}) collective-permute-start(f32[32,1536]{1,0:T(8,128)S(1)} %get-tuple-element.24), channel_id=1, source_target_pairs={{4,8},{12,16},{20,24},{28,32},{36,40},{44,48},{52,56},{60,64},{68,... | collective-permute-start | bytes 589832 | tf_op jit(solution)/shard_map/ppermute | solution.py:27
  44.8 4.3 %copy-start.2 = (bf16[20,4,4,1536]{3,2,1,0:T(4,128)(2,1)S(1)}, bf16[20,4,4,1536]{3,2,1,0:T(4,128)(2,1)}, u32[]{:S(2)}) copy-start(bf16[20,4,4,1536]{3,2,1,0:T(4,128)(2,1)} %alpha_ref.3) | copy-start | bytes 2949124
  44.8 4.3 %copy-start.4 = (bf16[20,4,4,1536]{3,2,1,0:T(4,128)(2,1)S(1)}, bf16[20,4,4,1536]{3,2,1,0:T(4,128)(2,1)}, u32[]{:S(2)}) copy-start(bf16[20,4,4,1536]{3,2,1,0:T(4,128)(2,1)} %perturb_ref.3) | copy-start | bytes 2949124

commit v2 on v1

v2 whole, which is shorter than its diff:
```python
import jax
import jax.numpy as jnp
from jax import lax
from jax.experimental import pallas as pl
from jax.experimental.pallas import tpu as pltpu
from jax.sharding import PartitionSpec as P

F32 = jnp.float32
BF16 = jnp.bfloat16
THIRD = 1.0 / 3.0
VMEM = pl.BlockSpec(memory_space=pltpu.VMEM)
SMEM = pl.BlockSpec(memory_space=pltpu.SMEM)
HBM = pl.BlockSpec(memory_space=pltpu.HBM)


def params(mib):
    return pltpu.CompilerParams(vmem_limit_bytes=mib << 20)


def same_chip(x):
    peers = lax.axis_size("band")
    return lax.ppermute(x, "band", [(i, i ^ 1) for i in range(peers)])


def cross_chip(x):
    bands, mems = lax.axis_size("band"), lax.axis_size("mem")
    pairs = []
    for m in range(mems):
        pairs += [(i * mems + m, (i + 1) * mems + m) for i in range(1, bands - 1, 2)]
        pairs += [((i + 1) * mems + m, i * mems + m) for i in range(1, bands - 1, 2)]
        pairs += [(i * mems + m, i * mems + (m ^ 1)) for i in (0, bands - 1)]
    return lax.ppermute(x, ("band", "mem"), pairs)


def mem_peer(x, by):
    peers = lax.axis_size("mem")
    return lax.ppermute(x, "mem", [(i, (i + by) % peers) for i in range(peers)])


def triple_table(width, transposed):
    rows = lax.broadcasted_iota(jnp.int32, (3 * width, 3 * width), 0)
    cols = lax.broadcasted_iota(jnp.int32, (3 * width, 3 * width), 1)
    if transposed:
        rows, cols = cols, rows
    return (rows == 3 * (cols % width) + cols // width).astype(BF16)


def lane_roll(x, by):
    return pltpu.roll(x, by % x.shape[-1], x.ndim - 1)


def smooth(planes, north, south):
    f0, f1, f2 = planes
    west0 = lane_roll(f2, 1)
    east2 = lane_roll(f0, -1)
    common = f0 + f1
    tail = f1 + f2
    return (
        0.2 * (common + west0 + (north[0] + south[0])),
        0.2 * (common + f2 + (north[1] + south[1])),
        0.2 * (tail + east2 + (north[2] + south[2])),
    )


def spread_own(own, first, last, live, row_ids, exists):
    top = row_ids == 0
    bottom = row_ids == live - 1
    count = own[0].shape[0]

    def shifted(v, lower, upper):
        north = [jnp.where(top, lo, pltpu.roll(x, 1, 0)) for x, lo in zip(v, lower)]
        south = [jnp.where(bottom, up, pltpu.roll(x, count - 1, 0)) for x, up in zip(v, upper)]
        return north, south

    zero = [0.0] * 3
    once = smooth(own, *shifted(own, zero, zero))
    below = [f * (0.2 * exists[0]) for f in first]
    above = [f * (0.2 * exists[1]) for f in last]
    return smooth(once, *shifted(once, below, above))


def spread_halo(rows, nearest):
    pair = lax.broadcasted_iota(jnp.int32, (rows[0].shape[0], 1), 0) % 2
    touching = [pltpu.roll(r, (r.shape[0] - 1) if nearest == 1 else 1, 0) for r in rows]
    t0, t1, t2 = touching
    spreads = (t0 + t1 + lane_roll(t2, 1), t0 + t1 + t2, t1 + t2 + lane_roll(t0, -1))
    return [0.04 * jnp.where(pair == 1 - nearest, 2.0 * s + r, r) for s, r in zip(spreads, rows)]


def neighbours(scalars_ref):
    device, bands = scalars_ref[2], scalars_ref[4]
    return (device > 0).astype(F32), (device < bands - 1).astype(F32)


def halo_rows(same_ref, cross_ref, scalars_ref, at, size):
    parity = scalars_ref[3]
    exists = neighbours(scalars_ref)
    same, cross = same_ref[at : at + size, :], cross_ref[at : at + size, :]
    return jnp.where(parity == 0, cross, same) * exists[0], jnp.where(parity == 0, same, cross) * exists[1]


def localize_kernel(alpha_ref, perturb_ref, loc_ref, out_ref, alpha_scr, perturb_scr, loc_scr, sems):
    members, levels, slots, count = alpha_ref.shape
    chunk = 512
    steps = count // chunk
    alpha_load = pltpu.make_async_copy(alpha_ref, alpha_scr, sems.at[0])
    perturb_load = pltpu.make_async_copy(perturb_ref, perturb_scr, sems.at[1])
    loads = []
    for c in range(steps):
        span = pl.ds(c * chunk, chunk)
        loads.append(pltpu.make_async_copy(loc_ref.at[:, span], loc_scr.at[:, span], sems.at[2 + c]))
    alpha_load.start()
    loads[0].start()
    loads[1].start()
    alpha_load.wait()
    perturb_load.start()
    alpha = alpha_scr[...].reshape(members * levels * slots, count)
    for c in range(steps):
        span = slice(c * chunk, (c + 1) * chunk)
        loads[c].wait()
        if c + 2 < steps:
            loads[c + 2].start()
        localized = jnp.dot(alpha, loc_scr[:, span], preferred_element_type=F32)
        if c == 0:
            perturb_load.wait()
        perturb = perturb_scr[:, :, :, span].astype(F32).reshape(members * levels * slots, chunk)
        out_ref[:, span] = jnp.sum((perturb * localized).reshape(members, levels * slots, chunk), axis=0)


def split_kernel(
    device_ref, coarse_ref, fine_ref, control_ref, innovation_ref, weight_ref,
    scalars_out, control_out, static_out, weight_out, same_out, cross_out, innovation_scr,
):
    bands = coarse_ref.shape[0]
    device = device_ref[0]
    parity = device % 2
    own_fine = fine_ref[device]
    scalars_out[0] = coarse_ref[device]
    scalars_out[1] = own_fine
    scalars_out[2] = device
    scalars_out[3] = parity
    scalars_out[4] = bands
    scalars_out[5] = 3 * (device - parity) + parity * coarse_ref[device - parity]
    levels, slots, count = control_ref.shape
    width = 128
    table = triple_table(width, False)
    rows = levels * slots
    live = (lax.broadcasted_iota(jnp.int32, (rows, 1), 0) % slots < own_fine).astype(F32)
    for block in range(count // (3 * width)):
        span = slice(3 * width * block, 3 * width * (block + 1))
        stacked = jnp.concatenate(
            [r[:, :, span].reshape(rows, 3 * width) for r in (control_ref, innovation_ref, weight_ref)], axis=0
        )
        planes = jnp.dot(stacked, table, preferred_element_type=F32)
        out = slice(width * block, width * (block + 1))
        for p in range(3):
            part = planes[:, p * width : (p + 1) * width]
            control_out[p, :, :, out] = (part[:rows] * live).reshape(levels, slots, width)
            innovation_scr[p, :, :, out] = part[rows : 2 * rows].reshape(levels, slots, width)
            weight_out[p, :, :, out] = (part[2 * rows :] * live).reshape(levels, slots, width).astype(BF16)
    same_start = jnp.where(parity == 0, own_fine - 2, 0)
    cross_start = jnp.where(parity == 0, 0, own_fine - 2)
    row_ids = lax.broadcasted_iota(jnp.int32, (slots, 1), 0)
    exists = (device > 0).astype(F32), (device < bands - 1).astype(F32)
    for l in range(levels):
        for p in range(3):
            at = (p * levels + l) * 2
            for k in range(2):
                same_out[at + k : at + k + 1, :] = control_out[p, l, pl.ds(same_start + k, 1), :]
                cross_out[at + k : at + k + 1, :] = control_out[p, l, pl.ds(cross_start + k, 1), :]
        own = [control_out[p, l] for p in range(3)]
        first = [control_out[p, l, 0:1, :] for p in range(3)]
        last = [control_out[p, l, pl.ds(own_fine - 1, 1), :] for p in range(3)]
        result = spread_own(own, first, last, own_fine, row_ids, exists)
        for p in range(3):
            static_out[p, l] = result[p] - innovation_scr[p, l]


def increment_kernel(scalars_ref, own_ref, a_ref, b_ref, c_ref, same_in, cross_in, total_ref, same_out, cross_out):
    own_coarse, parity = scalars_ref[0], scalars_ref[3]
    total_ref[...] = (own_ref[...] + a_ref[...]) + (b_ref[...] + c_ref[...])
    levels = total_ref.shape[0] // 4
    at = same_out.shape[0] - 2 * levels
    same_start = jnp.where(parity == 0, own_coarse - 2, 0)
    cross_start = jnp.where(parity == 0, 0, own_coarse - 2)
    for l in range(levels):
        for k in range(2):
            row = at + 2 * l + k
            same_out[row : row + 1, :] = total_ref[pl.ds(4 * l + same_start + k, 1), :]
            cross_out[row : row + 1, :] = total_ref[pl.ds(4 * l + cross_start + k, 1), :]


def residual_kernel(
    scalars_ref, source_ref, upper_ref, total_ref, same_ref, cross_ref, static_ref, weight_ref,
    residual_out, back_out, same_out, cross_out, lower_scr, higher_scr,
):
    own_coarse, own_fine, device, parity, bands, first_row = (scalars_ref[i] for i in range(6))
    planes, levels, slots, count = static_ref.shape
    size = 2 * levels
    row_ids = lax.broadcasted_iota(jnp.int32, (slots, 1), 0)
    picked = lax.broadcasted_iota(jnp.int32, (slots, slots), 0) == lax.broadcasted_iota(jnp.int32, (slots, slots), 1)
    source = jnp.sum(jnp.where(picked, source_ref[...], 0), axis=1, keepdims=True)
    upper = jnp.sum(jnp.where(picked, upper_ref[...], 0.0), axis=1, keepdims=True)
    live = (row_ids < own_fine).astype(F32)
    low_weight, high_weight = live * (1.0 - upper), live * upper
    latitudes = [first_row - 2, first_row - 1] + [first_row + s for s in range(4)]
    latitudes += [first_row + own_coarse, first_row + own_coarse + 1]
    usable = [device > 0] * 2 + [s < own_coarse for s in range(4)] + [device < bands - 1] * 2
    coefficients = [
        (jnp.where(source == lat, low_weight, 0.0) + jnp.where(source + 1 == lat, high_weight, 0.0)) * ok.astype(F32)
        for lat, ok in zip(latitudes, usable)
    ]
    halos = [halo_rows(same_ref, cross_ref, scalars_ref, p * size, size) for p in range(3)]
    static_below = spread_halo([h[0] for h in halos], 1)
    static_above = spread_halo([h[1] for h in halos], 0)
    edges = [row_ids == 0, row_ids == 1, row_ids == own_fine - 2, row_ids == own_fine - 1]
    row_below, row_above = halo_rows(same_ref, cross_ref, scalars_ref, 3 * size, size)
    for l in range(levels):
        at = 2 * l
        rows = [row_below[at : at + 1], row_below[at + 1 : at + 2]]
        rows += [total_ref[4 * l + s : 4 * l + s + 1, :] for s in range(4)]
        rows += [row_above[at : at + 1], row_above[at + 1 : at + 2]]
        band = coefficients[0] * rows[0]
        for c, r in zip(coefficients[1:], rows[1:]):
            band = band + c * r
        following = lane_roll(band, -1)
        fine = (band, (2.0 * band + following) * THIRD, (band + 2.0 * following) * THIRD)
        residual = []
        for p in range(3):
            lower, higher = static_below[p], static_above[p]
            low = jnp.where(edges[0], lower[at : at + 1], jnp.where(edges[1], lower[at + 1 : at + 2], 0.0))
            high = jnp.where(edges[2], higher[at : at + 1], jnp.where(edges[3], higher[at + 1 : at + 2], 0.0))
            value = weight_ref[p, l].astype(F32) * (fine[p] + (static_ref[p, l] + (low + high)))
            value = jnp.where(row_ids < own_fine, value, 0.0)
            residual_out[p, l] = value
            residual.append(value)
        g0, g1, g2 = residual
        back = (g0 + g1 * (2.0 * THIRD) + g2 * THIRD) + lane_roll(g1 * THIRD + g2 * (2.0 * THIRD), 1)
        sums = [jnp.sum(c * back, axis=0, keepdims=True) for c in coefficients]
        for s in range(4):
            back_out[4 * l + s : 4 * l + s + 1, :] = sums[2 + s]
        for k in range(2):
            lower_scr[at + k : at + k + 1, :] = sums[k]
            higher_scr[at + k : at + k + 1, :] = sums[6 + k]
    same_start = jnp.where(parity == 0, own_fine - 2, 0)
    cross_start = jnp.where(parity == 0, 0, own_fine - 2)
    for p in range(3):
        for l in range(levels):
            at = (p * levels + l) * 2
            for k in range(2):
                same_out[at + k : at + k + 1, :] = residual_out[p, l, pl.ds(same_start + k, 1), :]
                cross_out[at + k : at + k + 1, :] = residual_out[p, l, pl.ds(cross_start + k, 1), :]
    lower, higher = lower_scr[...], higher_scr[...]
    same_out[3 * size : 4 * size, :] = jnp.where(parity == 0, higher, lower)
    cross_out[3 * size : 4 * size, :] = jnp.where(parity == 0, lower, higher)


def join_planes(planes):
    width = 128
    rows, count = planes[0].shape
    blocks = count // width
    spans = [slice(width * block, width * (block + 1)) for block in range(blocks)]
    joined = jnp.concatenate([jnp.concatenate([p[:, span] for p in planes], axis=1) for span in spans], axis=0)
    high = joined.astype(BF16)
    low = (joined - high.astype(F32)).astype(BF16)
    both = jnp.dot(jnp.concatenate([high, low], axis=0), triple_table(width, True), preferred_element_type=F32)
    mixed = both[: blocks * rows] + both[blocks * rows :]
    return [mixed[block * rows : (block + 1) * rows] for block in range(blocks)]


def own_gradient_kernel(scalars_ref, control_ref, residual_ref, out_ref, grad_scr):
    own_fine = scalars_ref[1]
    planes, levels, slots, count = control_ref.shape
    row_ids = lax.broadcasted_iota(jnp.int32, (slots, 1), 0)
    exists = neighbours(scalars_ref)
    for l in range(levels):
        own = [residual_ref[p, l] for p in range(3)]
        first = [residual_ref[p, l, 0:1, :] for p in range(3)]
        last = [residual_ref[p, l, pl.ds(own_fine - 1, 1), :] for p in range(3)]
        result = spread_own(own, first, last, own_fine, row_ids, exists)
        for p in range(3):
            grad_scr[p, l] = jnp.where(row_ids < own_fine, control_ref[p, l] + result[p], 0.0)
    mixed = join_planes([grad_scr[p].reshape(levels * slots, count) for p in range(3)])
    for block, part in enumerate(mixed):
        out_ref[:, :, 384 * block : 384 * (block + 1)] = part.reshape(levels, slots, 384)


def gradient_kernel(
    scalars_ref, back_ref, same_ref, cross_ref, own_static_ref, alpha_ref, perturb_ref, loc_ref,
    alpha_out, static_out, full_scr, schur_scr, stage_scr, halo_scr, static_scr, sems,
):
    own_coarse, own_fine = scalars_ref[0], scalars_ref[1]
    members, levels, slots, count = perturb_ref.shape
    size = 2 * levels
    below, above = halo_rows(same_ref, cross_ref, scalars_ref, 3 * size, size)
    full_scr[...] = back_ref[...]
    for l in range(levels):
        full_scr[4 * l : 4 * l + 2, :] += below[2 * l : 2 * l + 2]
        for k in range(2):
            full_scr[pl.ds(4 * l + own_coarse - 2 + k, 1), :] += above[2 * l + k : 2 * l + k + 1]
    rows = members * levels * slots
    chunk = 256
    for c in range(count // chunk):
        span = slice(c * chunk, (c + 1) * chunk)
        perturb = perturb_ref[:, :, :, span].astype(F32).reshape(members, levels * slots, chunk)
        schur_scr[:, span] = (perturb * full_scr[:, span][None]).astype(BF16).reshape(rows, chunk)

    halos = [halo_rows(same_ref, cross_ref, scalars_ref, p * size, size) for p in range(3)]
    lower = spread_halo([h[0] for h in halos], 1)
    higher = spread_halo([h[1] for h in halos], 0)
    mixed = join_planes([jnp.concatenate([lower[p], higher[p]], axis=0) for p in range(3)])
    for block, part in enumerate(mixed):
        halo_scr[:, 384 * block : 384 * (block + 1)] = part
    static_scr[...] = own_static_ref[...]
    for l in range(levels):
        static_scr[l, 0:2, :] += halo_scr[2 * l : 2 * l + 2, :]
        for k in range(2):
            at = size + 2 * l + k
            static_scr[l, pl.ds(own_fine - 2 + k, 1), :] += halo_scr[at : at + 1, :]
    copies = [pltpu.make_async_copy(static_scr, static_out, sems.at[0])]
    copies[0].start()

    schur = schur_scr[...]
    live = (lax.broadcasted_iota(jnp.int32, (rows, 1), 0) % slots < own_coarse).astype(F32)
    for c in range(count // chunk):
        span = slice(c * chunk, (c + 1) * chunk)
        pulled = lax.dot_general(schur, loc_ref[span, :], (((1,), (1,)), ((), ())), preferred_element_type=F32)
        alpha = alpha_ref[:, :, :, span].astype(F32).reshape(rows, chunk)
        stage_scr[:, :, :, span] = ((alpha + pulled) * live).reshape(members, levels, slots, chunk).astype(BF16)
        copies.append(
            pltpu.make_async_copy(
                stage_scr.at[:, :, :, pl.ds(c * chunk, chunk)], alpha_out.at[:, :, :, pl.ds(c * chunk, chunk)], sems.at[1 + c]
            )
        )
        copies[-1].start()
    for copy in copies:
        copy.wait()


def on_device(
    perturb, alpha_control, loc_factor, static_control, innovation, obs_weight, coarse_rows, fine_rows, source_row, row_weight
):
    device = lax.axis_index("band").astype(jnp.int32).reshape(1)
    members, levels, slots, count = perturb.shape
    fine_slots = static_control.shape[1]
    rows = levels * slots
    steps = count // 256

    partial = pl.pallas_call(
        localize_kernel,
        out_shape=jax.ShapeDtypeStruct((rows, count), F32),
        in_specs=[HBM] * 3,
        out_specs=VMEM,
        scratch_shapes=[
            pltpu.VMEM(alpha_control.shape, BF16),
            pltpu.VMEM(perturb.shape, BF16),
            pltpu.VMEM(loc_factor.shape, BF16),
            pltpu.SemaphoreType.DMA((2 + count // 512,)),
        ],
        compiler_params=params(61),
    )(alpha_control, perturb, loc_factor)
    peers = [mem_peer(partial, by) for by in (1, 3, 2)]

    plane = (3, levels, fine_slots, count)
    outgoing = jax.ShapeDtypeStruct((8 * levels, count), F32)
    scalars, control, static_minus, weight_planes, same_send, cross_send = pl.pallas_call(
        split_kernel,
        out_shape=(
            jax.ShapeDtypeStruct((8,), jnp.int32),
            jax.ShapeDtypeStruct(plane, F32),
            jax.ShapeDtypeStruct(plane, F32),
            jax.ShapeDtypeStruct(plane, BF16),
            outgoing,
            outgoing,
        ),
        in_specs=[SMEM] * 3 + [VMEM] * 3,
        out_specs=(SMEM,) + (VMEM,) * 5,
        scratch_shapes=[pltpu.VMEM(plane, F32)],
        compiler_params=params(24),
    )(device, coarse_rows, fine_rows, static_control, innovation, obs_weight)

    total, same_send, cross_send = pl.pallas_call(
        increment_kernel,
        out_shape=(jax.ShapeDtypeStruct((rows, count), F32), outgoing, outgoing),
        in_specs=[SMEM] + [VMEM] * 6,
        out_specs=(VMEM,) * 3,
        input_output_aliases={5: 1, 6: 2},
        compiler_params=params(24),
    )(scalars, partial, *peers, same_send, cross_send)
    from_cross = cross_chip(cross_send)
    from_same = same_chip(same_send)

    residual, back, same_send, cross_send = pl.pallas_call(
        residual_kernel,
        out_shape=(jax.ShapeDtypeStruct(plane, F32), jax.ShapeDtypeStruct((rows, count), F32), outgoing, outgoing),
        in_specs=[SMEM] + [VMEM] * 7,
        out_specs=(VMEM,) * 4,
        scratch_shapes=[pltpu.VMEM((2 * levels, count), F32), pltpu.VMEM((2 * levels, count), F32)],
        compiler_params=params(24),
    )(
        scalars, source_row.reshape(1, fine_slots), row_weight.reshape(1, fine_slots), total, from_same, from_cross,
        static_minus, weight_planes,
    )
    from_cross = cross_chip(cross_send)
    from_same = same_chip(same_send)

    own_static = pl.pallas_call(
        own_gradient_kernel,
        out_shape=jax.ShapeDtypeStruct(static_control.shape, F32),
        in_specs=[SMEM] + [VMEM] * 2,
        out_specs=VMEM,
        scratch_shapes=[pltpu.VMEM(plane, F32)],
        compiler_params=params(24),
    )(scalars, control, residual)

    return pl.pallas_call(
        gradient_kernel,
        out_shape=(jax.ShapeDtypeStruct(perturb.shape, BF16), jax.ShapeDtypeStruct(static_control.shape, F32)),
        in_specs=[SMEM] + [VMEM] * 7,
        out_specs=(HBM, HBM),
        scratch_shapes=[
            pltpu.VMEM((rows, count), F32),
            pltpu.VMEM((members * rows, count), BF16),
            pltpu.VMEM(perturb.shape, BF16),
            pltpu.VMEM((rows, 3 * count), F32),
            pltpu.VMEM(static_control.shape, F32),
            pltpu.SemaphoreType.DMA((1 + steps,)),
        ],
        compiler_params=params(24),
    )(scalars, back, from_same, from_cross, own_static, alpha_control, perturb, loc_factor)


def solution(mesh):
    placed = (
        P("mem", None, "band", None),
        P("mem", None, "band", None),
        P(),
        P(None, "band", None),
        P(None, "band", None),
        P(None, "band", None),
        P(),
        P(),
        P("band"),
        P("band"),
    )
    return jax.shard_map(
        on_device,
        mesh=mesh,
        in_specs=placed,
        out_specs=(P("mem", None, "band", None), P(None, "band", None)),
        check_vma=False,
    )
```

time: 54.3 us -> 40.7 us (0.75)
  the two profiles are of different devices: /device:TPU:8 before, /device:TPU:6 now
where the time goes in v2:
time: 40.7 us; the launch traced here: 40.6 us
  Pallas kernels  17.7 us (43%)
  starting transfers between devices  15.8 us (39%)
  waiting for transfers between devices  6.1 us (15%)
  between operations  0.97 us (2%)
    ppermute x2, starting transfers between devices, cross_chip(): return lax.ppermute(x, ('band', 'mem'), pairs)  10.3 us
    pallas_call x1, Pallas kernels, on_device(): pl.pallas_call(localize_kernel, out_shape=jax.ShapeDtypeStruct((rows, cou...  5.51 us
    ppermute x3, starting transfers between devices, mem_peer(): return lax.ppermute(x, 'mem', [(i, (i + by) % peers) for i in range(peers)])  5.31 us
    ppermute x2, waiting for transfers between devices, cross_chip(): return lax.ppermute(x, ('band', 'mem'), pairs)  4.24 us
    pallas_call x1, Pallas kernels, on_device(): pl.pallas_call(gradient_kernel, out_shape=(jax.ShapeDtypeStruct(perturb.s...  3.71 us
    pallas_call x1, Pallas kernels, on_device(): pl.pallas_call(split_kernel, out_shape=(jax.ShapeDtypeStruct((8,), jnp.in...  3.16 us
    pallas_call x1, Pallas kernels, on_device(): pl.pallas_call(own_gradient_kernel, out_shape=jax.ShapeDtypeStruct(static...  2.45 us
    pallas_call x1, Pallas kernels, on_device(): pl.pallas_call(residual_kernel, out_shape=(jax.ShapeDtypeStruct(plane, F3...  2.25 us
  transfers between devices with their start and end apart: 7, of which 4 were waited for; matrix products, arithmetic and copies ran while one was open for 0% of the time, Pallas kernels for 14%

profile of v2, /device:TPU:6, one launch (start us, length us, event | category | flops | bytes accessed | tf_op | source)
XLA Modules:
  0.0 40.6 jit_solution(9136591565502048207)
XLA Ops:
  0.7 0.0 slice-start
  0.7 5.5 %shard_map.114.own_ref = f32[16,1536]{1,0:T(8,128)} custom-call(bf16[20,4,4,1536]{3,2,1,0:T(4,128)(2,1)} %alpha_ref.3, bf16[20,4,4,1536]{3,2,1,0:T(4,128)(2,1)} %perturb_ref.3, bf16[1536,1536]{1,0:T(8,128)(2,1)} %loc_ref.3), custom_call_target="tpu_custom_call" | custom-call | tf_op jit(solution)/shard_map/pallas_call | solution.py:349
  6.2 0.0 copy-start.5
  6.2 3.3 %collective-permute-start.2 = (f32[16,1536]{1,0:T(8,128)}, f32[16,1536]{1,0:T(8,128)S(1)}, u32[]{:S(2)}, u32[]{:S(2)}) collective-permute-start(f32[16,1536]{1,0:T(8,128)} %shard_map.114.own_ref), channel_id=1, source_target_pairs={{0,2},{1,3},{2,0},{3,1},{4,6},{5,7},{6,4},{7,5},{8,10},{9,11},{10,... | collective-permute-start | bytes 294920 | tf_op jit(solution)/shard_map/ppermute | solution.py:37
  9.5 1.1 %collective-permute-start.1 = (f32[16,1536]{1,0:T(8,128)}, f32[16,1536]{1,0:T(8,128)S(1)}, u32[]{:S(2)}, u32[]{:S(2)}) collective-permute-start(f32[16,1536]{1,0:T(8,128)} %shard_map.114.own_ref), channel_id=1, source_target_pairs={{0,3},{1,0},{2,1},{3,2},{4,7},{5,4},{6,5},{7,6},{8,11},{9,8},{10,9... | collective-permute-start | bytes 294920 | tf_op jit(solution)/shard_map/ppermute | solution.py:37
  10.6 1.0 %collective-permute-start = (f32[16,1536]{1,0:T(8,128)}, f32[16,1536]{1,0:T(8,128)S(1)}, u32[]{:S(2)}, u32[]{:S(2)}) collective-permute-start(f32[16,1536]{1,0:T(8,128)} %shard_map.114.own_ref), channel_id=1, source_target_pairs={{0,1},{1,2},{2,3},{3,0},{4,5},{5,6},{6,7},{7,4},{8,9},{9,10},{10,1... | collective-permute-start | bytes 294920 | tf_op jit(solution)/shard_map/ppermute | solution.py:37
  11.6 0.0 copy-done.6
  11.6 0.0 slice-start.1
  11.6 3.2 %shard_map.113 = (s32[8]{0:T(128)S(1)}, f32[3,4,16,1536]{3,2,1,0:T(8,128)S(1)}, f32[3,4,16,1536]{3,2,1,0:T(8,128)S(1)}, bf16[3,4,16,1536]{3,2,1,0:T(8,128)(2,1)S...) custom-call(s32[1]{0:T(128)} %bitcast.device_ref, s32[64]{0:T(128)S(1)} %copy-done.6, s32[64]{0:T(128)S(1)} %copy-done.7, ...), custom_call_target="tpu_custom_call" | custom-call | tf_op jit(solution)/shard_map/pallas_call | solution.py:366
  14.8 0.0 collective-permute-done.2.c_ref
  14.8 0.3 collective-permute-done.1.b_ref
  15.1 1.6 %collective-permute-done.a_ref = f32[16,1536]{1,0:T(8,128)S(1)} collective-permute-done((f32[16,1536]{1,0:T(8,128)}, f32[16,1536]{1,0:T(8,128)S(1)}, u32[]{:S(2)}, u32[]{:S(2)}) %collective-permute-start) | collective-permute-done | bytes 98336 | tf_op jit(solution)/shard_map/ppermute | solution.py:37
  16.6 0.6 %shard_map.115 = (f32[16,1536]{1,0:T(8,128)S(1)}, f32[32,1536]{1,0:T(8,128)S(1)}, f32[32,1536]{1,0:T(8,128)S(1)}) custom-call(s32[8]{0:T(128)S(1)} %get-tuple-element.15.scalars_ref, f32[16,1536]{1,0:T(8,128)S(1)} %copy-done.5, f32[16,1536]{1,0:T(8,128)S(1)} %collective-permute-done.a_ref, ...), custom_call_target="tpu_custom_call", output_to_operand_aliasing={{1}: (5, {}), {2}: (6, {})} | custom-call | tf_op jit(solution)/shard_map/pallas_call | solution.py:382
  17.2 0.1 collective-permute-start.3
  17.3 6.2 %collective-permute-start.4 = (f32[32,1536]{1,0:T(8,128)S(1)}, f32[32,1536]{1,0:T(8,128)S(1)}, u32[]{:S(2)}, u32[]{:S(2)}) collective-permute-start(f32[32,1536]{1,0:T(8,128)S(1)} %get-tuple-element.20), channel_id=1, source_target_pairs={{4,8},{12,16},{20,24},{28,32},{36,40},{44,48},{52,56},{60,64},{68,... | collective-permute-start | bytes 589832 | tf_op jit(solution)/shard_map/ppermute | solution.py:32
  23.6 0.0 collective-permute-done.3.same_ref
  23.6 3.3 %collective-permute-done.4.cross_ref = f32[32,1536]{1,0:T(8,128)S(1)} collective-permute-done((f32[32,1536]{1,0:T(8,128)S(1)}, f32[32,1536]{1,0:T(8,128)S(1)}, u32[]{:S(2)}, u32[]{:S(2)}) %collective-permute-start.4) | collective-permute-done | bytes 196640 | tf_op jit(solution)/shard_map/ppermute | solution.py:32
  26.9 2.2 %shard_map.116 = (f32[3,4,16,1536]{3,2,1,0:T(8,128)S(1)}, f32[16,1536]{1,0:T(8,128)S(1)}, f32[32,1536]{1,0:T(8,128)S(1)}, f32[32,1536]{1,0:T(8,128)S(1)}) custom-call(s32[8]{0:T(128)S(1)} %get-tuple-element.15.scalars_ref, s32[1,16]{1,0:T(1,128)S(1)} %bitcast.5, f32[1,16]{1,0:T(1,128)S(1)} %bitcast.6, f32[16,1536]{1,0:T(8,128)S(1)} %get-tuple-element.18.total_ref, ...), custom_call_target="tpu_custom_call" | custom-call | tf_op jit(solution)/shard_map/pallas_call | solution.py:393
  29.2 0.1 collective-permute-start.5
  29.3 4.1 %collective-permute-start.6 = (f32[32,1536]{1,0:T(8,128)S(1)}, f32[32,1536]{1,0:T(8,128)S(1)}, u32[]{:S(2)}, u32[]{:S(2)}) collective-permute-start(f32[32,1536]{1,0:T(8,128)S(1)} %get-tuple-element.25), channel_id=1, source_target_pairs={{4,8},{12,16},{20,24},{28,32},{36,40},{44,48},{52,56},{60,64},{68,... | collective-permute-start | bytes 589832 | tf_op jit(solution)/shard_map/ppermute | solution.py:32
  33.4 2.4 %shard_map.117.own_static_ref = f32[4,16,4608]{2,1,0:T(8,128)S(1)} custom-call(s32[8]{0:T(128)S(1)} %get-tuple-element.15.scalars_ref, f32[3,4,16,1536]{3,2,1,0:T(8,128)S(1)} %get-tuple-element.26.control_ref, f32[3,4,16,1536]{3,2,1,0:T(8,128)S(1)} %get-tuple-element.27.residual_ref), custom_call_target="tpu_custom_call" | custom-call | tf_op jit(solution)/shard_map/pallas_call | solution.py:407
  35.8 0.0 collective-permute-done.5.same_ref
  35.8 0.9 %collective-permute-done.6.cross_ref = f32[32,1536]{1,0:T(8,128)S(1)} collective-permute-done((f32[32,1536]{1,0:T(8,128)S(1)}, f32[32,1536]{1,0:T(8,128)S(1)}, u32[]{:S(2)}, u32[]{:S(2)}) %collective-permute-start.6) | collective-permute-done | bytes 196640 | tf_op jit(solution)/shard_map/ppermute | solution.py:32
  36.8 3.7 %shard_map.118 = (bf16[20,4,4,1536]{3,2,1,0:T(4,128)(2,1)}, f32[4,16,4608]{2,1,0:T(8,128)}) custom-call(s32[8]{0:T(128)S(1)} %get-tuple-element.15.scalars_ref, f32[16,1536]{1,0:T(8,128)S(1)} %get-tuple-element.23.back_ref, f32[32,1536]{1,0:T(8,128)S(1)} %collective-permute-done.5.same_ref, f32[32,1536]{1,0:T(8,128)S(1)} %collective-permute-done.6.cross_ref, ...), custom_call_target="tpu_custom_call" | custom-call | tf_op jit(solution)/shard_map/pallas_call | solution.py:416
  (21 shorter events, 0.0 us)
Async XLA Ops:
  0.6 10.9 %copy-start.7 = (s32[64]{0:T(128)S(1)}, s32[64]{0:T(128)}, u32[]{:S(2)}) copy-start(s32[64]{0:T(128)} %fine_ref.1) | copy-start | bytes 772
  0.6 10.9 %copy-start.6 = (s32[64]{0:T(128)S(1)}, s32[64]{0:T(128)}, u32[]{:S(2)}) copy-start(s32[64]{0:T(128)} %coarse_ref.1) | copy-start | bytes 772
  0.7 10.9 %copy-start.4 = (bf16[4,16,4608]{2,1,0:T(8,128)(2,1)S(1)}, bf16[4,16,4608]{2,1,0:T(8,128)(2,1)}, u32[]{:S(2)}) copy-start(bf16[4,16,4608]{2,1,0:T(8,128)(2,1)} %weight_ref.1) | copy-start | bytes 1769476
  0.7 10.9 %copy-start.3 = (bf16[4,16,4608]{2,1,0:T(8,128)(2,1)S(1)}, bf16[4,16,4608]{2,1,0:T(8,128)(2,1)}, u32[]{:S(2)}) copy-start(bf16[4,16,4608]{2,1,0:T(8,128)(2,1)} %innovation_ref.1) | copy-start | bytes 1769476
  0.7 10.9 %copy-start.2 = (bf16[4,16,4608]{2,1,0:T(8,128)(2,1)S(1)}, bf16[4,16,4608]{2,1,0:T(8,128)(2,1)}, u32[]{:S(2)}) copy-start(bf16[4,16,4608]{2,1,0:T(8,128)(2,1)} %control_ref.1) | copy-start | bytes 1769476
  0.7 26.2 %copy-start.8 = (s32[16]{0:T(128)S(1)}, s32[16]{0:T(128)}, u32[]{:S(2)}) copy-start(s32[16]{0:T(128)} %param.18) | copy-start | bytes 196
  0.7 26.2 %copy-start.9 = (f32[16]{0:T(128)S(1)}, f32[16]{0:T(128)}, u32[]{:S(2)}) copy-start(f32[16]{0:T(128)} %param.19) | copy-start | bytes 196
  0.7 36.0 %slice-start = ((s8[4718592]{0:T(1024)(128)(4,1)}), s8[524288]{0:T(1024)(128)(4,1)S(1)}, s32[]{:S(2)}) async-start(s8[4718592]{0:T(1024)(128)(4,1)} %bitcast.3), calls=%async_computation | async-start | bytes 1048576
  6.2 10.4 %copy-start.5 = (f32[16,1536]{1,0:T(8,128)S(1)}, f32[16,1536]{1,0:T(8,128)}, u32[]{:S(2)}) copy-start(f32[16,1536]{1,0:T(8,128)} %shard_map.114.own_ref) | copy-start | bytes 294916
  6.2 8.5 %collective-permute-start.2 = (f32[16,1536]{1,0:T(8,128)}, f32[16,1536]{1,0:T(8,128)S(1)}, u32[]{:S(2)}, u32[]{:S(2)}) collective-permute-start(f32[16,1536]{1,0:T(8,128)} %shard_map.114.own_ref), channel_id=1, source_target_pairs={{0,2},{1,3},{2,0},{3,1},{4,6},{5,7},{6,4},{7,5},{8,10},{9,11},{10,... | collective-permute-start | bytes 294920 | tf_op jit(solution)/shard_map/ppermute | solution.py:37
  9.5 5.5 %collective-permute-start.1 = (f32[16,1536]{1,0:T(8,128)}, f32[16,1536]{1,0:T(8,128)S(1)}, u32[]{:S(2)}, u32[]{:S(2)}) collective-permute-start(f32[16,1536]{1,0:T(8,128)} %shard_map.114.own_ref), channel_id=1, source_target_pairs={{0,3},{1,0},{2,1},{3,2},{4,7},{5,4},{6,5},{7,6},{8,11},{9,8},{10,9... | collective-permute-start | bytes 294920 | tf_op jit(solution)/shard_map/ppermute | solution.py:37
  10.6 6.0 %collective-permute-start = (f32[16,1536]{1,0:T(8,128)}, f32[16,1536]{1,0:T(8,128)S(1)}, u32[]{:S(2)}, u32[]{:S(2)}) collective-permute-start(f32[16,1536]{1,0:T(8,128)} %shard_map.114.own_ref), channel_id=1, source_target_pairs={{0,1},{1,2},{2,3},{3,0},{4,5},{5,6},{6,7},{7,4},{8,9},{9,10},{10,1... | collective-permute-start | bytes 294920 | tf_op jit(solution)/shard_map/ppermute | solution.py:37
  11.6 25.2 %slice-start.1 = ((s8[4718592]{0:T(1024)(128)(4,1)}), s8[4194304]{0:T(1024)(128)(4,1)S(1)}, s32[]{:S(2)}) async-start(s8[4718592]{0:T(1024)(128)(4,1)} %bitcast.3), calls=%async_computation.1 | async-start | bytes 8388608
  17.2 6.3 %collective-permute-start.3 = (f32[32,1536]{1,0:T(8,128)S(1)}, f32[32,1536]{1,0:T(8,128)S(1)}, u32[]{:S(2)}, u32[]{:S(2)}) collective-permute-start(f32[32,1536]{1,0:T(8,128)S(1)} %get-tuple-element.19), channel_id=1, source_target_pairs={{0,4},{4,0},{8,12},{12,8},{16,20},{20,16},{24,28},{28,24},{32,36},... | collective-permute-start | bytes 589832 | tf_op jit(solution)/shard_map/ppermute | solution.py:22
  17.3 9.6 %collective-permute-start.4 = (f32[32,1536]{1,0:T(8,128)S(1)}, f32[32,1536]{1,0:T(8,128)S(1)}, u32[]{:S(2)}, u32[]{:S(2)}) collective-permute-start(f32[32,1536]{1,0:T(8,128)S(1)} %get-tuple-element.20), channel_id=1, source_target_pairs={{4,8},{12,16},{20,24},{28,32},{36,40},{44,48},{52,56},{60,64},{68,... | collective-permute-start | bytes 589832 | tf_op jit(solution)/shard_map/ppermute | solution.py:32
  29.2 6.7 %collective-permute-start.5 = (f32[32,1536]{1,0:T(8,128)S(1)}, f32[32,1536]{1,0:T(8,128)S(1)}, u32[]{:S(2)}, u32[]{:S(2)}) collective-permute-start(f32[32,1536]{1,0:T(8,128)S(1)} %get-tuple-element.24), channel_id=1, source_target_pairs={{0,4},{4,0},{8,12},{12,8},{16,20},{20,16},{24,28},{28,24},{32,36},... | collective-permute-start | bytes 589832 | tf_op jit(solution)/shard_map/ppermute | solution.py:22
  29.3 7.5 %collective-permute-start.6 = (f32[32,1536]{1,0:T(8,128)S(1)}, f32[32,1536]{1,0:T(8,128)S(1)}, u32[]{:S(2)}, u32[]{:S(2)}) collective-permute-start(f32[32,1536]{1,0:T(8,128)S(1)} %get-tuple-element.25), channel_id=1, source_target_pairs={{4,8},{12,16},{20,24},{28,32},{36,40},{44,48},{52,56},{60,64},{68,... | collective-permute-start | bytes 589832 | tf_op jit(solution)/shard_map/ppermute | solution.py:32
  33.4 3.4 %copy-start = (bf16[20,4,4,1536]{3,2,1,0:T(4,128)(2,1)S(1)}, bf16[20,4,4,1536]{3,2,1,0:T(4,128)(2,1)}, u32[]{:S(2)}) copy-start(bf16[20,4,4,1536]{3,2,1,0:T(4,128)(2,1)} %alpha_ref.3) | copy-start | bytes 2949124
  33.4 3.4 %copy-start.1 = (bf16[20,4,4,1536]{3,2,1,0:T(4,128)(2,1)S(1)}, bf16[20,4,4,1536]{3,2,1,0:T(4,128)(2,1)}, u32[]{:S(2)}) copy-start(bf16[20,4,4,1536]{3,2,1,0:T(4,128)(2,1)} %perturb_ref.3) | copy-start | bytes 2949124

commit v3 on v2

--- a/solution.py
+++ b/solution.py
@@ -9,7 +9,6 @@
 BF16 = jnp.bfloat16
 THIRD = 1.0 / 3.0
 VMEM = pl.BlockSpec(memory_space=pltpu.VMEM)
-SMEM = pl.BlockSpec(memory_space=pltpu.SMEM)
 HBM = pl.BlockSpec(memory_space=pltpu.HBM)
 
 
@@ -88,12 +87,12 @@
 
 
 def neighbours(scalars_ref):
-    device, bands = scalars_ref[2], scalars_ref[4]
+    device, bands = scalars_ref[2, 0], scalars_ref[4, 0]
     return (device > 0).astype(F32), (device < bands - 1).astype(F32)
 
 
 def halo_rows(same_ref, cross_ref, scalars_ref, at, size):
-    parity = scalars_ref[3]
+    parity = scalars_ref[3, 0]
     exists = neighbours(scalars_ref)
     same, cross = same_ref[at : at + size, :], cross_ref[at : at + size, :]
     return jnp.where(parity == 0, cross, same) * exists[0], jnp.where(parity == 0, same, cross) * exists[1]
@@ -131,33 +130,36 @@
     device_ref, coarse_ref, fine_ref, control_ref, innovation_ref, weight_ref,
     scalars_out, control_out, static_out, weight_out, same_out, cross_out, innovation_scr,
 ):
-    bands = coarse_ref.shape[0]
-    device = device_ref[0]
+    bands = coarse_ref.shape[1]
+    device = device_ref[0, 0]
     parity = device % 2
-    own_fine = fine_ref[device]
-    scalars_out[0] = coarse_ref[device]
-    scalars_out[1] = own_fine
-    scalars_out[2] = device
-    scalars_out[3] = parity
-    scalars_out[4] = bands
-    scalars_out[5] = 3 * (device - parity) + parity * coarse_ref[device - parity]
+    band_ids = lax.broadcasted_iota(jnp.int32, (1, bands), 1)
+    own_coarse = jnp.sum(jnp.where(band_ids == device, coarse_ref[...], 0))
+    own_fine = jnp.sum(jnp.where(band_ids == device, fine_ref[...], 0))
+    first_row = 3 * (device - parity) + parity * (6 - own_coarse)
+    for i, value in enumerate((own_coarse, own_fine, device, parity, bands, first_row)):
+        scalars_out[i : i + 1, :] = jnp.full((1, scalars_out.shape[1]), value, jnp.int32)
     levels, slots, count = control_ref.shape
     width = 128
     table = triple_table(width, False)
     rows = levels * slots
     live = (lax.broadcasted_iota(jnp.int32, (rows, 1), 0) % slots < own_fine).astype(F32)
-    for block in range(count // (3 * width)):
-        span = slice(3 * width * block, 3 * width * (block + 1))
-        stacked = jnp.concatenate(
-            [r[:, :, span].reshape(rows, 3 * width) for r in (control_ref, innovation_ref, weight_ref)], axis=0
-        )
-        planes = jnp.dot(stacked, table, preferred_element_type=F32)
-        out = slice(width * block, width * (block + 1))
+    blocks = count // (3 * width)
+    stacked = [
+        r[:, :, 3 * width * i : 3 * width * (i + 1)].reshape(rows, 3 * width)
+        for r in (control_ref, innovation_ref, weight_ref)
+        for i in range(blocks)
+    ]
+    planes = jnp.dot(jnp.concatenate(stacked, axis=0), table, preferred_element_type=F32)
+    for i in range(blocks):
+        out = slice(width * i, width * (i + 1))
         for p in range(3):
-            part = planes[:, p * width : (p + 1) * width]
-            control_out[p, :, :, out] = (part[:rows] * live).reshape(levels, slots, width)
-            innovation_scr[p, :, :, out] = part[rows : 2 * rows].reshape(levels, slots, width)
-            weight_out[p, :, :, out] = (part[2 * rows :] * live).reshape(levels, slots, width).astype(BF16)
+            control, innovation, weight = (
+                planes[rows * (k * blocks + i) : rows * (k * blocks + i + 1), p * width : (p + 1) * width] for k in range(3)
+            )
+            control_out[p, :, :, out] = (control * live).reshape(levels, slots, width)
+            innovation_scr[p, :, :, out] = innovation.reshape(levels, slots, width)
+            weight_out[p, :, :, out] = (weight * live).reshape(levels, slots, width).astype(BF16)
     same_start = jnp.where(parity == 0, own_fine - 2, 0)
     cross_start = jnp.where(parity == 0, 0, own_fine - 2)
     row_ids = lax.broadcasted_iota(jnp.int32, (slots, 1), 0)
@@ -176,25 +178,43 @@
             static_out[p, l] = result[p] - innovation_scr[p, l]
 
 
-def increment_kernel(scalars_ref, own_ref, a_ref, b_ref, c_ref, same_in, cross_in, total_ref, same_out, cross_out):
-    own_coarse, parity = scalars_ref[0], scalars_ref[3]
+def static_edge_kernel(scalars_ref, cross_ref, same_ref, static_in, static_out):
+    own_fine = scalars_ref[1, 0]
+    planes, levels, slots, count = static_out.shape
+    size = 2 * levels
+    halos = [halo_rows(same_ref, cross_ref, scalars_ref, p * size, size) for p in range(3)]
+    lower = spread_halo([h[0] for h in halos], 1)
+    higher = spread_halo([h[1] for h in halos], 0)
+    for p in range(3):
+        for l in range(levels):
+            static_out[p, l, 0:2, :] += lower[p][2 * l : 2 * l + 2]
+            for k in range(2):
+                static_out[p, l, pl.ds(own_fine - 2 + k, 1), :] += higher[p][2 * l + k : 2 * l + k + 1]
+
+
+def increment_kernel(scalars_ref, own_ref, a_ref, b_ref, c_ref, total_ref, same_out, cross_out):
+    own_coarse, parity = scalars_ref[0, 0], scalars_ref[3, 0]
     total_ref[...] = (own_ref[...] + a_ref[...]) + (b_ref[...] + c_ref[...])
     levels = total_ref.shape[0] // 4
-    at = same_out.shape[0] - 2 * levels
     same_start = jnp.where(parity == 0, own_coarse - 2, 0)
     cross_start = jnp.where(parity == 0, 0, own_coarse - 2)
     for l in range(levels):
         for k in range(2):
-            row = at + 2 * l + k
+            row = 2 * l + k
             same_out[row : row + 1, :] = total_ref[pl.ds(4 * l + same_start + k, 1), :]
             cross_out[row : row + 1, :] = total_ref[pl.ds(4 * l + cross_start + k, 1), :]
 
 
+def halves(x):
+    high = x.astype(BF16)
+    return high, (x - high.astype(F32)).astype(BF16)
+
+
 def residual_kernel(
-    scalars_ref, source_ref, upper_ref, total_ref, same_ref, cross_ref, static_ref, weight_ref,
+    scalars_ref, source_ref, upper_ref, total_ref, cross_ref, same_ref, static_ref, weight_ref,
     residual_out, back_out, same_out, cross_out, lower_scr, higher_scr,
 ):
-    own_coarse, own_fine, device, parity, bands, first_row = (scalars_ref[i] for i in range(6))
+    own_coarse, own_fine, device, parity, bands, first_row = (scalars_ref[i, 0] for i in range(6))
     planes, levels, slots, count = static_ref.shape
     size = 2 * levels
     row_ids = lax.broadcasted_iota(jnp.int32, (slots, 1), 0)
@@ -210,11 +230,9 @@
         (jnp.where(source == lat, low_weight, 0.0) + jnp.where(source + 1 == lat, high_weight, 0.0)) * ok.astype(F32)
         for lat, ok in zip(latitudes, usable)
     ]
-    halos = [halo_rows(same_ref, cross_ref, scalars_ref, p * size, size) for p in range(3)]
-    static_below = spread_halo([h[0] for h in halos], 1)
-    static_above = spread_halo([h[1] for h in halos], 0)
-    edges = [row_ids == 0, row_ids == 1, row_ids == own_fine - 2, row_ids == own_fine - 1]
-    row_below, row_above = halo_rows(same_ref, cross_ref, scalars_ref, 3 * size, size)
+    high_part, low_part = halves(jnp.concatenate(coefficients, axis=1))
+    gather = jnp.concatenate([high_part, high_part, low_part], axis=0)
+    row_below, row_above = halo_rows(same_ref, cross_ref, scalars_ref, 0, size)
     for l in range(levels):
         at = 2 * l
         rows = [row_below[at : at + 1], row_below[at + 1 : at + 2]]
@@ -227,21 +245,18 @@
         fine = (band, (2.0 * band + following) * THIRD, (band + 2.0 * following) * THIRD)
         residual = []
         for p in range(3):
-            lower, higher = static_below[p], static_above[p]
-            low = jnp.where(edges[0], lower[at : at + 1], jnp.where(edges[1], lower[at + 1 : at + 2], 0.0))
-            high = jnp.where(edges[2], higher[at : at + 1], jnp.where(edges[3], higher[at + 1 : at + 2], 0.0))
-            value = weight_ref[p, l].astype(F32) * (fine[p] + (static_ref[p, l] + (low + high)))
+            value = weight_ref[p, l].astype(F32) * (fine[p] + static_ref[p, l])
             value = jnp.where(row_ids < own_fine, value, 0.0)
             residual_out[p, l] = value
             residual.append(value)
         g0, g1, g2 = residual
         back = (g0 + g1 * (2.0 * THIRD) + g2 * THIRD) + lane_roll(g1 * THIRD + g2 * (2.0 * THIRD), 1)
-        sums = [jnp.sum(c * back, axis=0, keepdims=True) for c in coefficients]
-        for s in range(4):
-            back_out[4 * l + s : 4 * l + s + 1, :] = sums[2 + s]
-        for k in range(2):
-            lower_scr[at + k : at + k + 1, :] = sums[k]
-            higher_scr[at + k : at + k + 1, :] = sums[6 + k]
+        back_high, back_low = halves(back)
+        stacked = jnp.concatenate([back_high, back_low, back_high], axis=0)
+        sums = lax.dot_general(gather, stacked, (((0,), (0,)), ((), ())), preferred_element_type=F32)
+        back_out[4 * l : 4 * l + 4, :] = sums[2:6]
+        lower_scr[at : at + 2, :] = sums[0:2]
+        higher_scr[at : at + 2, :] = sums[6:8]
     same_start = jnp.where(parity == 0, own_fine - 2, 0)
     cross_start = jnp.where(parity == 0, 0, own_fine - 2)
     for p in range(3):
@@ -261,15 +276,14 @@
     blocks = count // width
     spans = [slice(width * block, width * (block + 1)) for block in range(blocks)]
     joined = jnp.concatenate([jnp.concatenate([p[:, span] for p in planes], axis=1) for span in spans], axis=0)
-    high = joined.astype(BF16)
-    low = (joined - high.astype(F32)).astype(BF16)
+    high, low = halves(joined)
     both = jnp.dot(jnp.concatenate([high, low], axis=0), triple_table(width, True), preferred_element_type=F32)
     mixed = both[: blocks * rows] + both[blocks * rows :]
     return [mixed[block * rows : (block + 1) * rows] for block in range(blocks)]
 
 
 def own_gradient_kernel(scalars_ref, control_ref, residual_ref, out_ref, grad_scr):
-    own_fine = scalars_ref[1]
+    own_fine = scalars_ref[1, 0]
     planes, levels, slots, count = control_ref.shape
     row_ids = lax.broadcasted_iota(jnp.int32, (slots, 1), 0)
     exists = neighbours(scalars_ref)
@@ -286,10 +300,10 @@
 
 
 def gradient_kernel(
-    scalars_ref, back_ref, same_ref, cross_ref, own_static_ref, alpha_ref, perturb_ref, loc_ref,
+    scalars_ref, back_ref, cross_ref, same_ref, own_static_ref, alpha_ref, perturb_ref, loc_ref,
     alpha_out, static_out, full_scr, schur_scr, stage_scr, halo_scr, static_scr, sems,
 ):
-    own_coarse, own_fine = scalars_ref[0], scalars_ref[1]
+    own_coarse, own_fine = scalars_ref[0, 0], scalars_ref[1, 0]
     members, levels, slots, count = perturb_ref.shape
     size = 2 * levels
     below, above = halo_rows(same_ref, cross_ref, scalars_ref, 3 * size, size)
@@ -340,7 +354,7 @@
 def on_device(
     perturb, alpha_control, loc_factor, static_control, innovation, obs_weight, coarse_rows, fine_rows, source_row, row_weight
 ):
-    device = lax.axis_index("band").astype(jnp.int32).reshape(1)
+    device = lax.axis_index("band").astype(jnp.int32).reshape(1, 1)
     members, levels, slots, count = perturb.shape
     fine_slots = static_control.shape[1]
     rows = levels * slots
@@ -363,42 +377,54 @@
 
     plane = (3, levels, fine_slots, count)
     outgoing = jax.ShapeDtypeStruct((8 * levels, count), F32)
+    wide = jax.ShapeDtypeStruct((6 * levels, count), F32)
     scalars, control, static_minus, weight_planes, same_send, cross_send = pl.pallas_call(
         split_kernel,
         out_shape=(
-            jax.ShapeDtypeStruct((8,), jnp.int32),
+            jax.ShapeDtypeStruct((8, 128), jnp.int32),
             jax.ShapeDtypeStruct(plane, F32),
             jax.ShapeDtypeStruct(plane, F32),
             jax.ShapeDtypeStruct(plane, BF16),
-            outgoing,
-            outgoing,
+            wide,
+            wide,
         ),
-        in_specs=[SMEM] * 3 + [VMEM] * 3,
-        out_specs=(SMEM,) + (VMEM,) * 5,
+        in_specs=[VMEM] * 6,
+        out_specs=(VMEM,) * 6,
         scratch_shapes=[pltpu.VMEM(plane, F32)],
         compiler_params=params(24),
-    )(device, coarse_rows, fine_rows, static_control, innovation, obs_weight)
-
+    )(device, coarse_rows.reshape(1, -1), fine_rows.reshape(1, -1), static_control, innovation, obs_weight)
+
+    static_from_cross = cross_chip(cross_send)
+    static_from_same = same_chip(same_send)
+
+    pair = jax.ShapeDtypeStruct((2 * levels, count), F32)
     total, same_send, cross_send = pl.pallas_call(
         increment_kernel,
-        out_shape=(jax.ShapeDtypeStruct((rows, count), F32), outgoing, outgoing),
-        in_specs=[SMEM] + [VMEM] * 6,
+        out_shape=(jax.ShapeDtypeStruct((rows, count), F32), pair, pair),
+        in_specs=[VMEM] * 5,
         out_specs=(VMEM,) * 3,
-        input_output_aliases={5: 1, 6: 2},
-        compiler_params=params(24),
-    )(scalars, partial, *peers, same_send, cross_send)
+        compiler_params=params(24),
+    )(scalars, partial, *peers)
     from_cross = cross_chip(cross_send)
     from_same = same_chip(same_send)
+    static_minus = pl.pallas_call(
+        static_edge_kernel,
+        out_shape=jax.ShapeDtypeStruct(plane, F32),
+        in_specs=[VMEM] * 4,
+        out_specs=VMEM,
+        input_output_aliases={3: 0},
+        compiler_params=params(24),
+    )(scalars, static_from_cross, static_from_same, static_minus)
 
     residual, back, same_send, cross_send = pl.pallas_call(
         residual_kernel,
         out_shape=(jax.ShapeDtypeStruct(plane, F32), jax.ShapeDtypeStruct((rows, count), F32), outgoing, outgoing),
-        in_specs=[SMEM] + [VMEM] * 7,
+        in_specs=[VMEM] * 8,
         out_specs=(VMEM,) * 4,
         scratch_shapes=[pltpu.VMEM((2 * levels, count), F32), pltpu.VMEM((2 * levels, count), F32)],
         compiler_params=params(24),
     )(
-        scalars, source_row.reshape(1, fine_slots), row_weight.reshape(1, fine_slots), total, from_same, from_cross,
+        scalars, source_row.reshape(1, fine_slots), row_weight.reshape(1, fine_slots), total, from_cross, from_same,
         static_minus, weight_planes,
     )
     from_cross = cross_chip(cross_send)
@@ -407,7 +433,7 @@
     own_static = pl.pallas_call(
         own_gradient_kernel,
         out_shape=jax.ShapeDtypeStruct(static_control.shape, F32),
-        in_specs=[SMEM] + [VMEM] * 2,
+        in_specs=[VMEM] * 3,
         out_specs=VMEM,
         scratch_shapes=[pltpu.VMEM(plane, F32)],
         compiler_params=params(24),
@@ -416,7 +442,7 @@
     return pl.pallas_call(
         gradient_kernel,
         out_shape=(jax.ShapeDtypeStruct(perturb.shape, BF16), jax.ShapeDtypeStruct(static_control.shape, F32)),
-        in_specs=[SMEM] + [VMEM] * 7,
+        in_specs=[VMEM] * 8,
         out_specs=(HBM, HBM),
         scratch_shapes=[
             pltpu.VMEM((rows, count), F32),
@@ -427,7 +453,7 @@
             pltpu.SemaphoreType.DMA((1 + steps,)),
         ],
         compiler_params=params(24),
-    )(scalars, back, from_same, from_cross, own_static, alpha_control, perturb, loc_factor)
+    )(scalars, back, from_cross, from_same, own_static, alpha_control, perturb, loc_factor)
 
 
 def solution(mesh):

time: 40.7 us -> 36.6 us (0.90)
  Pallas kernels: 17.7 us -> 14.6 us
  starting transfers between devices: 15.8 us -> 13.5 us
  waiting for transfers between devices: 6.1 us -> 7.35 us
    ppermute x2 -> x3, waiting for transfers between devices: 4.24 us -> 7.33 us  [cross_chip(): return lax.ppermute(x, ('band', 'mem'), pairs)]
    ppermute x2 -> x3, starting transfers between devices: 10.3 us -> 8.19 us  [cross_chip(): return lax.ppermute(x, ('band', 'mem'), pairs)]
    ppermute x3, waiting for transfers between devices: 1.85 us -> 0.01 us  [mem_peer(): return lax.ppermute(x, 'mem', [(i, (i + by) % peers) for i in range(peers)])]
    pallas_call x1, Pallas kernels: 2.25 us -> 1.03 us  [on_device(): pl.pallas_call(residual_kernel, out_shape=(jax.ShapeDtypeStruct(plane, F3...]
    pallas_call x1, Pallas kernels: 2.45 us -> 1.92 us  [on_device(): pl.pallas_call(own_gradient_kernel, out_shape=jax.ShapeDtypeStruct(static...]
    pallas_call x1, Pallas kernels: 0.6 us -> 0.08 us  [on_device(): pl.pallas_call(increment_kernel, out_shape=(jax.ShapeDtypeStruct((rows, c...]
    pallas_call x1, Pallas kernels: 3.71 us -> 3.23 us  [on_device(): pl.pallas_call(gradient_kernel, out_shape=(jax.ShapeDtypeStruct(perturb.s...]
    pallas_call x1 -> x2, Pallas kernels: 3.16 us -> 2.9 us  [the longest x1 2.54 us: on_device(): pl.pallas_call(split_kernel, out_shape=(jax.ShapeDtypeStruct((8, 128), jn...]
  transfers between devices with their start and end apart: 7 -> 9, of which waited for: 4 -> 3; matrix products, arithmetic and copies ran while one was open for 0% -> 0% of each run, Pallas kernels for 14% -> 13%
where the time goes in v3:
time: 36.6 us; the launch traced here: 36.5 us
  Pallas kernels  14.6 us (40%)
  starting transfers between devices  13.5 us (37%)
  waiting for transfers between devices  7.35 us (20%)
  between operations  0.98 us (3%)
    ppermute x3, starting transfers between devices, cross_chip(): return lax.ppermute(x, ('band', 'mem'), pairs)  8.19 us
    ppermute x3, waiting for transfers between devices, cross_chip(): return lax.ppermute(x, ('band', 'mem'), pairs)  7.33 us
    pallas_call x1, Pallas kernels, on_device(): pl.pallas_call(localize_kernel, out_shape=jax.ShapeDtypeStruct((rows, cou...  5.5 us
    ppermute x3, starting transfers between devices, mem_peer(): return lax.ppermute(x, 'mem', [(i, (i + by) % peers) for i in range(peers)])  5.31 us
    pallas_call x1, Pallas kernels, on_device(): pl.pallas_call(gradient_kernel, out_shape=(jax.ShapeDtypeStruct(perturb.s...  3.23 us
    pallas_call x1, Pallas kernels, on_device(): pl.pallas_call(split_kernel, out_shape=(jax.ShapeDtypeStruct((8, 128), jn...  2.54 us
    pallas_call x1, Pallas kernels, on_device(): pl.pallas_call(own_gradient_kernel, out_shape=jax.ShapeDtypeStruct(static...  1.92 us
    pallas_call x1, Pallas kernels, on_device(): pl.pallas_call(residual_kernel, out_shape=(jax.ShapeDtypeStruct(plane, F3...  1.03 us
  transfers between devices with their start and end apart: 9, of which 3 were waited for; matrix products, arithmetic and copies ran while one was open for 0% of the time, Pallas kernels for 13%

profile of v3, /device:TPU:6, one launch (start us, length us, event | category | flops | bytes accessed | tf_op | source)
XLA Modules:
  0.0 36.5 jit_solution(10763607031786308638)
XLA Ops:
  0.7 0.0 slice-start
  0.7 5.5 %shard_map.114.own_ref = f32[16,1536]{1,0:T(8,128)} custom-call(bf16[20,4,4,1536]{3,2,1,0:T(4,128)(2,1)} %alpha_ref.3, bf16[20,4,4,1536]{3,2,1,0:T(4,128)(2,1)} %perturb_ref.3, bf16[1536,1536]{1,0:T(8,128)(2,1)} %loc_ref.3), custom_call_target="tpu_custom_call" | custom-call | tf_op jit(solution)/shard_map/pallas_call | solution.py:363
  6.2 0.0 copy-start.5
  6.2 3.3 %collective-permute-start.2 = (f32[16,1536]{1,0:T(8,128)}, f32[16,1536]{1,0:T(8,128)S(1)}, u32[]{:S(2)}, u32[]{:S(2)}) collective-permute-start(f32[16,1536]{1,0:T(8,128)} %shard_map.114.own_ref), channel_id=1, source_target_pairs={{0,2},{1,3},{2,0},{3,1},{4,6},{5,7},{6,4},{7,5},{8,10},{9,11},{10,... | collective-permute-start | bytes 294920 | tf_op jit(solution)/shard_map/ppermute | solution.py:36
  9.5 1.1 %collective-permute-start.1 = (f32[16,1536]{1,0:T(8,128)}, f32[16,1536]{1,0:T(8,128)S(1)}, u32[]{:S(2)}, u32[]{:S(2)}) collective-permute-start(f32[16,1536]{1,0:T(8,128)} %shard_map.114.own_ref), channel_id=1, source_target_pairs={{0,3},{1,0},{2,1},{3,2},{4,7},{5,4},{6,5},{7,6},{8,11},{9,8},{10,9... | collective-permute-start | bytes 294920 | tf_op jit(solution)/shard_map/ppermute | solution.py:36
  10.6 1.0 %collective-permute-start = (f32[16,1536]{1,0:T(8,128)}, f32[16,1536]{1,0:T(8,128)S(1)}, u32[]{:S(2)}, u32[]{:S(2)}) collective-permute-start(f32[16,1536]{1,0:T(8,128)} %shard_map.114.own_ref), channel_id=1, source_target_pairs={{0,1},{1,2},{2,3},{3,0},{4,5},{5,6},{6,7},{7,4},{8,9},{9,10},{10,1... | collective-permute-start | bytes 294920 | tf_op jit(solution)/shard_map/ppermute | solution.py:36
  11.5 0.0 copy-start.8
  11.6 0.0 copy-start.9
  11.6 2.5 %shard_map.113 = (s32[8,128]{1,0:T(8,128)S(1)}, f32[3,4,16,1536]{3,2,1,0:T(8,128)S(1)}, f32[3,4,16,1536]{3,2,1,0:T(8,128)S(1)}, bf16[3,4,16,1536]{3,2,1,0:T(8,12...) custom-call(s32[1,1]{1,0:T(1,128)} %bitcast.device_ref, s32[1,64]{1,0:T(1,128)S(1)} %bitcast.7, ...), custom_call_target="tpu_custom_call" | custom-call | tf_op jit(solution)/shard_map/pallas_call | solution.py:381
  14.1 4.8 %collective-permute-start.5 = (f32[24,1536]{1,0:T(8,128)S(1)}, f32[24,1536]{1,0:T(8,128)S(1)}, u32[]{:S(2)}, u32[]{:S(2)}) collective-permute-start(f32[24,1536]{1,0:T(8,128)S(1)} %get-tuple-element.19), channel_id=1, source_target_pairs={{4,8},{12,16},{20,24},{28,32},{36,40},{44,48},{52,56},{60,64},{68,... | collective-permute-start | bytes 442376 | tf_op jit(solution)/shard_map/ppermute | solution.py:31
  18.9 0.0 collective-permute-start.6
  18.9 0.0 collective-permute-done.2.c_ref
  19.0 0.0 slice-start.1
  19.0 0.1 shard_map.115
  19.1 1.7 %collective-permute-start.3 = (f32[8,1536]{1,0:T(8,128)S(1)}, f32[8,1536]{1,0:T(8,128)S(1)}, u32[]{:S(2)}, u32[]{:S(2)}) collective-permute-start(f32[8,1536]{1,0:T(8,128)S(1)} %get-tuple-element.17), channel_id=1, source_target_pairs={{4,8},{12,16},{20,24},{28,32},{36,40},{44,48},{52,56},{60,64},{68,... | collective-permute-start | bytes 147464 | tf_op jit(solution)/shard_map/ppermute | solution.py:31
  20.8 1.0 %collective-permute-done.5.cross_ref = f32[24,1536]{1,0:T(8,128)S(1)} collective-permute-done((f32[24,1536]{1,0:T(8,128)S(1)}, f32[24,1536]{1,0:T(8,128)S(1)}, u32[]{:S(2)}, u32[]{:S(2)}) %collective-permute-start.5) | collective-permute-done | bytes 147488 | tf_op jit(solution)/shard_map/ppermute | solution.py:31
  21.8 0.4 shard_map.116.static_ref
  22.1 2.7 %collective-permute-done.3.cross_ref = f32[8,1536]{1,0:T(8,128)S(1)} collective-permute-done((f32[8,1536]{1,0:T(8,128)S(1)}, f32[8,1536]{1,0:T(8,128)S(1)}, u32[]{:S(2)}, u32[]{:S(2)}) %collective-permute-start.3) | collective-permute-done | bytes 49184 | tf_op jit(solution)/shard_map/ppermute | solution.py:31
  24.8 1.0 %shard_map.117 = (f32[3,4,16,1536]{3,2,1,0:T(8,128)S(1)}, f32[16,1536]{1,0:T(8,128)S(1)}, f32[32,1536]{1,0:T(8,128)S(1)}, f32[32,1536]{1,0:T(8,128)S(1)}) custom-call(s32[8,128]{1,0:T(8,128)S(1)} %get-tuple-element.15.scalars_ref, s32[1,16]{1,0:T(1,128)S(1)} %bitcast.9, f32[1,16]{1,0:T(1,128)S(1)} %bitcast.10, f32[16,1536]{1,0:T(8,128)S(1)} %get-tuple-element.16.total_ref, ...), custom_call_target="tpu_custom_call" | custom-call | tf_op jit(solution)/shard_map/pallas_call | solution.py:419
  25.8 1.7 %collective-permute-start.7 = (f32[32,1536]{1,0:T(8,128)S(1)}, f32[32,1536]{1,0:T(8,128)S(1)}, u32[]{:S(2)}, u32[]{:S(2)}) collective-permute-start(f32[32,1536]{1,0:T(8,128)S(1)} %get-tuple-element.24), channel_id=1, source_target_pairs={{4,8},{12,16},{20,24},{28,32},{36,40},{44,48},{52,56},{60,64},{68,... | collective-permute-start | bytes 589832 | tf_op jit(solution)/shard_map/ppermute | solution.py:31
  27.5 0.0 collective-permute-start.8
  27.5 1.9 %shard_map.118.own_static_ref = f32[4,16,4608]{2,1,0:T(8,128)S(1)} custom-call(s32[8,128]{1,0:T(8,128)S(1)} %get-tuple-element.15.scalars_ref, f32[3,4,16,1536]{3,2,1,0:T(8,128)S(1)} %get-tuple-element.26.control_ref, f32[3,4,16,1536]{3,2,1,0:T(8,128)S(1)} %get-tuple-element.27.residual_ref), custom_call_target="tpu_custom_call" | custom-call | tf_op jit(solution)/shard_map/pallas_call | solution.py:433
  29.4 3.7 %collective-permute-done.7.cross_ref = f32[32,1536]{1,0:T(8,128)S(1)} collective-permute-done((f32[32,1536]{1,0:T(8,128)S(1)}, f32[32,1536]{1,0:T(8,128)S(1)}, u32[]{:S(2)}, u32[]{:S(2)}) %collective-permute-start.7) | collective-permute-done | bytes 196640 | tf_op jit(solution)/shard_map/ppermute | solution.py:31
  33.2 3.2 %shard_map.119 = (bf16[20,4,4,1536]{3,2,1,0:T(4,128)(2,1)}, f32[4,16,4608]{2,1,0:T(8,128)}) custom-call(s32[8,128]{1,0:T(8,128)S(1)} %get-tuple-element.15.scalars_ref, f32[16,1536]{1,0:T(8,128)S(1)} %get-tuple-element.23.back_ref, f32[32,1536]{1,0:T(8,128)S(1)} %collective-permute-done.7.cross_ref, f32[32,1536]{1,0:T(8,128)S(1)} %collective-permute-done.8.same_ref, ...), custom_call_target="tpu_custom_call" | custom-call | tf_op jit(solution)/shard_map/pallas_call | solution.py:442
  (26 shorter events, 0.1 us)
Async XLA Ops:
  0.6 10.9 %copy-start.7 = (s32[64]{0:T(128)S(1)}, s32[64]{0:T(128)}, u32[]{:S(2)}) copy-start(s32[64]{0:T(128)} %param.17) | copy-start | bytes 772
  0.6 10.9 %copy-start.6 = (s32[64]{0:T(128)S(1)}, s32[64]{0:T(128)}, u32[]{:S(2)}) copy-start(s32[64]{0:T(128)} %param.16) | copy-start | bytes 772
  0.7 10.9 %copy-start.4 = (bf16[4,16,4608]{2,1,0:T(8,128)(2,1)S(1)}, bf16[4,16,4608]{2,1,0:T(8,128)(2,1)}, u32[]{:S(2)}) copy-start(bf16[4,16,4608]{2,1,0:T(8,128)(2,1)} %weight_ref.1) | copy-start | bytes 1769476
  0.7 10.9 %copy-start.3 = (bf16[4,16,4608]{2,1,0:T(8,128)(2,1)S(1)}, bf16[4,16,4608]{2,1,0:T(8,128)(2,1)}, u32[]{:S(2)}) copy-start(bf16[4,16,4608]{2,1,0:T(8,128)(2,1)} %innovation_ref.1) | copy-start | bytes 1769476
  0.7 10.9 %copy-start.2 = (bf16[4,16,4608]{2,1,0:T(8,128)(2,1)S(1)}, bf16[4,16,4608]{2,1,0:T(8,128)(2,1)}, u32[]{:S(2)}) copy-start(bf16[4,16,4608]{2,1,0:T(8,128)(2,1)} %control_ref.1) | copy-start | bytes 1769476
  0.7 32.4 %slice-start = ((s8[4718592]{0:T(1024)(128)(4,1)}), s8[524288]{0:T(1024)(128)(4,1)S(1)}, s32[]{:S(2)}) async-start(s8[4718592]{0:T(1024)(128)(4,1)} %bitcast.5), calls=%async_computation | async-start | bytes 1048576
  6.2 12.8 %copy-start.5 = (f32[16,1536]{1,0:T(8,128)S(1)}, f32[16,1536]{1,0:T(8,128)}, u32[]{:S(2)}) copy-start(f32[16,1536]{1,0:T(8,128)} %shard_map.114.own_ref) | copy-start | bytes 294916
  6.2 12.7 %collective-permute-start.2 = (f32[16,1536]{1,0:T(8,128)}, f32[16,1536]{1,0:T(8,128)S(1)}, u32[]{:S(2)}, u32[]{:S(2)}) collective-permute-start(f32[16,1536]{1,0:T(8,128)} %shard_map.114.own_ref), channel_id=1, source_target_pairs={{0,2},{1,3},{2,0},{3,1},{4,6},{5,7},{6,4},{7,5},{8,10},{9,11},{10,... | collective-permute-start | bytes 294920 | tf_op jit(solution)/shard_map/ppermute | solution.py:36
  9.5 9.4 %collective-permute-start.1 = (f32[16,1536]{1,0:T(8,128)}, f32[16,1536]{1,0:T(8,128)S(1)}, u32[]{:S(2)}, u32[]{:S(2)}) collective-permute-start(f32[16,1536]{1,0:T(8,128)} %shard_map.114.own_ref), channel_id=1, source_target_pairs={{0,3},{1,0},{2,1},{3,2},{4,7},{5,4},{6,5},{7,6},{8,11},{9,8},{10,9... | collective-permute-start | bytes 294920 | tf_op jit(solution)/shard_map/ppermute | solution.py:36
  10.6 8.4 %collective-permute-start = (f32[16,1536]{1,0:T(8,128)}, f32[16,1536]{1,0:T(8,128)S(1)}, u32[]{:S(2)}, u32[]{:S(2)}) collective-permute-start(f32[16,1536]{1,0:T(8,128)} %shard_map.114.own_ref), channel_id=1, source_target_pairs={{0,1},{1,2},{2,3},{3,0},{4,5},{5,6},{6,7},{7,4},{8,9},{9,10},{10,1... | collective-permute-start | bytes 294920 | tf_op jit(solution)/shard_map/ppermute | solution.py:36
  11.5 13.2 %copy-start.8 = (s32[16]{0:T(128)S(1)}, s32[16]{0:T(128)}, u32[]{:S(2)}) copy-start(s32[16]{0:T(128)} %param.18) | copy-start | bytes 196
  11.6 13.2 %copy-start.9 = (f32[16]{0:T(128)S(1)}, f32[16]{0:T(128)}, u32[]{:S(2)}) copy-start(f32[16]{0:T(128)} %param.19) | copy-start | bytes 196
  14.1 7.6 %collective-permute-start.5 = (f32[24,1536]{1,0:T(8,128)S(1)}, f32[24,1536]{1,0:T(8,128)S(1)}, u32[]{:S(2)}, u32[]{:S(2)}) collective-permute-start(f32[24,1536]{1,0:T(8,128)S(1)} %get-tuple-element.19), channel_id=1, source_target_pairs={{4,8},{12,16},{20,24},{28,32},{36,40},{44,48},{52,56},{60,64},{68,... | collective-permute-start | bytes 442376 | tf_op jit(solution)/shard_map/ppermute | solution.py:31
  18.9 2.8 %collective-permute-start.6 = (f32[24,1536]{1,0:T(8,128)S(1)}, f32[24,1536]{1,0:T(8,128)S(1)}, u32[]{:S(2)}, u32[]{:S(2)}) collective-permute-start(f32[24,1536]{1,0:T(8,128)S(1)} %get-tuple-element.20), channel_id=1, source_target_pairs={{0,4},{4,0},{8,12},{12,8},{16,20},{20,16},{24,28},{28,24},{32,36},... | collective-permute-start | bytes 442376 | tf_op jit(solution)/shard_map/ppermute | solution.py:21
  19.0 14.2 %slice-start.1 = ((s8[4718592]{0:T(1024)(128)(4,1)}), s8[4194304]{0:T(1024)(128)(4,1)S(1)}, s32[]{:S(2)}) async-start(s8[4718592]{0:T(1024)(128)(4,1)} %bitcast.5), calls=%async_computation.1 | async-start | bytes 8388608
  19.1 5.7 %collective-permute-start.3 = (f32[8,1536]{1,0:T(8,128)S(1)}, f32[8,1536]{1,0:T(8,128)S(1)}, u32[]{:S(2)}, u32[]{:S(2)}) collective-permute-start(f32[8,1536]{1,0:T(8,128)S(1)} %get-tuple-element.17), channel_id=1, source_target_pairs={{4,8},{12,16},{20,24},{28,32},{36,40},{44,48},{52,56},{60,64},{68,... | collective-permute-start | bytes 147464 | tf_op jit(solution)/shard_map/ppermute | solution.py:31
  20.8 4.0 %collective-permute-start.4 = (f32[8,1536]{1,0:T(8,128)S(1)}, f32[8,1536]{1,0:T(8,128)S(1)}, u32[]{:S(2)}, u32[]{:S(2)}) collective-permute-start(f32[8,1536]{1,0:T(8,128)S(1)} %get-tuple-element.18), channel_id=1, source_target_pairs={{0,4},{4,0},{8,12},{12,8},{16,20},{20,16},{24,28},{28,24},{32,36},... | collective-permute-start | bytes 147464 | tf_op jit(solution)/shard_map/ppermute | solution.py:21
  25.8 7.3 %collective-permute-start.7 = (f32[32,1536]{1,0:T(8,128)S(1)}, f32[32,1536]{1,0:T(8,128)S(1)}, u32[]{:S(2)}, u32[]{:S(2)}) collective-permute-start(f32[32,1536]{1,0:T(8,128)S(1)} %get-tuple-element.24), channel_id=1, source_target_pairs={{4,8},{12,16},{20,24},{28,32},{36,40},{44,48},{52,56},{60,64},{68,... | collective-permute-start | bytes 589832 | tf_op jit(solution)/shard_map/ppermute | solution.py:31
  27.5 5.6 %collective-permute-start.8 = (f32[32,1536]{1,0:T(8,128)S(1)}, f32[32,1536]{1,0:T(8,128)S(1)}, u32[]{:S(2)}, u32[]{:S(2)}) collective-permute-start(f32[32,1536]{1,0:T(8,128)S(1)} %get-tuple-element.25), channel_id=1, source_target_pairs={{0,4},{4,0},{8,12},{12,8},{16,20},{20,16},{24,28},{28,24},{32,36},... | collective-permute-start | bytes 589832 | tf_op jit(solution)/shard_map/ppermute | solution.py:21
  27.5 5.6 %copy-start = (bf16[20,4,4,1536]{3,2,1,0:T(4,128)(2,1)S(1)}, bf16[20,4,4,1536]{3,2,1,0:T(4,128)(2,1)}, u32[]{:S(2)}) copy-start(bf16[20,4,4,1536]{3,2,1,0:T(4,128)(2,1)} %alpha_ref.3) | copy-start | bytes 2949124
  27.5 5.6 %copy-start.1 = (bf16[20,4,4,1536]{3,2,1,0:T(4,128)(2,1)S(1)}, bf16[20,4,4,1536]{3,2,1,0:T(4,128)(2,1)}, u32[]{:S(2)}) copy-start(bf16[20,4,4,1536]{3,2,1,0:T(4,128)(2,1)} %perturb_ref.3) | copy-start | bytes 2949124

commit v4 on v3

--- a/solution.py
+++ b/solution.py
@@ -126,10 +126,7 @@
         out_ref[:, span] = jnp.sum((perturb * localized).reshape(members, levels * slots, chunk), axis=0)
 
 
-def split_kernel(
-    device_ref, coarse_ref, fine_ref, control_ref, innovation_ref, weight_ref,
-    scalars_out, control_out, static_out, weight_out, same_out, cross_out, innovation_scr,
-):
+def edges_kernel(device_ref, coarse_ref, fine_ref, control_ref, after_ref, scalars_out, same_out, cross_out):
     bands = coarse_ref.shape[1]
     device = device_ref[0, 0]
     parity = device % 2
@@ -140,8 +137,32 @@
     for i, value in enumerate((own_coarse, own_fine, device, parity, bands, first_row)):
         scalars_out[i : i + 1, :] = jnp.full((1, scalars_out.shape[1]), value, jnp.int32)
     levels, slots, count = control_ref.shape
+    same_start = jnp.where(parity == 0, own_fine - 2, 0)
+    cross_start = jnp.where(parity == 0, 0, own_fine - 2)
+    take = lax.broadcasted_iota(jnp.int32, (8, slots), 0)
+    slot = lax.broadcasted_iota(jnp.int32, (8, slots), 1)
+    wanted = jnp.where(take < 2, same_start + take, cross_start + take - 2)
+    pick = ((slot == wanted) & (take < 4)).astype(BF16)
     width = 128
-    table = triple_table(width, False)
+    blocks = count // (3 * width)
+    rows = [jnp.dot(pick, control_ref[l], preferred_element_type=F32) for l in range(levels)]
+    stacked = [rows[l][:, 3 * width * i : 3 * width * (i + 1)] for i in range(blocks) for l in range(levels)]
+    stacked = jnp.concatenate(stacked, axis=0).astype(BF16)
+    planes = jnp.dot(stacked, triple_table(width, False), preferred_element_type=F32)
+    for i in range(blocks):
+        out = slice(width * i, width * (i + 1))
+        for l in range(levels):
+            at = (i * levels + l) * 8
+            for p in range(3):
+                to = (p * levels + l) * 2
+                same_out[to : to + 2, out] = planes[at : at + 2, p * width : (p + 1) * width]
+                cross_out[to : to + 2, out] = planes[at + 2 : at + 4, p * width : (p + 1) * width]
+
+
+def planes_kernel(scalars_ref, after_ref, control_ref, innovation_ref, weight_ref, control_out, innovation_out, weight_out):
+    own_fine = scalars_ref[1, 0]
+    levels, slots, count = control_ref.shape
+    width = 128
     rows = levels * slots
     live = (lax.broadcasted_iota(jnp.int32, (rows, 1), 0) % slots < own_fine).astype(F32)
     blocks = count // (3 * width)
@@ -150,7 +171,7 @@
         for r in (control_ref, innovation_ref, weight_ref)
         for i in range(blocks)
     ]
-    planes = jnp.dot(jnp.concatenate(stacked, axis=0), table, preferred_element_type=F32)
+    planes = jnp.dot(jnp.concatenate(stacked, axis=0), triple_table(width, False), preferred_element_type=F32)
     for i in range(blocks):
         out = slice(width * i, width * (i + 1))
         for p in range(3):
@@ -158,35 +179,26 @@
                 planes[rows * (k * blocks + i) : rows * (k * blocks + i + 1), p * width : (p + 1) * width] for k in range(3)
             )
             control_out[p, :, :, out] = (control * live).reshape(levels, slots, width)
-            innovation_scr[p, :, :, out] = innovation.reshape(levels, slots, width)
+            innovation_out[p, :, :, out] = innovation.reshape(levels, slots, width).astype(BF16)
             weight_out[p, :, :, out] = (weight * live).reshape(levels, slots, width).astype(BF16)
-    same_start = jnp.where(parity == 0, own_fine - 2, 0)
-    cross_start = jnp.where(parity == 0, 0, own_fine - 2)
+
+
+def static_kernel(scalars_ref, cross_ref, same_ref, control_ref, innovation_ref, static_out):
+    own_fine = scalars_ref[1, 0]
+    planes, levels, slots, count = control_ref.shape
+    size = 2 * levels
     row_ids = lax.broadcasted_iota(jnp.int32, (slots, 1), 0)
-    exists = (device > 0).astype(F32), (device < bands - 1).astype(F32)
-    for l in range(levels):
-        for p in range(3):
-            at = (p * levels + l) * 2
-            for k in range(2):
-                same_out[at + k : at + k + 1, :] = control_out[p, l, pl.ds(same_start + k, 1), :]
-                cross_out[at + k : at + k + 1, :] = control_out[p, l, pl.ds(cross_start + k, 1), :]
-        own = [control_out[p, l] for p in range(3)]
-        first = [control_out[p, l, 0:1, :] for p in range(3)]
-        last = [control_out[p, l, pl.ds(own_fine - 1, 1), :] for p in range(3)]
-        result = spread_own(own, first, last, own_fine, row_ids, exists)
-        for p in range(3):
-            static_out[p, l] = result[p] - innovation_scr[p, l]
-
-
-def static_edge_kernel(scalars_ref, cross_ref, same_ref, static_in, static_out):
-    own_fine = scalars_ref[1, 0]
-    planes, levels, slots, count = static_out.shape
-    size = 2 * levels
+    exists = neighbours(scalars_ref)
     halos = [halo_rows(same_ref, cross_ref, scalars_ref, p * size, size) for p in range(3)]
     lower = spread_halo([h[0] for h in halos], 1)
     higher = spread_halo([h[1] for h in halos], 0)
-    for p in range(3):
-        for l in range(levels):
+    for l in range(levels):
+        own = [control_ref[p, l] for p in range(3)]
+        first = [control_ref[p, l, 0:1, :] for p in range(3)]
+        last = [control_ref[p, l, pl.ds(own_fine - 1, 1), :] for p in range(3)]
+        result = spread_own(own, first, last, own_fine, row_ids, exists)
+        for p in range(3):
+            static_out[p, l] = result[p] - innovation_ref[p, l].astype(F32)
             static_out[p, l, 0:2, :] += lower[p][2 * l : 2 * l + 2]
             for k in range(2):
                 static_out[p, l, pl.ds(own_fine - 2 + k, 1), :] += higher[p][2 * l + k : 2 * l + k + 1]
@@ -378,25 +390,15 @@
     plane = (3, levels, fine_slots, count)
     outgoing = jax.ShapeDtypeStruct((8 * levels, count), F32)
     wide = jax.ShapeDtypeStruct((6 * levels, count), F32)
-    scalars, control, static_minus, weight_planes, same_send, cross_send = pl.pallas_call(
-        split_kernel,
-        out_shape=(
-            jax.ShapeDtypeStruct((8, 128), jnp.int32),
-            jax.ShapeDtypeStruct(plane, F32),
-            jax.ShapeDtypeStruct(plane, F32),
-            jax.ShapeDtypeStruct(plane, BF16),
-            wide,
-            wide,
-        ),
-        in_specs=[VMEM] * 6,
-        out_specs=(VMEM,) * 6,
-        scratch_shapes=[pltpu.VMEM(plane, F32)],
-        compiler_params=params(24),
-    )(device, coarse_rows.reshape(1, -1), fine_rows.reshape(1, -1), static_control, innovation, obs_weight)
-
+    scalars, same_send, cross_send = pl.pallas_call(
+        edges_kernel,
+        out_shape=(jax.ShapeDtypeStruct((8, 128), jnp.int32), wide, wide),
+        in_specs=[VMEM] * 4 + [HBM],
+        out_specs=(VMEM,) * 3,
+        compiler_params=params(24),
+    )(device, coarse_rows.reshape(1, -1), fine_rows.reshape(1, -1), static_control, partial)
     static_from_cross = cross_chip(cross_send)
     static_from_same = same_chip(same_send)
-
     pair = jax.ShapeDtypeStruct((2 * levels, count), F32)
     total, same_send, cross_send = pl.pallas_call(
         increment_kernel,
@@ -407,14 +409,22 @@
     )(scalars, partial, *peers)
     from_cross = cross_chip(cross_send)
     from_same = same_chip(same_send)
+    control, innovation_planes, weight_planes = pl.pallas_call(
+        planes_kernel,
+        out_shape=(
+            jax.ShapeDtypeStruct(plane, F32), jax.ShapeDtypeStruct(plane, BF16), jax.ShapeDtypeStruct(plane, BF16)
+        ),
+        in_specs=[VMEM, HBM] + [VMEM] * 3,
+        out_specs=(VMEM,) * 3,
+        compiler_params=params(24),
+    )(scalars, total, static_control, innovation, obs_weight)
     static_minus = pl.pallas_call(
-        static_edge_kernel,
+        static_kernel,
         out_shape=jax.ShapeDtypeStruct(plane, F32),
-        in_specs=[VMEM] * 4,
+        in_specs=[VMEM] * 5,
         out_specs=VMEM,
-        input_output_aliases={3: 0},
-        compiler_params=params(24),
-    )(scalars, static_from_cross, static_from_same, static_minus)
+        compiler_params=params(24),
+    )(scalars, static_from_cross, static_from_same, control, innovation_planes)
 
     residual, back, same_send, cross_send = pl.pallas_call(
         residual_kernel,

time: 36.6 us -> 35.6 us (0.973)
  waiting for transfers between devices: 7.35 us -> 3.11 us
  starting transfers between devices: 13.5 us -> 15.2 us
  local copies, waits for them, and re-layouts: 0.06 us -> 0.97 us
  Pallas kernels: 14.6 us -> 15.2 us
    ppermute x3, waiting for transfers between devices: 7.33 us -> 3.1 us  [cross_chip(): return lax.ppermute(x, ('band', 'mem'), pairs)]
    ppermute x3, starting transfers between devices: 8.19 us -> 9.86 us  [cross_chip(): return lax.ppermute(x, ('band', 'mem'), pairs)]
    unnamed x24, local copies, waits for them, and re-layouts: 0.06 us -> 0.97 us
    pallas_call x2 -> x3, Pallas kernels: 2.9 us -> 3.58 us  [the longest x1 1.59 us: on_device(): pl.pallas_call(static_kernel, out_shape=jax.ShapeDtypeStruct(plane, F32),...]
  transfers between devices with their start and end apart: 9 -> 9, of which waited for: 3 -> 2; matrix products, arithmetic and copies ran while one was open for 0% -> 0% of each run, Pallas kernels for 13% -> 16%
where the time goes in v4:
time: 35.6 us; the launch traced here: 35.4 us
  Pallas kernels  15.2 us (43%)
  starting transfers between devices  15.2 us (43%)
  waiting for transfers between devices  3.11 us (9%)
  local copies, waits for them, and re-layouts  0.97 us (3%)
  between operations  0.97 us (3%)
    ppermute x3, starting transfers between devices, cross_chip(): return lax.ppermute(x, ('band', 'mem'), pairs)  9.86 us
    pallas_call x1, Pallas kernels, on_device(): pl.pallas_call(localize_kernel, out_shape=jax.ShapeDtypeStruct((rows, cou...  5.36 us
    ppermute x3, starting transfers between devices, mem_peer(): return lax.ppermute(x, 'mem', [(i, (i + by) % peers) for i in range(peers)])  5.31 us
    pallas_call x1, Pallas kernels, on_device(): pl.pallas_call(gradient_kernel, out_shape=(jax.ShapeDtypeStruct(perturb.s...  3.23 us
    ppermute x3, waiting for transfers between devices, cross_chip(): return lax.ppermute(x, ('band', 'mem'), pairs)  3.1 us
    pallas_call x1, Pallas kernels, on_device(): pl.pallas_call(own_gradient_kernel, out_shape=jax.ShapeDtypeStruct(static...  1.92 us
    pallas_call x1, Pallas kernels, on_device(): pl.pallas_call(static_kernel, out_shape=jax.ShapeDtypeStruct(plane, F32),...  1.59 us
    pallas_call x1, Pallas kernels, on_device(): pl.pallas_call(planes_kernel, out_shape=(jax.ShapeDtypeStruct(plane, F32)...  1.24 us
  transfers between devices with their start and end apart: 9, of which 2 were waited for; matrix products, arithmetic and copies ran while one was open for 0% of the time, Pallas kernels for 16%

profile of v4, /device:TPU:6, one launch (start us, length us, event | category | flops | bytes accessed | tf_op | source)
XLA Modules:
  0.0 35.4 jit_solution(4857543617451567264)
XLA Ops:
  0.7 5.4 %shard_map.113.after_ref.own_ref = f32[16,1536]{1,0:T(8,128)} custom-call(bf16[20,4,4,1536]{3,2,1,0:T(4,128)(2,1)} %alpha_ref.3, bf16[20,4,4,1536]{3,2,1,0:T(4,128)(2,1)} %perturb_ref.3, bf16[1536,1536]{1,0:T(8,128)(2,1)} %loc_ref.3), custom_call_target="tpu_custom_call" | custom-call | tf_op jit(solution)/shard_map/pallas_call | solution.py:375
  6.0 3.3 %collective-permute-start.2 = (f32[16,1536]{1,0:T(8,128)}, f32[16,1536]{1,0:T(8,128)S(1)}, u32[]{:S(2)}, u32[]{:S(2)}) collective-permute-start(f32[16,1536]{1,0:T(8,128)} %shard_map.113.after_ref.own_ref), channel_id=1, source_target_pairs={{0,2},{1,3},{2,0},{3,1},{4,6},{5,7},{6,4},{7,5},{8,10},{9,11},{10,... | collective-permute-start | bytes 294920 | tf_op jit(solution)/shard_map/ppermute | solution.py:36
  9.3 1.1 %collective-permute-start.1 = (f32[16,1536]{1,0:T(8,128)}, f32[16,1536]{1,0:T(8,128)S(1)}, u32[]{:S(2)}, u32[]{:S(2)}) collective-permute-start(f32[16,1536]{1,0:T(8,128)} %shard_map.113.after_ref.own_ref), channel_id=1, source_target_pairs={{0,3},{1,0},{2,1},{3,2},{4,7},{5,4},{6,5},{7,6},{8,11},{9,8},{10,9... | collective-permute-start | bytes 294920 | tf_op jit(solution)/shard_map/ppermute | solution.py:36
  10.4 1.0 %collective-permute-start = (f32[16,1536]{1,0:T(8,128)}, f32[16,1536]{1,0:T(8,128)S(1)}, u32[]{:S(2)}, u32[]{:S(2)}) collective-permute-start(f32[16,1536]{1,0:T(8,128)} %shard_map.113.after_ref.own_ref), channel_id=1, source_target_pairs={{0,1},{1,2},{2,3},{3,0},{4,5},{5,6},{6,7},{7,4},{8,9},{9,10},{10,1... | collective-permute-start | bytes 294920 | tf_op jit(solution)/shard_map/ppermute | solution.py:36
  11.4 0.9 %copy-done.3 = f32[16,1536]{1,0:T(8,128)S(1)} copy-done((f32[16,1536]{1,0:T(8,128)S(1)}, f32[16,1536]{1,0:T(8,128)}, u32[]{:S(2)}) %copy-start.3) | copy-done | bytes 98328
  12.3 0.8 %shard_map.114 = (s32[8,128]{1,0:T(8,128)S(1)}, f32[24,1536]{1,0:T(8,128)S(1)}, f32[24,1536]{1,0:T(8,128)S(1)}) custom-call(s32[1,1]{1,0:T(1,128)} %bitcast.device_ref, s32[1,64]{1,0:T(1,128)S(1)} %bitcast.7, s32[1,64]{1,0:T(1,128)S(1)} %bitcast.8, bf16[4,16,4608]{2,1,0:T(8,128)(2,1)S(1)} %copy-done.2, f32[16,1536]{1,0:T(8,128)S(1)} %copy-done.3), custom_call_target="tpu_custom_call" | custom-call | tf_op jit(solution)/shard_map/pallas_call | solution.py:393
  13.0 4.8 %collective-permute-start.5 = (f32[24,1536]{1,0:T(8,128)S(1)}, f32[24,1536]{1,0:T(8,128)S(1)}, u32[]{:S(2)}, u32[]{:S(2)}) collective-permute-start(f32[24,1536]{1,0:T(8,128)S(1)} %get-tuple-element.19), channel_id=1, source_target_pairs={{4,8},{12,16},{20,24},{28,32},{36,40},{44,48},{52,56},{60,64},{68,... | collective-permute-start | bytes 442376 | tf_op jit(solution)/shard_map/ppermute | solution.py:31
  17.8 0.0 collective-permute-start.6
  17.8 0.0 collective-permute-done.2.c_ref
  17.8 0.0 collective-permute-done.1.b_ref
  17.9 0.1 shard_map.115
  17.9 2.5 %collective-permute-start.3 = (f32[8,1536]{1,0:T(8,128)S(1)}, f32[8,1536]{1,0:T(8,128)S(1)}, u32[]{:S(2)}, u32[]{:S(2)}) collective-permute-start(f32[8,1536]{1,0:T(8,128)S(1)} %get-tuple-element.17), channel_id=1, source_target_pairs={{4,8},{12,16},{20,24},{28,32},{36,40},{44,48},{52,56},{60,64},{68,... | collective-permute-start | bytes 147464 | tf_op jit(solution)/shard_map/ppermute | solution.py:31
  20.5 1.2 %shard_map.116 = (f32[3,4,16,1536]{3,2,1,0:T(8,128)S(1)}, bf16[3,4,16,1536]{3,2,1,0:T(8,128)(2,1)S(1)}, bf16[3,4,16,1536]{3,2,1,0:T(8,128)(2,1)S(1)}) custom-call(s32[8,128]{1,0:T(8,128)S(1)} %get-tuple-element.15.scalars_ref, f32[16,1536]{1,0:T(8,128)S(1)} %get-tuple-element.16.after_ref.total_ref, bf16[4,16,4608]{2,1,0:T(8,128)(2,1)S(1)} %copy-done.2, ...), custom_call_target="tpu_custom_call" | custom-call | tf_op jit(solution)/shard_map/pallas_call | solution.py:412
  21.7 0.0 copy-start.8
  21.7 0.0 copy-start.9
  21.8 0.0 slice-start.1
  21.8 1.6 %shard_map.117.static_ref = f32[3,4,16,1536]{3,2,1,0:T(8,128)S(1)} custom-call(s32[8,128]{1,0:T(8,128)S(1)} %get-tuple-element.15.scalars_ref, f32[24,1536]{1,0:T(8,128)S(1)} %collective-permute-done.5.cross_ref, f32[24,1536]{1,0:T(8,128)S(1)} %collective-permute-done.6.same_ref, f32[3,4,16,1536]{3,2,1,0:T(8,128)S(1)} %get-tuple-element.21.control_ref, ...), custom_call_target="tpu_custom_call" | custom-call | tf_op jit(solution)/shard_map/pallas_call | solution.py:421
  23.4 0.3 collective-permute-done.3.cross_ref
  23.7 1.0 %shard_map.118 = (f32[3,4,16,1536]{3,2,1,0:T(8,128)S(1)}, f32[16,1536]{1,0:T(8,128)S(1)}, f32[32,1536]{1,0:T(8,128)S(1)}, f32[32,1536]{1,0:T(8,128)S(1)}) custom-call(s32[8,128]{1,0:T(8,128)S(1)} %get-tuple-element.15.scalars_ref, s32[1,16]{1,0:T(1,128)S(1)} %bitcast.9, f32[1,16]{1,0:T(1,128)S(1)} %bitcast.10, ...), custom_call_target="tpu_custom_call" | custom-call | tf_op jit(solution)/shard_map/pallas_call | solution.py:429
  24.7 2.6 %collective-permute-start.7 = (f32[32,1536]{1,0:T(8,128)S(1)}, f32[32,1536]{1,0:T(8,128)S(1)}, u32[]{:S(2)}, u32[]{:S(2)}) collective-permute-start(f32[32,1536]{1,0:T(8,128)S(1)} %get-tuple-element.25), channel_id=1, source_target_pairs={{4,8},{12,16},{20,24},{28,32},{36,40},{44,48},{52,56},{60,64},{68,... | collective-permute-start | bytes 589832 | tf_op jit(solution)/shard_map/ppermute | solution.py:31
  27.3 0.0 collective-permute-start.8
  27.3 1.9 %shard_map.119.own_static_ref = f32[4,16,4608]{2,1,0:T(8,128)S(1)} custom-call(s32[8,128]{1,0:T(8,128)S(1)} %get-tuple-element.15.scalars_ref, f32[3,4,16,1536]{3,2,1,0:T(8,128)S(1)} %get-tuple-element.21.control_ref, f32[3,4,16,1536]{3,2,1,0:T(8,128)S(1)} %get-tuple-element.27.residual_ref), custom_call_target="tpu_custom_call" | custom-call | tf_op jit(solution)/shard_map/pallas_call | solution.py:443
  29.2 2.8 %collective-permute-done.7.cross_ref = f32[32,1536]{1,0:T(8,128)S(1)} collective-permute-done((f32[32,1536]{1,0:T(8,128)S(1)}, f32[32,1536]{1,0:T(8,128)S(1)}, u32[]{:S(2)}, u32[]{:S(2)}) %collective-permute-start.7) | collective-permute-done | bytes 196640 | tf_op jit(solution)/shard_map/ppermute | solution.py:31
  32.1 3.2 %shard_map.120 = (bf16[20,4,4,1536]{3,2,1,0:T(4,128)(2,1)}, f32[4,16,4608]{2,1,0:T(8,128)}) custom-call(s32[8,128]{1,0:T(8,128)S(1)} %get-tuple-element.15.scalars_ref, f32[16,1536]{1,0:T(8,128)S(1)} %get-tuple-element.24.back_ref, f32[32,1536]{1,0:T(8,128)S(1)} %collective-permute-done.7.cross_ref, f32[32,1536]{1,0:T(8,128)S(1)} %collective-permute-done.8.same_ref, ...), custom_call_target="tpu_custom_call" | custom-call | tf_op jit(solution)/shard_map/pallas_call | solution.py:452
  (27 shorter events, 0.1 us)
Async XLA Ops:
  0.6 10.7 %copy-start.2 = (bf16[4,16,4608]{2,1,0:T(8,128)(2,1)S(1)}, bf16[4,16,4608]{2,1,0:T(8,128)(2,1)}, u32[]{:S(2)}) copy-start(bf16[4,16,4608]{2,1,0:T(8,128)(2,1)} %control_ref.3) | copy-start | bytes 1769476
  0.6 10.7 %copy-start.7 = (s32[64]{0:T(128)S(1)}, s32[64]{0:T(128)}, u32[]{:S(2)}) copy-start(s32[64]{0:T(128)} %param.17) | copy-start | bytes 772
  0.7 10.7 %copy-start.6 = (s32[64]{0:T(128)S(1)}, s32[64]{0:T(128)}, u32[]{:S(2)}) copy-start(s32[64]{0:T(128)} %param.16) | copy-start | bytes 772
  0.7 19.8 %copy-start.4 = (bf16[4,16,4608]{2,1,0:T(8,128)(2,1)S(1)}, bf16[4,16,4608]{2,1,0:T(8,128)(2,1)}, u32[]{:S(2)}) copy-start(bf16[4,16,4608]{2,1,0:T(8,128)(2,1)} %innovation_ref.1) | copy-start | bytes 1769476
  0.7 19.8 %copy-start.5 = (bf16[4,16,4608]{2,1,0:T(8,128)(2,1)S(1)}, bf16[4,16,4608]{2,1,0:T(8,128)(2,1)}, u32[]{:S(2)}) copy-start(bf16[4,16,4608]{2,1,0:T(8,128)(2,1)} %weight_ref.1) | copy-start | bytes 1769476
  6.0 11.8 %collective-permute-start.2 = (f32[16,1536]{1,0:T(8,128)}, f32[16,1536]{1,0:T(8,128)S(1)}, u32[]{:S(2)}, u32[]{:S(2)}) collective-permute-start(f32[16,1536]{1,0:T(8,128)} %shard_map.113.after_ref.own_ref), channel_id=1, source_target_pairs={{0,2},{1,3},{2,0},{3,1},{4,6},{5,7},{6,4},{7,5},{8,10},{9,11},{10,... | collective-permute-start | bytes 294920 | tf_op jit(solution)/shard_map/ppermute | solution.py:36
  9.3 8.5 %collective-permute-start.1 = (f32[16,1536]{1,0:T(8,128)}, f32[16,1536]{1,0:T(8,128)S(1)}, u32[]{:S(2)}, u32[]{:S(2)}) collective-permute-start(f32[16,1536]{1,0:T(8,128)} %shard_map.113.after_ref.own_ref), channel_id=1, source_target_pairs={{0,3},{1,0},{2,1},{3,2},{4,7},{5,4},{6,5},{7,6},{8,11},{9,8},{10,9... | collective-permute-start | bytes 294920 | tf_op jit(solution)/shard_map/ppermute | solution.py:36
  10.4 7.5 %collective-permute-start = (f32[16,1536]{1,0:T(8,128)}, f32[16,1536]{1,0:T(8,128)S(1)}, u32[]{:S(2)}, u32[]{:S(2)}) collective-permute-start(f32[16,1536]{1,0:T(8,128)} %shard_map.113.after_ref.own_ref), channel_id=1, source_target_pairs={{0,1},{1,2},{2,3},{3,0},{4,5},{5,6},{6,7},{7,4},{8,9},{9,10},{10,1... | collective-permute-start | bytes 294920 | tf_op jit(solution)/shard_map/ppermute | solution.py:36
  11.4 0.9 %copy-start.3 = (f32[16,1536]{1,0:T(8,128)S(1)}, f32[16,1536]{1,0:T(8,128)}, u32[]{:S(2)}) copy-start(f32[16,1536]{1,0:T(8,128)} %shard_map.113.after_ref.own_ref) | copy-start | bytes 294916
  12.3 19.7 %slice-start = ((s8[4718592]{0:T(1024)(128)(4,1)}), s8[4194304]{0:T(1024)(128)(4,1)S(1)}, s32[]{:S(2)}) async-start(s8[4718592]{0:T(1024)(128)(4,1)} %bitcast.5), calls=%async_computation | async-start | bytes 8388608
  13.0 8.7 %collective-permute-start.5 = (f32[24,1536]{1,0:T(8,128)S(1)}, f32[24,1536]{1,0:T(8,128)S(1)}, u32[]{:S(2)}, u32[]{:S(2)}) collective-permute-start(f32[24,1536]{1,0:T(8,128)S(1)} %get-tuple-element.19), channel_id=1, source_target_pairs={{4,8},{12,16},{20,24},{28,32},{36,40},{44,48},{52,56},{60,64},{68,... | collective-permute-start | bytes 442376 | tf_op jit(solution)/shard_map/ppermute | solution.py:31
  17.8 3.9 %collective-permute-start.6 = (f32[24,1536]{1,0:T(8,128)S(1)}, f32[24,1536]{1,0:T(8,128)S(1)}, u32[]{:S(2)}, u32[]{:S(2)}) collective-permute-start(f32[24,1536]{1,0:T(8,128)S(1)} %get-tuple-element.20), channel_id=1, source_target_pairs={{0,4},{4,0},{8,12},{12,8},{16,20},{20,16},{24,28},{28,24},{32,36},... | collective-permute-start | bytes 442376 | tf_op jit(solution)/shard_map/ppermute | solution.py:21
  17.9 5.7 %collective-permute-start.3 = (f32[8,1536]{1,0:T(8,128)S(1)}, f32[8,1536]{1,0:T(8,128)S(1)}, u32[]{:S(2)}, u32[]{:S(2)}) collective-permute-start(f32[8,1536]{1,0:T(8,128)S(1)} %get-tuple-element.17), channel_id=1, source_target_pairs={{4,8},{12,16},{20,24},{28,32},{36,40},{44,48},{52,56},{60,64},{68,... | collective-permute-start | bytes 147464 | tf_op jit(solution)/shard_map/ppermute | solution.py:31
  20.4 3.2 %collective-permute-start.4 = (f32[8,1536]{1,0:T(8,128)S(1)}, f32[8,1536]{1,0:T(8,128)S(1)}, u32[]{:S(2)}, u32[]{:S(2)}) collective-permute-start(f32[8,1536]{1,0:T(8,128)S(1)} %get-tuple-element.18), channel_id=1, source_target_pairs={{0,4},{4,0},{8,12},{12,8},{16,20},{20,16},{24,28},{28,24},{32,36},... | collective-permute-start | bytes 147464 | tf_op jit(solution)/shard_map/ppermute | solution.py:21
  21.7 1.9 %copy-start.8 = (s32[16]{0:T(128)S(1)}, s32[16]{0:T(128)}, u32[]{:S(2)}) copy-start(s32[16]{0:T(128)} %param.18) | copy-start | bytes 196
  21.7 1.9 %copy-start.9 = (f32[16]{0:T(128)S(1)}, f32[16]{0:T(128)}, u32[]{:S(2)}) copy-start(f32[16]{0:T(128)} %param.19) | copy-start | bytes 196
  21.8 10.3 %slice-start.1 = ((s8[4718592]{0:T(1024)(128)(4,1)}), s8[524288]{0:T(1024)(128)(4,1)S(1)}, s32[]{:S(2)}) async-start(s8[4718592]{0:T(1024)(128)(4,1)} %bitcast.5), calls=%async_computation.1 | async-start | bytes 1048576
  24.7 7.3 %collective-permute-start.7 = (f32[32,1536]{1,0:T(8,128)S(1)}, f32[32,1536]{1,0:T(8,128)S(1)}, u32[]{:S(2)}, u32[]{:S(2)}) collective-permute-start(f32[32,1536]{1,0:T(8,128)S(1)} %get-tuple-element.25), channel_id=1, source_target_pairs={{4,8},{12,16},{20,24},{28,32},{36,40},{44,48},{52,56},{60,64},{68,... | collective-permute-start | bytes 589832 | tf_op jit(solution)/shard_map/ppermute | solution.py:31
  27.3 4.7 %collective-permute-start.8 = (f32[32,1536]{1,0:T(8,128)S(1)}, f32[32,1536]{1,0:T(8,128)S(1)}, u32[]{:S(2)}, u32[]{:S(2)}) collective-permute-start(f32[32,1536]{1,0:T(8,128)S(1)} %get-tuple-element.26), channel_id=1, source_target_pairs={{0,4},{4,0},{8,12},{12,8},{16,20},{20,16},{24,28},{28,24},{32,36},... | collective-permute-start | bytes 589832 | tf_op jit(solution)/shard_map/ppermute | solution.py:21
  27.3 4.7 %copy-start = (bf16[20,4,4,1536]{3,2,1,0:T(4,128)(2,1)S(1)}, bf16[20,4,4,1536]{3,2,1,0:T(4,128)(2,1)}, u32[]{:S(2)}) copy-start(bf16[20,4,4,1536]{3,2,1,0:T(4,128)(2,1)} %alpha_ref.3) | copy-start | bytes 2949124
  27.3 4.7 %copy-start.1 = (bf16[20,4,4,1536]{3,2,1,0:T(4,128)(2,1)S(1)}, bf16[20,4,4,1536]{3,2,1,0:T(4,128)(2,1)}, u32[]{:S(2)}) copy-start(bf16[20,4,4,1536]{3,2,1,0:T(4,128)(2,1)} %perturb_ref.3) | copy-start | bytes 2949124

commit v5 on v4

--- a/solution.py
+++ b/solution.py
@@ -126,7 +126,7 @@
         out_ref[:, span] = jnp.sum((perturb * localized).reshape(members, levels * slots, chunk), axis=0)
 
 
-def edges_kernel(device_ref, coarse_ref, fine_ref, control_ref, after_ref, scalars_out, same_out, cross_out):
+def edges_kernel(device_ref, coarse_ref, fine_ref, control_ref, scalars_out, same_out, cross_out):
     bands = coarse_ref.shape[1]
     device = device_ref[0, 0]
     parity = device % 2
@@ -383,20 +383,21 @@
             pltpu.VMEM(loc_factor.shape, BF16),
             pltpu.SemaphoreType.DMA((2 + count // 512,)),
         ],
-        compiler_params=params(61),
+        compiler_params=params(53),
     )(alpha_control, perturb, loc_factor)
     peers = [mem_peer(partial, by) for by in (1, 3, 2)]
 
     plane = (3, levels, fine_slots, count)
     outgoing = jax.ShapeDtypeStruct((8 * levels, count), F32)
+    device, partial = lax.optimization_barrier((device, partial))
     wide = jax.ShapeDtypeStruct((6 * levels, count), F32)
     scalars, same_send, cross_send = pl.pallas_call(
         edges_kernel,
         out_shape=(jax.ShapeDtypeStruct((8, 128), jnp.int32), wide, wide),
-        in_specs=[VMEM] * 4 + [HBM],
+        in_specs=[VMEM] * 4,
         out_specs=(VMEM,) * 3,
         compiler_params=params(24),
-    )(device, coarse_rows.reshape(1, -1), fine_rows.reshape(1, -1), static_control, partial)
+    )(device, coarse_rows.reshape(1, -1), fine_rows.reshape(1, -1), static_control)
     static_from_cross = cross_chip(cross_send)
     static_from_same = same_chip(same_send)
     pair = jax.ShapeDtypeStruct((2 * levels, count), F32)

time: 35.6 us -> 34.3 us (0.963)
  local copies, waits for them, and re-layouts: 0.97 us -> 0.05 us
  starting transfers between devices: 15.2 us -> 16.1 us
  Pallas kernels: 15.2 us -> 14.4 us
  waiting for transfers between devices: 3.11 us -> 2.61 us
    ppermute x3, starting transfers between devices: 9.86 us -> 10.8 us  [cross_chip(): return lax.ppermute(x, ('band', 'mem'), pairs)]
    unnamed x24 -> x22, local copies, waits for them, and re-layouts: 0.97 us -> 0.05 us
    pallas_call x1, Pallas kernels: 5.36 us -> 4.56 us  [on_device(): pl.pallas_call(localize_kernel, out_shape=jax.ShapeDtypeStruct((rows, cou...]
    ppermute x3, waiting for transfers between devices: 3.1 us -> 2.59 us  [cross_chip(): return lax.ppermute(x, ('band', 'mem'), pairs)]
  transfers between devices with their start and end apart: 9 -> 9, of which waited for: 2 -> 1; matrix products, arithmetic and copies ran while one was open for 0% -> 0% of each run, Pallas kernels for 16% -> 16%
where the time goes in v5:
time: 34.3 us; the launch traced here: 34.2 us
  starting transfers between devices  16.1 us (47%)
  Pallas kernels  14.4 us (42%)
  waiting for transfers between devices  2.61 us (8%)
  between operations  1.01 us (3%)
    ppermute x3, starting transfers between devices, cross_chip(): return lax.ppermute(x, ('band', 'mem'), pairs)  10.8 us
    ppermute x3, starting transfers between devices, mem_peer(): return lax.ppermute(x, 'mem', [(i, (i + by) % peers) for i in range(peers)])  5.31 us
    pallas_call x1, Pallas kernels, on_device(): pl.pallas_call(localize_kernel, out_shape=jax.ShapeDtypeStruct((rows, cou...  4.56 us
    pallas_call x1, Pallas kernels, on_device(): pl.pallas_call(gradient_kernel, out_shape=(jax.ShapeDtypeStruct(perturb.s...  3.26 us
    ppermute x3, waiting for transfers between devices, cross_chip(): return lax.ppermute(x, ('band', 'mem'), pairs)  2.59 us
    pallas_call x1, Pallas kernels, on_device(): pl.pallas_call(own_gradient_kernel, out_shape=jax.ShapeDtypeStruct(static...  1.92 us
    pallas_call x1, Pallas kernels, on_device(): pl.pallas_call(static_kernel, out_shape=jax.ShapeDtypeStruct(plane, F32),...  1.58 us
    pallas_call x1, Pallas kernels, on_device(): pl.pallas_call(planes_kernel, out_shape=(jax.ShapeDtypeStruct(plane, F32)...  1.24 us
  transfers between devices with their start and end apart: 9, of which 1 were waited for; matrix products, arithmetic and copies ran while one was open for 0% of the time, Pallas kernels for 16%

profile of v5, /device:TPU:6, one launch (start us, length us, event | category | flops | bytes accessed | tf_op | source)
XLA Modules:
  0.0 34.2 jit_solution(17262036378520095495)
XLA Ops:
  0.7 4.6 %shard_map.113.own_ref = f32[16,1536]{1,0:T(8,128)S(1)} custom-call(bf16[20,4,4,1536]{3,2,1,0:T(4,128)(2,1)} %alpha_ref.3, bf16[20,4,4,1536]{3,2,1,0:T(4,128)(2,1)} %perturb_ref.3, bf16[1536,1536]{1,0:T(8,128)(2,1)} %loc_ref.3), custom_call_target="tpu_custom_call" | custom-call | tf_op jit(solution)/shard_map/pallas_call | solution.py:375
  5.2 0.0 copy-start.3
  5.2 3.3 %collective-permute-start.2 = (f32[16,1536]{1,0:T(8,128)S(1)}, f32[16,1536]{1,0:T(8,128)S(1)}, u32[]{:S(2)}, u32[]{:S(2)}) collective-permute-start(f32[16,1536]{1,0:T(8,128)S(1)} %shard_map.113.own_ref), channel_id=1, source_target_pairs={{0,2},{1,3},{2,0},{3,1},{4,6},{5,7},{6,4},{7,5},{8,10},{9,11},{10,... | collective-permute-start | bytes 294920 | tf_op jit(solution)/shard_map/ppermute | solution.py:36
  8.5 1.1 %collective-permute-start.1 = (f32[16,1536]{1,0:T(8,128)S(1)}, f32[16,1536]{1,0:T(8,128)S(1)}, u32[]{:S(2)}, u32[]{:S(2)}) collective-permute-start(f32[16,1536]{1,0:T(8,128)S(1)} %shard_map.113.own_ref), channel_id=1, source_target_pairs={{0,3},{1,0},{2,1},{3,2},{4,7},{5,4},{6,5},{7,6},{8,11},{9,8},{10,9... | collective-permute-start | bytes 294920 | tf_op jit(solution)/shard_map/ppermute | solution.py:36
  9.6 1.0 %collective-permute-start = (f32[16,1536]{1,0:T(8,128)S(1)}, f32[16,1536]{1,0:T(8,128)S(1)}, u32[]{:S(2)}, u32[]{:S(2)}) collective-permute-start(f32[16,1536]{1,0:T(8,128)S(1)} %shard_map.113.own_ref), channel_id=1, source_target_pairs={{0,1},{1,2},{2,3},{3,0},{4,5},{5,6},{6,7},{7,4},{8,9},{9,10},{10,1... | collective-permute-start | bytes 294920 | tf_op jit(solution)/shard_map/ppermute | solution.py:36
  10.6 0.7 %shard_map.114 = (s32[8,128]{1,0:T(8,128)S(1)}, f32[24,1536]{1,0:T(8,128)S(1)}, f32[24,1536]{1,0:T(8,128)S(1)}) custom-call(s32[1,1]{1,0:T(1,128)} %bitcast.device_ref, s32[1,64]{1,0:T(1,128)S(1)} %bitcast.9, s32[1,64]{1,0:T(1,128)S(1)} %bitcast.10, bf16[4,16,4608]{2,1,0:T(8,128)(2,1)S(1)} %copy-done.2), custom_call_target="tpu_custom_call" | custom-call | tf_op jit(solution)/shard_map/pallas_call | solution.py:394
  11.3 4.8 %collective-permute-start.5 = (f32[24,1536]{1,0:T(8,128)S(1)}, f32[24,1536]{1,0:T(8,128)S(1)}, u32[]{:S(2)}, u32[]{:S(2)}) collective-permute-start(f32[24,1536]{1,0:T(8,128)S(1)} %get-tuple-element.23), channel_id=1, source_target_pairs={{4,8},{12,16},{20,24},{28,32},{36,40},{44,48},{52,56},{60,64},{68,... | collective-permute-start | bytes 442376 | tf_op jit(solution)/shard_map/ppermute | solution.py:31
  16.1 0.0 collective-permute-done.1.b_ref
  16.1 0.1 shard_map.115
  16.2 3.2 %collective-permute-start.3 = (f32[8,1536]{1,0:T(8,128)S(1)}, f32[8,1536]{1,0:T(8,128)S(1)}, u32[]{:S(2)}, u32[]{:S(2)}) collective-permute-start(f32[8,1536]{1,0:T(8,128)S(1)} %get-tuple-element.21), channel_id=1, source_target_pairs={{4,8},{12,16},{20,24},{28,32},{36,40},{44,48},{52,56},{60,64},{68,... | collective-permute-start | bytes 147464 | tf_op jit(solution)/shard_map/ppermute | solution.py:31
  19.4 0.0 collective-permute-start.4
  19.4 1.2 %shard_map.116 = (f32[3,4,16,1536]{3,2,1,0:T(8,128)S(1)}, bf16[3,4,16,1536]{3,2,1,0:T(8,128)(2,1)S(1)}, bf16[3,4,16,1536]{3,2,1,0:T(8,128)(2,1)S(1)}) custom-call(s32[8,128]{1,0:T(8,128)S(1)} %get-tuple-element.18.scalars_ref, f32[16,1536]{1,0:T(8,128)S(1)} %get-tuple-element.20.after_ref.total_ref, bf16[4,16,4608]{2,1,0:T(8,128)(2,1)S(1)} %copy-done.2, ...), custom_call_target="tpu_custom_call" | custom-call | tf_op jit(solution)/shard_map/pallas_call | solution.py:413
  20.7 0.0 collective-permute-done.5.cross_ref
  20.7 0.0 copy-start.5
  20.7 0.0 copy-start.6
  20.7 0.0 slice-start.1
  20.8 1.6 %shard_map.117.static_ref = f32[3,4,16,1536]{3,2,1,0:T(8,128)S(1)} custom-call(s32[8,128]{1,0:T(8,128)S(1)} %get-tuple-element.18.scalars_ref, f32[24,1536]{1,0:T(8,128)S(1)} %collective-permute-done.5.cross_ref, f32[24,1536]{1,0:T(8,128)S(1)} %collective-permute-done.6.same_ref, f32[3,4,16,1536]{3,2,1,0:T(8,128)S(1)} %get-tuple-element.25.control_ref, ...), custom_call_target="tpu_custom_call" | custom-call | tf_op jit(solution)/shard_map/pallas_call | solution.py:422
  22.4 0.0 collective-permute-done.4.same_ref
  22.4 1.0 %shard_map.118 = (f32[3,4,16,1536]{3,2,1,0:T(8,128)S(1)}, f32[16,1536]{1,0:T(8,128)S(1)}, f32[32,1536]{1,0:T(8,128)S(1)}, f32[32,1536]{1,0:T(8,128)S(1)}) custom-call(s32[8,128]{1,0:T(8,128)S(1)} %get-tuple-element.18.scalars_ref, s32[1,16]{1,0:T(1,128)S(1)} %bitcast.7, f32[1,16]{1,0:T(1,128)S(1)} %bitcast.8, ...), custom_call_target="tpu_custom_call" | custom-call | tf_op jit(solution)/shard_map/pallas_call | solution.py:430
  23.4 2.8 %collective-permute-start.7 = (f32[32,1536]{1,0:T(8,128)S(1)}, f32[32,1536]{1,0:T(8,128)S(1)}, u32[]{:S(2)}, u32[]{:S(2)}) collective-permute-start(f32[32,1536]{1,0:T(8,128)S(1)} %get-tuple-element.29), channel_id=1, source_target_pairs={{4,8},{12,16},{20,24},{28,32},{36,40},{44,48},{52,56},{60,64},{68,... | collective-permute-start | bytes 589832 | tf_op jit(solution)/shard_map/ppermute | solution.py:31
  26.2 0.0 collective-permute-start.8
  26.2 1.9 %shard_map.119.own_static_ref = f32[4,16,4608]{2,1,0:T(8,128)S(1)} custom-call(s32[8,128]{1,0:T(8,128)S(1)} %get-tuple-element.18.scalars_ref, f32[3,4,16,1536]{3,2,1,0:T(8,128)S(1)} %get-tuple-element.25.control_ref, f32[3,4,16,1536]{3,2,1,0:T(8,128)S(1)} %get-tuple-element.31.residual_ref), custom_call_target="tpu_custom_call" | custom-call | tf_op jit(solution)/shard_map/pallas_call | solution.py:444
  28.1 2.6 %collective-permute-done.7.cross_ref = f32[32,1536]{1,0:T(8,128)S(1)} collective-permute-done((f32[32,1536]{1,0:T(8,128)S(1)}, f32[32,1536]{1,0:T(8,128)S(1)}, u32[]{:S(2)}, u32[]{:S(2)}) %collective-permute-start.7) | collective-permute-done | bytes 196640 | tf_op jit(solution)/shard_map/ppermute | solution.py:31
  30.8 3.3 %shard_map.120 = (bf16[20,4,4,1536]{3,2,1,0:T(4,128)(2,1)}, f32[4,16,4608]{2,1,0:T(8,128)}) custom-call(s32[8,128]{1,0:T(8,128)S(1)} %get-tuple-element.18.scalars_ref, f32[16,1536]{1,0:T(8,128)S(1)} %get-tuple-element.28.back_ref, f32[32,1536]{1,0:T(8,128)S(1)} %collective-permute-done.7.cross_ref, f32[32,1536]{1,0:T(8,128)S(1)} %collective-permute-done.8.same_ref, ...), custom_call_target="tpu_custom_call" | custom-call | tf_op jit(solution)/shard_map/pallas_call | solution.py:453
  (25 shorter events, 0.1 us)
Async XLA Ops:
  0.6 9.9 %copy-start.2 = (bf16[4,16,4608]{2,1,0:T(8,128)(2,1)S(1)}, bf16[4,16,4608]{2,1,0:T(8,128)(2,1)}, u32[]{:S(2)}) copy-start(bf16[4,16,4608]{2,1,0:T(8,128)(2,1)} %control_ref.3) | copy-start | bytes 1769476
  0.6 9.9 %copy-start.8 = (s32[64]{0:T(128)S(1)}, s32[64]{0:T(128)}, u32[]{:S(2)}) copy-start(s32[64]{0:T(128)} %param.17) | copy-start | bytes 772
  0.7 9.9 %copy-start.7 = (s32[64]{0:T(128)S(1)}, s32[64]{0:T(128)}, u32[]{:S(2)}) copy-start(s32[64]{0:T(128)} %param.16) | copy-start | bytes 772
  0.7 18.8 %copy-start.4 = (bf16[4,16,4608]{2,1,0:T(8,128)(2,1)S(1)}, bf16[4,16,4608]{2,1,0:T(8,128)(2,1)}, u32[]{:S(2)}) copy-start(bf16[4,16,4608]{2,1,0:T(8,128)(2,1)} %weight_ref.1) | copy-start | bytes 1769476
  5.2 14.2 %copy-start.3 = (bf16[4,16,4608]{2,1,0:T(8,128)(2,1)S(1)}, bf16[4,16,4608]{2,1,0:T(8,128)(2,1)}, u32[]{:S(2)}) copy-start(bf16[4,16,4608]{2,1,0:T(8,128)(2,1)} %innovation_ref.1) | copy-start | bytes 1769476
  5.2 10.9 %collective-permute-start.2 = (f32[16,1536]{1,0:T(8,128)S(1)}, f32[16,1536]{1,0:T(8,128)S(1)}, u32[]{:S(2)}, u32[]{:S(2)}) collective-permute-start(f32[16,1536]{1,0:T(8,128)S(1)} %shard_map.113.own_ref), channel_id=1, source_target_pairs={{0,2},{1,3},{2,0},{3,1},{4,6},{5,7},{6,4},{7,5},{8,10},{9,11},{10,... | collective-permute-start | bytes 294920 | tf_op jit(solution)/shard_map/ppermute | solution.py:36
  8.5 7.6 %collective-permute-start.1 = (f32[16,1536]{1,0:T(8,128)S(1)}, f32[16,1536]{1,0:T(8,128)S(1)}, u32[]{:S(2)}, u32[]{:S(2)}) collective-permute-start(f32[16,1536]{1,0:T(8,128)S(1)} %shard_map.113.own_ref), channel_id=1, source_target_pairs={{0,3},{1,0},{2,1},{3,2},{4,7},{5,4},{6,5},{7,6},{8,11},{9,8},{10,9... | collective-permute-start | bytes 294920 | tf_op jit(solution)/shard_map/ppermute | solution.py:36
  9.6 6.6 %collective-permute-start = (f32[16,1536]{1,0:T(8,128)S(1)}, f32[16,1536]{1,0:T(8,128)S(1)}, u32[]{:S(2)}, u32[]{:S(2)}) collective-permute-start(f32[16,1536]{1,0:T(8,128)S(1)} %shard_map.113.own_ref), channel_id=1, source_target_pairs={{0,1},{1,2},{2,3},{3,0},{4,5},{5,6},{6,7},{7,4},{8,9},{9,10},{10,1... | collective-permute-start | bytes 294920 | tf_op jit(solution)/shard_map/ppermute | solution.py:36
  10.6 20.2 %slice-start = ((s8[4718592]{0:T(1024)(128)(4,1)}), s8[4194304]{0:T(1024)(128)(4,1)S(1)}, s32[]{:S(2)}) async-start(s8[4718592]{0:T(1024)(128)(4,1)} %bitcast.5), calls=%async_computation | async-start | bytes 8388608
  11.3 9.4 %collective-permute-start.5 = (f32[24,1536]{1,0:T(8,128)S(1)}, f32[24,1536]{1,0:T(8,128)S(1)}, u32[]{:S(2)}, u32[]{:S(2)}) collective-permute-start(f32[24,1536]{1,0:T(8,128)S(1)} %get-tuple-element.23), channel_id=1, source_target_pairs={{4,8},{12,16},{20,24},{28,32},{36,40},{44,48},{52,56},{60,64},{68,... | collective-permute-start | bytes 442376 | tf_op jit(solution)/shard_map/ppermute | solution.py:31
  16.1 4.6 %collective-permute-start.6 = (f32[24,1536]{1,0:T(8,128)S(1)}, f32[24,1536]{1,0:T(8,128)S(1)}, u32[]{:S(2)}, u32[]{:S(2)}) collective-permute-start(f32[24,1536]{1,0:T(8,128)S(1)} %get-tuple-element.24), channel_id=1, source_target_pairs={{0,4},{4,0},{8,12},{12,8},{16,20},{20,16},{24,28},{28,24},{32,36},... | collective-permute-start | bytes 442376 | tf_op jit(solution)/shard_map/ppermute | solution.py:21
  16.2 6.1 %collective-permute-start.3 = (f32[8,1536]{1,0:T(8,128)S(1)}, f32[8,1536]{1,0:T(8,128)S(1)}, u32[]{:S(2)}, u32[]{:S(2)}) collective-permute-start(f32[8,1536]{1,0:T(8,128)S(1)} %get-tuple-element.21), channel_id=1, source_target_pairs={{4,8},{12,16},{20,24},{28,32},{36,40},{44,48},{52,56},{60,64},{68,... | collective-permute-start | bytes 147464 | tf_op jit(solution)/shard_map/ppermute | solution.py:31
  19.4 2.9 %collective-permute-start.4 = (f32[8,1536]{1,0:T(8,128)S(1)}, f32[8,1536]{1,0:T(8,128)S(1)}, u32[]{:S(2)}, u32[]{:S(2)}) collective-permute-start(f32[8,1536]{1,0:T(8,128)S(1)} %get-tuple-element.22), channel_id=1, source_target_pairs={{0,4},{4,0},{8,12},{12,8},{16,20},{20,16},{24,28},{28,24},{32,36},... | collective-permute-start | bytes 147464 | tf_op jit(solution)/shard_map/ppermute | solution.py:21
  20.7 1.6 %copy-start.5 = (s32[16]{0:T(128)S(1)}, s32[16]{0:T(128)}, u32[]{:S(2)}) copy-start(s32[16]{0:T(128)} %param.18) | copy-start | bytes 196
  20.7 1.6 %copy-start.6 = (f32[16]{0:T(128)S(1)}, f32[16]{0:T(128)}, u32[]{:S(2)}) copy-start(f32[16]{0:T(128)} %param.19) | copy-start | bytes 196
  20.7 10.0 %slice-start.1 = ((s8[4718592]{0:T(1024)(128)(4,1)}), s8[524288]{0:T(1024)(128)(4,1)S(1)}, s32[]{:S(2)}) async-start(s8[4718592]{0:T(1024)(128)(4,1)} %bitcast.5), calls=%async_computation.1 | async-start | bytes 1048576
  23.4 7.3 %collective-permute-start.7 = (f32[32,1536]{1,0:T(8,128)S(1)}, f32[32,1536]{1,0:T(8,128)S(1)}, u32[]{:S(2)}, u32[]{:S(2)}) collective-permute-start(f32[32,1536]{1,0:T(8,128)S(1)} %get-tuple-element.29), channel_id=1, source_target_pairs={{4,8},{12,16},{20,24},{28,32},{36,40},{44,48},{52,56},{60,64},{68,... | collective-permute-start | bytes 589832 | tf_op jit(solution)/shard_map/ppermute | solution.py:31
  26.2 4.5 %collective-permute-start.8 = (f32[32,1536]{1,0:T(8,128)S(1)}, f32[32,1536]{1,0:T(8,128)S(1)}, u32[]{:S(2)}, u32[]{:S(2)}) collective-permute-start(f32[32,1536]{1,0:T(8,128)S(1)} %get-tuple-element.30), channel_id=1, source_target_pairs={{0,4},{4,0},{8,12},{12,8},{16,20},{20,16},{24,28},{28,24},{32,36},... | collective-permute-start | bytes 589832 | tf_op jit(solution)/shard_map/ppermute | solution.py:21
  26.2 4.5 %copy-start = (bf16[20,4,4,1536]{3,2,1,0:T(4,128)(2,1)S(1)}, bf16[20,4,4,1536]{3,2,1,0:T(4,128)(2,1)}, u32[]{:S(2)}) copy-start(bf16[20,4,4,1536]{3,2,1,0:T(4,128)(2,1)} %alpha_ref.3) | copy-start | bytes 2949124
  26.2 4.5 %copy-start.1 = (bf16[20,4,4,1536]{3,2,1,0:T(4,128)(2,1)S(1)}, bf16[20,4,4,1536]{3,2,1,0:T(4,128)(2,1)}, u32[]{:S(2)}) copy-start(bf16[20,4,4,1536]{3,2,1,0:T(4,128)(2,1)} %perturb_ref.3) | copy-start | bytes 2949124

commit v6 on v5

--- a/solution.py
+++ b/solution.py
@@ -159,7 +159,10 @@
                 cross_out[to : to + 2, out] = planes[at + 2 : at + 4, p * width : (p + 1) * width]
 
 
-def planes_kernel(scalars_ref, after_ref, control_ref, innovation_ref, weight_ref, control_out, innovation_out, weight_out):
+def static_kernel(
+    scalars_ref, after_ref, cross_ref, same_ref, control_ref, innovation_ref, weight_ref,
+    control_out, static_out, weight_out, innovation_scr,
+):
     own_fine = scalars_ref[1, 0]
     levels, slots, count = control_ref.shape
     width = 128
@@ -179,13 +182,8 @@
                 planes[rows * (k * blocks + i) : rows * (k * blocks + i + 1), p * width : (p + 1) * width] for k in range(3)
             )
             control_out[p, :, :, out] = (control * live).reshape(levels, slots, width)
-            innovation_out[p, :, :, out] = innovation.reshape(levels, slots, width).astype(BF16)
+            innovation_scr[p, :, :, out] = innovation.reshape(levels, slots, width)
             weight_out[p, :, :, out] = (weight * live).reshape(levels, slots, width).astype(BF16)
-
-
-def static_kernel(scalars_ref, cross_ref, same_ref, control_ref, innovation_ref, static_out):
-    own_fine = scalars_ref[1, 0]
-    planes, levels, slots, count = control_ref.shape
     size = 2 * levels
     row_ids = lax.broadcasted_iota(jnp.int32, (slots, 1), 0)
     exists = neighbours(scalars_ref)
@@ -193,12 +191,12 @@
     lower = spread_halo([h[0] for h in halos], 1)
     higher = spread_halo([h[1] for h in halos], 0)
     for l in range(levels):
-        own = [control_ref[p, l] for p in range(3)]
-        first = [control_ref[p, l, 0:1, :] for p in range(3)]
-        last = [control_ref[p, l, pl.ds(own_fine - 1, 1), :] for p in range(3)]
+        own = [control_out[p, l] for p in range(3)]
+        first = [control_out[p, l, 0:1, :] for p in range(3)]
+        last = [control_out[p, l, pl.ds(own_fine - 1, 1), :] for p in range(3)]
         result = spread_own(own, first, last, own_fine, row_ids, exists)
         for p in range(3):
-            static_out[p, l] = result[p] - innovation_ref[p, l].astype(F32)
+            static_out[p, l] = result[p] - innovation_scr[p, l]
             static_out[p, l, 0:2, :] += lower[p][2 * l : 2 * l + 2]
             for k in range(2):
                 static_out[p, l, pl.ds(own_fine - 2 + k, 1), :] += higher[p][2 * l + k : 2 * l + k + 1]
@@ -313,7 +311,7 @@
 
 def gradient_kernel(
     scalars_ref, back_ref, cross_ref, same_ref, own_static_ref, alpha_ref, perturb_ref, loc_ref,
-    alpha_out, static_out, full_scr, schur_scr, stage_scr, halo_scr, static_scr, sems,
+    alpha_out, static_out, static_scr, full_scr, schur_scr, stage_scr, halo_scr, sems,
 ):
     own_coarse, own_fine = scalars_ref[0, 0], scalars_ref[1, 0]
     members, levels, slots, count = perturb_ref.shape
@@ -337,7 +335,6 @@
     mixed = join_planes([jnp.concatenate([lower[p], higher[p]], axis=0) for p in range(3)])
     for block, part in enumerate(mixed):
         halo_scr[:, 384 * block : 384 * (block + 1)] = part
-    static_scr[...] = own_static_ref[...]
     for l in range(levels):
         static_scr[l, 0:2, :] += halo_scr[2 * l : 2 * l + 2, :]
         for k in range(2):
@@ -410,22 +407,16 @@
     )(scalars, partial, *peers)
     from_cross = cross_chip(cross_send)
     from_same = same_chip(same_send)
-    control, innovation_planes, weight_planes = pl.pallas_call(
-        planes_kernel,
+    control, static_minus, weight_planes = pl.pallas_call(
+        static_kernel,
         out_shape=(
-            jax.ShapeDtypeStruct(plane, F32), jax.ShapeDtypeStruct(plane, BF16), jax.ShapeDtypeStruct(plane, BF16)
+            jax.ShapeDtypeStruct(plane, F32), jax.ShapeDtypeStruct(plane, F32), jax.ShapeDtypeStruct(plane, BF16)
         ),
-        in_specs=[VMEM, HBM] + [VMEM] * 3,
+        in_specs=[VMEM, HBM] + [VMEM] * 5,
         out_specs=(VMEM,) * 3,
-        compiler_params=params(24),
-    )(scalars, total, static_control, innovation, obs_weight)
-    static_minus = pl.pallas_call(
-        static_kernel,
-        out_shape=jax.ShapeDtypeStruct(plane, F32),
-        in_specs=[VMEM] * 5,
-        out_specs=VMEM,
-        compiler_params=params(24),
-    )(scalars, static_from_cross, static_from_same, control, innovation_planes)
+        scratch_shapes=[pltpu.VMEM(plane, F32)],
+        compiler_params=params(24),
+    )(scalars, total, static_from_cross, static_from_same, static_control, innovation, obs_weight)
 
     residual, back, same_send, cross_send = pl.pallas_call(
         residual_kernel,
@@ -450,21 +441,26 @@
         compiler_params=params(24),
     )(scalars, control, residual)
 
-    return pl.pallas_call(
+    grad_alpha, grad_static, _ = pl.pallas_call(
         gradient_kernel,
-        out_shape=(jax.ShapeDtypeStruct(perturb.shape, BF16), jax.ShapeDtypeStruct(static_control.shape, F32)),
+        out_shape=(
+            jax.ShapeDtypeStruct(perturb.shape, BF16),
+            jax.ShapeDtypeStruct(static_control.shape, F32),
+            jax.ShapeDtypeStruct(static_control.shape, F32),
+        ),
         in_specs=[VMEM] * 8,
-        out_specs=(HBM, HBM),
+        out_specs=(HBM, HBM, VMEM),
+        input_output_aliases={4: 2},
         scratch_shapes=[
             pltpu.VMEM((rows, count), F32),
             pltpu.VMEM((members * rows, count), BF16),
             pltpu.VMEM(perturb.shape, BF16),
             pltpu.VMEM((rows, 3 * count), F32),
-            pltpu.VMEM(static_control.shape, F32),
             pltpu.SemaphoreType.DMA((1 + steps,)),
         ],
         compiler_params=params(24),
     )(scalars, back, from_cross, from_same, own_static, alpha_control, perturb, loc_factor)
+    return grad_alpha, grad_static
 
 
 def solution(mesh):

time: 34.3 us -> 34 us (level)
  waiting for transfers between devices: 2.61 us -> 1.96 us
  starting transfers between devices: 16.1 us -> 16.7 us
    ppermute x3, waiting for transfers between devices: 2.59 us -> 1.94 us  [cross_chip(): return lax.ppermute(x, ('band', 'mem'), pairs)]
    ppermute x3, starting transfers between devices: 10.8 us -> 11.4 us  [cross_chip(): return lax.ppermute(x, ('band', 'mem'), pairs)]
    pallas_call x2 -> x1, Pallas kernels: 2.82 us -> 2.57 us  [on_device(): pl.pallas_call(static_kernel, out_shape=(jax.ShapeDtypeStruct(plane, F32)...]
where the time goes in v6:
time: 34 us; the launch traced here: 33.9 us
  starting transfers between devices  16.7 us (49%)
  Pallas kernels  14.2 us (42%)
  waiting for transfers between devices  1.96 us (6%)
  between operations  1 us (3%)
    ppermute x3, starting transfers between devices, cross_chip(): return lax.ppermute(x, ('band', 'mem'), pairs)  11.4 us
    ppermute x3, starting transfers between devices, mem_peer(): return lax.ppermute(x, 'mem', [(i, (i + by) % peers) for i in range(peers)])  5.31 us
    pallas_call x1, Pallas kernels, on_device(): pl.pallas_call(localize_kernel, out_shape=jax.ShapeDtypeStruct((rows, cou...  4.7 us
    pallas_call x1, Pallas kernels, on_device(): pl.pallas_call(gradient_kernel, out_shape=(jax.ShapeDtypeStruct(perturb.s...  3.17 us
    pallas_call x1, Pallas kernels, on_device(): pl.pallas_call(static_kernel, out_shape=(jax.ShapeDtypeStruct(plane, F32)...  2.57 us
    ppermute x3, waiting for transfers between devices, cross_chip(): return lax.ppermute(x, ('band', 'mem'), pairs)  1.94 us
    pallas_call x1, Pallas kernels, on_device(): pl.pallas_call(own_gradient_kernel, out_shape=jax.ShapeDtypeStruct(static...  1.91 us
    pallas_call x1, Pallas kernels, on_device(): pl.pallas_call(residual_kernel, out_shape=(jax.ShapeDtypeStruct(plane, F3...  1.03 us
  transfers between devices with their start and end apart: 9, of which 1 were waited for; matrix products, arithmetic and copies ran while one was open for 0% of the time, Pallas kernels for 16%

profile of v6, /device:TPU:6, one launch (start us, length us, event | category | flops | bytes accessed | tf_op | source)
XLA Modules:
  0.0 33.9 jit_solution(7003808694582478645)
XLA Ops:
  0.7 0.0 slice-start
  0.7 4.7 %shard_map.113.own_ref = f32[16,1536]{1,0:T(8,128)S(1)} custom-call(bf16[20,4,4,1536]{3,2,1,0:T(4,128)(2,1)} %alpha_ref.3, bf16[20,4,4,1536]{3,2,1,0:T(4,128)(2,1)} %perturb_ref.3, bf16[1536,1536]{1,0:T(8,128)(2,1)} %loc_ref.3), custom_call_target="tpu_custom_call" | custom-call | tf_op jit(solution)/shard_map/pallas_call | solution.py:372
  5.4 0.0 copy-start.3
  5.4 3.3 %collective-permute-start.2 = (f32[16,1536]{1,0:T(8,128)S(1)}, f32[16,1536]{1,0:T(8,128)S(1)}, u32[]{:S(2)}, u32[]{:S(2)}) collective-permute-start(f32[16,1536]{1,0:T(8,128)S(1)} %shard_map.113.own_ref), channel_id=1, source_target_pairs={{0,2},{1,3},{2,0},{3,1},{4,6},{5,7},{6,4},{7,5},{8,10},{9,11},{10,... | collective-permute-start | bytes 294920 | tf_op jit(solution)/shard_map/ppermute | solution.py:36
  8.7 1.1 %collective-permute-start.1 = (f32[16,1536]{1,0:T(8,128)S(1)}, f32[16,1536]{1,0:T(8,128)S(1)}, u32[]{:S(2)}, u32[]{:S(2)}) collective-permute-start(f32[16,1536]{1,0:T(8,128)S(1)} %shard_map.113.own_ref), channel_id=1, source_target_pairs={{0,3},{1,0},{2,1},{3,2},{4,7},{5,4},{6,5},{7,6},{8,11},{9,8},{10,9... | collective-permute-start | bytes 294920 | tf_op jit(solution)/shard_map/ppermute | solution.py:36
  9.7 1.0 %collective-permute-start = (f32[16,1536]{1,0:T(8,128)S(1)}, f32[16,1536]{1,0:T(8,128)S(1)}, u32[]{:S(2)}, u32[]{:S(2)}) collective-permute-start(f32[16,1536]{1,0:T(8,128)S(1)} %shard_map.113.own_ref), channel_id=1, source_target_pairs={{0,1},{1,2},{2,3},{3,0},{4,5},{5,6},{6,7},{7,4},{8,9},{9,10},{10,1... | collective-permute-start | bytes 294920 | tf_op jit(solution)/shard_map/ppermute | solution.py:36
  10.7 0.7 %shard_map.114 = (s32[8,128]{1,0:T(8,128)S(1)}, f32[24,1536]{1,0:T(8,128)S(1)}, f32[24,1536]{1,0:T(8,128)S(1)}) custom-call(s32[1,1]{1,0:T(1,128)} %bitcast.device_ref, s32[1,64]{1,0:T(1,128)S(1)} %bitcast.9, s32[1,64]{1,0:T(1,128)S(1)} %bitcast.10, bf16[4,16,4608]{2,1,0:T(8,128)(2,1)S(1)} %copy-done.2), custom_call_target="tpu_custom_call" | custom-call | tf_op jit(solution)/shard_map/pallas_call | solution.py:391
  11.5 4.8 %collective-permute-start.5 = (f32[24,1536]{1,0:T(8,128)S(1)}, f32[24,1536]{1,0:T(8,128)S(1)}, u32[]{:S(2)}, u32[]{:S(2)}) collective-permute-start(f32[24,1536]{1,0:T(8,128)S(1)} %get-tuple-element.25), channel_id=1, source_target_pairs={{4,8},{12,16},{20,24},{28,32},{36,40},{44,48},{52,56},{60,64},{68,... | collective-permute-start | bytes 442376 | tf_op jit(solution)/shard_map/ppermute | solution.py:31
  16.3 0.0 collective-permute-start.6
  16.3 0.0 collective-permute-done.a_ref
  16.3 0.0 copy-start.5
  16.3 0.0 copy-start.6
  16.3 0.0 slice-start.1
  16.3 0.1 shard_map.115
  16.4 3.2 %collective-permute-start.3 = (f32[8,1536]{1,0:T(8,128)S(1)}, f32[8,1536]{1,0:T(8,128)S(1)}, u32[]{:S(2)}, u32[]{:S(2)}) collective-permute-start(f32[8,1536]{1,0:T(8,128)S(1)} %get-tuple-element.23), channel_id=1, source_target_pairs={{4,8},{12,16},{20,24},{28,32},{36,40},{44,48},{52,56},{60,64},{68,... | collective-permute-start | bytes 147464 | tf_op jit(solution)/shard_map/ppermute | solution.py:31
  19.6 0.0 collective-permute-done.5.cross_ref
  19.6 0.0 collective-permute-done.6.same_ref
  19.6 2.6 %shard_map.116 = (f32[3,4,16,1536]{3,2,1,0:T(8,128)S(1)}, f32[3,4,16,1536]{3,2,1,0:T(8,128)S(1)}, bf16[3,4,16,1536]{3,2,1,0:T(8,128)(2,1)S(1)}) custom-call(s32[8,128]{1,0:T(8,128)S(1)} %get-tuple-element.20.scalars_ref, f32[16,1536]{1,0:T(8,128)S(1)} %get-tuple-element.22.after_ref.total_ref, f32[24,1536]{1,0:T(8,128)S(1)} %collective-permute-done.5.cross_ref, ...), custom_call_target="tpu_custom_call" | custom-call | tf_op jit(solution)/shard_map/pallas_call | solution.py:410
  22.2 1.0 %shard_map.117 = (f32[3,4,16,1536]{3,2,1,0:T(8,128)S(1)}, f32[16,1536]{1,0:T(8,128)S(1)}, f32[32,1536]{1,0:T(8,128)S(1)}, f32[32,1536]{1,0:T(8,128)S(1)}) custom-call(s32[8,128]{1,0:T(8,128)S(1)} %get-tuple-element.20.scalars_ref, s32[1,16]{1,0:T(1,128)S(1)} %bitcast.7, f32[1,16]{1,0:T(1,128)S(1)} %bitcast.8, ...), custom_call_target="tpu_custom_call" | custom-call | tf_op jit(solution)/shard_map/pallas_call | solution.py:421
  23.3 3.4 %collective-permute-start.7 = (f32[32,1536]{1,0:T(8,128)S(1)}, f32[32,1536]{1,0:T(8,128)S(1)}, u32[]{:S(2)}, u32[]{:S(2)}) collective-permute-start(f32[32,1536]{1,0:T(8,128)S(1)} %get-tuple-element.30), channel_id=1, source_target_pairs={{4,8},{12,16},{20,24},{28,32},{36,40},{44,48},{52,56},{60,64},{68,... | collective-permute-start | bytes 589832 | tf_op jit(solution)/shard_map/ppermute | solution.py:31
  26.7 0.0 collective-permute-start.8
  26.7 1.9 %shard_map.118.own_static_ref = f32[4,16,4608]{2,1,0:T(8,128)S(1)} custom-call(s32[8,128]{1,0:T(8,128)S(1)} %get-tuple-element.20.scalars_ref, f32[3,4,16,1536]{3,2,1,0:T(8,128)S(1)} %get-tuple-element.32.control_ref, f32[3,4,16,1536]{3,2,1,0:T(8,128)S(1)} %get-tuple-element.33.residual_ref), custom_call_target="tpu_custom_call" | custom-call | tf_op jit(solution)/shard_map/pallas_call | solution.py:435
  28.6 1.9 %collective-permute-done.7.cross_ref = f32[32,1536]{1,0:T(8,128)S(1)} collective-permute-done((f32[32,1536]{1,0:T(8,128)S(1)}, f32[32,1536]{1,0:T(8,128)S(1)}, u32[]{:S(2)}, u32[]{:S(2)}) %collective-permute-start.7) | collective-permute-done | bytes 196640 | tf_op jit(solution)/shard_map/ppermute | solution.py:31
  30.6 3.2 %shard_map.119 = (bf16[20,4,4,1536]{3,2,1,0:T(4,128)(2,1)}, f32[4,16,4608]{2,1,0:T(8,128)}, f32[4,16,4608]{2,1,0:T(8,128)S(1)}) custom-call(s32[8,128]{1,0:T(8,128)S(1)} %get-tuple-element.20.scalars_ref, f32[16,1536]{1,0:T(8,128)S(1)} %get-tuple-element.29.back_ref, ...), custom_call_target="tpu_custom_call", output_to_operand_aliasing={{2}: (4, {})} | custom-call | tf_op jit(solution)/shard_map/pallas_call | solution.py:444
  (24 shorter events, 0.1 us)
Async XLA Ops:
  0.6 10.1 %copy-start.2 = (bf16[4,16,4608]{2,1,0:T(8,128)(2,1)S(1)}, bf16[4,16,4608]{2,1,0:T(8,128)(2,1)}, u32[]{:S(2)}) copy-start(bf16[4,16,4608]{2,1,0:T(8,128)(2,1)} %control_ref.3) | copy-start | bytes 1769476
  0.6 10.1 %copy-start.8 = (s32[64]{0:T(128)S(1)}, s32[64]{0:T(128)}, u32[]{:S(2)}) copy-start(s32[64]{0:T(128)} %param.17) | copy-start | bytes 772
  0.7 10.1 %copy-start.7 = (s32[64]{0:T(128)S(1)}, s32[64]{0:T(128)}, u32[]{:S(2)}) copy-start(s32[64]{0:T(128)} %param.16) | copy-start | bytes 772
  0.7 18.9 %copy-start.4 = (bf16[4,16,4608]{2,1,0:T(8,128)(2,1)S(1)}, bf16[4,16,4608]{2,1,0:T(8,128)(2,1)}, u32[]{:S(2)}) copy-start(bf16[4,16,4608]{2,1,0:T(8,128)(2,1)} %weight_ref.1) | copy-start | bytes 1769476
  0.7 29.9 %slice-start = ((s8[4718592]{0:T(1024)(128)(4,1)}), s8[524288]{0:T(1024)(128)(4,1)S(1)}, s32[]{:S(2)}) async-start(s8[4718592]{0:T(1024)(128)(4,1)} %bitcast.5), calls=%async_computation | async-start | bytes 1048576
  5.4 14.2 %copy-start.3 = (bf16[4,16,4608]{2,1,0:T(8,128)(2,1)S(1)}, bf16[4,16,4608]{2,1,0:T(8,128)(2,1)}, u32[]{:S(2)}) copy-start(bf16[4,16,4608]{2,1,0:T(8,128)(2,1)} %innovation_ref.1) | copy-start | bytes 1769476
  5.4 10.9 %collective-permute-start.2 = (f32[16,1536]{1,0:T(8,128)S(1)}, f32[16,1536]{1,0:T(8,128)S(1)}, u32[]{:S(2)}, u32[]{:S(2)}) collective-permute-start(f32[16,1536]{1,0:T(8,128)S(1)} %shard_map.113.own_ref), channel_id=1, source_target_pairs={{0,2},{1,3},{2,0},{3,1},{4,6},{5,7},{6,4},{7,5},{8,10},{9,11},{10,... | collective-permute-start | bytes 294920 | tf_op jit(solution)/shard_map/ppermute | solution.py:36
  8.7 7.6 %collective-permute-start.1 = (f32[16,1536]{1,0:T(8,128)S(1)}, f32[16,1536]{1,0:T(8,128)S(1)}, u32[]{:S(2)}, u32[]{:S(2)}) collective-permute-start(f32[16,1536]{1,0:T(8,128)S(1)} %shard_map.113.own_ref), channel_id=1, source_target_pairs={{0,3},{1,0},{2,1},{3,2},{4,7},{5,4},{6,5},{7,6},{8,11},{9,8},{10,9... | collective-permute-start | bytes 294920 | tf_op jit(solution)/shard_map/ppermute | solution.py:36
  9.7 6.6 %collective-permute-start = (f32[16,1536]{1,0:T(8,128)S(1)}, f32[16,1536]{1,0:T(8,128)S(1)}, u32[]{:S(2)}, u32[]{:S(2)}) collective-permute-start(f32[16,1536]{1,0:T(8,128)S(1)} %shard_map.113.own_ref), channel_id=1, source_target_pairs={{0,1},{1,2},{2,3},{3,0},{4,5},{5,6},{6,7},{7,4},{8,9},{9,10},{10,1... | collective-permute-start | bytes 294920 | tf_op jit(solution)/shard_map/ppermute | solution.py:36
  11.5 8.1 %collective-permute-start.5 = (f32[24,1536]{1,0:T(8,128)S(1)}, f32[24,1536]{1,0:T(8,128)S(1)}, u32[]{:S(2)}, u32[]{:S(2)}) collective-permute-start(f32[24,1536]{1,0:T(8,128)S(1)} %get-tuple-element.25), channel_id=1, source_target_pairs={{4,8},{12,16},{20,24},{28,32},{36,40},{44,48},{52,56},{60,64},{68,... | collective-permute-start | bytes 442376 | tf_op jit(solution)/shard_map/ppermute | solution.py:31
  16.3 3.3 %collective-permute-start.6 = (f32[24,1536]{1,0:T(8,128)S(1)}, f32[24,1536]{1,0:T(8,128)S(1)}, u32[]{:S(2)}, u32[]{:S(2)}) collective-permute-start(f32[24,1536]{1,0:T(8,128)S(1)} %get-tuple-element.26), channel_id=1, source_target_pairs={{0,4},{4,0},{8,12},{12,8},{16,20},{20,16},{24,28},{28,24},{32,36},... | collective-permute-start | bytes 442376 | tf_op jit(solution)/shard_map/ppermute | solution.py:21
  16.3 5.9 %copy-start.5 = (s32[16]{0:T(128)S(1)}, s32[16]{0:T(128)}, u32[]{:S(2)}) copy-start(s32[16]{0:T(128)} %param.18) | copy-start | bytes 196
  16.3 5.9 %copy-start.6 = (f32[16]{0:T(128)S(1)}, f32[16]{0:T(128)}, u32[]{:S(2)}) copy-start(f32[16]{0:T(128)} %param.19) | copy-start | bytes 196
  16.3 14.3 %slice-start.1 = ((s8[4718592]{0:T(1024)(128)(4,1)}), s8[4194304]{0:T(1024)(128)(4,1)S(1)}, s32[]{:S(2)}) async-start(s8[4718592]{0:T(1024)(128)(4,1)} %bitcast.5), calls=%async_computation.1 | async-start | bytes 8388608
  16.4 5.8 %collective-permute-start.3 = (f32[8,1536]{1,0:T(8,128)S(1)}, f32[8,1536]{1,0:T(8,128)S(1)}, u32[]{:S(2)}, u32[]{:S(2)}) collective-permute-start(f32[8,1536]{1,0:T(8,128)S(1)} %get-tuple-element.23), channel_id=1, source_target_pairs={{4,8},{12,16},{20,24},{28,32},{36,40},{44,48},{52,56},{60,64},{68,... | collective-permute-start | bytes 147464 | tf_op jit(solution)/shard_map/ppermute | solution.py:31
  19.6 2.6 %collective-permute-start.4 = (f32[8,1536]{1,0:T(8,128)S(1)}, f32[8,1536]{1,0:T(8,128)S(1)}, u32[]{:S(2)}, u32[]{:S(2)}) collective-permute-start(f32[8,1536]{1,0:T(8,128)S(1)} %get-tuple-element.24), channel_id=1, source_target_pairs={{0,4},{4,0},{8,12},{12,8},{16,20},{20,16},{24,28},{28,24},{32,36},... | collective-permute-start | bytes 147464 | tf_op jit(solution)/shard_map/ppermute | solution.py:21
  23.3 7.3 %collective-permute-start.7 = (f32[32,1536]{1,0:T(8,128)S(1)}, f32[32,1536]{1,0:T(8,128)S(1)}, u32[]{:S(2)}, u32[]{:S(2)}) collective-permute-start(f32[32,1536]{1,0:T(8,128)S(1)} %get-tuple-element.30), channel_id=1, source_target_pairs={{4,8},{12,16},{20,24},{28,32},{36,40},{44,48},{52,56},{60,64},{68,... | collective-permute-start | bytes 589832 | tf_op jit(solution)/shard_map/ppermute | solution.py:31
  26.7 3.9 %collective-permute-start.8 = (f32[32,1536]{1,0:T(8,128)S(1)}, f32[32,1536]{1,0:T(8,128)S(1)}, u32[]{:S(2)}, u32[]{:S(2)}) collective-permute-start(f32[32,1536]{1,0:T(8,128)S(1)} %get-tuple-element.31), channel_id=1, source_target_pairs={{0,4},{4,0},{8,12},{12,8},{16,20},{20,16},{24,28},{28,24},{32,36},... | collective-permute-start | bytes 589832 | tf_op jit(solution)/shard_map/ppermute | solution.py:21
  26.7 3.9 %copy-start = (bf16[20,4,4,1536]{3,2,1,0:T(4,128)(2,1)S(1)}, bf16[20,4,4,1536]{3,2,1,0:T(4,128)(2,1)}, u32[]{:S(2)}) copy-start(bf16[20,4,4,1536]{3,2,1,0:T(4,128)(2,1)} %alpha_ref.3) | copy-start | bytes 2949124
  26.7 3.9 %copy-start.1 = (bf16[20,4,4,1536]{3,2,1,0:T(4,128)(2,1)S(1)}, bf16[20,4,4,1536]{3,2,1,0:T(4,128)(2,1)}, u32[]{:S(2)}) copy-start(bf16[20,4,4,1536]{3,2,1,0:T(4,128)(2,1)} %perturb_ref.3) | copy-start | bytes 2949124
